TPU v7x, 32 devices: a whole 2x2x4 slice. The times are simulated.
32 devices in a mesh: group: 8 (over y, x, core), head: 4 (over z).
Axes of the slice: x: 2, y: 2, z: 4, core: 2. Of those that a mesh axis runs over, the one named last changes fastest.
Arguments:
- key_grad: bfloat16 [4096, 16384], P('group', 'head'), may hold values from -6 to 6
- value_grad: bfloat16 [4096, 16384], P('group', 'head'), may hold values from -6 to 6
- rope_grad: bfloat16 [4096, 8192], P('group', 'head'), may hold values from -1.5 to 1.5
- key_lift: bfloat16 [512, 16384], P(None, 'head'), may hold values from -0.046875 to 0.046875
- value_lift: bfloat16 [512, 16384], P(None, 'head'), may hold values from -0.046875 to 0.046875
- latent: bfloat16 [4096, 512], P('group'), may hold values from -40 to 40
- norm_gain: float32 [512], replicated, may hold values from 0.25 to 1.75
- doc_lengths: int32 [8, 4], P('group'), may hold values from 1 to 256, 512 in all within a row
- hidden: bfloat16 [4096, 7168], P('group', 'head'), may hold values from -0.25 to 0.25
- down_proj: bfloat16 [7168, 576], P('head'), may hold values from -0.0625 to 0.0625
Outputs:
- hidden_grad: bfloat16 [4096, 7168], P('group', 'head')
- weight_grad: float32 [576, 7168], P('group', 'head')
Inputs may be any that keep to these rules, and one draw needn't show every extreme that they name: `doc_lengths`: each row sums to 512 and its largest entry is 256.
All inputs are finite; a program needn't handle non-finite values.
Results may differ from a plain program's by a relative error of at most 0.0049.
Values may be sent and summed in bfloat16 or wider, within the bound.
No kernel may reach another device: no remote copies, remote signals or barrier semaphores. Data moves between devices by JAX's collectives and lax.ppermute only.
A program may use at most 64 MiB of HBM per device.

v0:
```python
import jax
import jax.numpy as jnp
from jax import lax
from jax.sharding import PartitionSpec as P

LATENT = 512
ROPE = 64


def positions(lengths, token_index):
    doc_ends = jnp.cumsum(lengths, axis=1)
    doc_start = jnp.max(jnp.where(doc_ends <= token_index[:, None], doc_ends, 0), axis=1)
    return token_index - doc_start


def kva_rows_grad(stacked, latent, norm_gain, position):
    latent_part = stacked[:, :LATENT]
    rotary_part = stacked[:, LATENT:]
    values = latent.astype(jnp.float32)
    inverse_rms = lax.rsqrt(jnp.mean(values * values, axis=1, keepdims=True) + 1e-06)
    scaled_grad = latent_part * norm_gain[None, :]
    norm_grad = inverse_rms * (
        scaled_grad
        - values * inverse_rms * inverse_rms * jnp.mean(scaled_grad * values, axis=1, keepdims=True)
    )
    half_width = rotary_part.shape[1] // 2
    inv_freq = 10000.0 ** (-(2.0 * jnp.arange(half_width, dtype=jnp.float32)) / (2.0 * half_width))
    angles = position.astype(jnp.float32)[:, None] * inv_freq[None, :]
    cosine = jnp.cos(angles)
    sine = jnp.sin(angles)
    first_half = rotary_part[:, :half_width]
    second_half = rotary_part[:, half_width:]
    rot_first = first_half * cosine + second_half * sine
    rot_second = second_half * cosine - first_half * sine
    return jnp.concatenate([norm_grad, rot_first, rot_second], axis=1).astype(jnp.bfloat16)


def on_device(
    key_grad,
    value_grad,
    rope_grad,
    key_lift,
    value_lift,
    latent,
    norm_gain,
    doc_lengths,
    hidden,
    down_proj,
):
    contract = (((1,), (1,)), ((), ()))
    seq_len = key_grad.shape[0]
    head_terms = lax.dot_general(key_grad, key_lift, contract, preferred_element_type=jnp.float32)
    head_terms = head_terms + lax.dot_general(
        value_grad, value_lift, contract, preferred_element_type=jnp.float32
    )
    heads_here = rope_grad.shape[1] // ROPE
    rope_terms = jnp.sum(rope_grad.reshape(seq_len, heads_here, ROPE), axis=1, dtype=jnp.float32)
    stacked = jnp.concatenate([head_terms, rope_terms], axis=1)
    shared = lax.psum_scatter(stacked, "head", scatter_dimension=0, tiled=True)
    share_rows = shared.shape[0]
    first_row = lax.axis_index("head") * share_rows
    own_latent = lax.dynamic_slice_in_dim(latent, first_row, share_rows, 0)
    token_index = first_row + jnp.arange(share_rows, dtype=jnp.int32)
    row_lengths = jnp.broadcast_to(doc_lengths, (share_rows, doc_lengths.shape[1]))
    own_grad = kva_rows_grad(shared, own_latent, norm_gain, positions(row_lengths, token_index))
    kva_grad = lax.all_gather(own_grad, "head", axis=0, tiled=True)
    hidden_grad = lax.dot_general(
        kva_grad, down_proj, contract, preferred_element_type=jnp.float32
    ).astype(jnp.bfloat16)
    weight_grad = lax.psum_scatter(
        lax.dot_general(
            kva_grad, hidden, (((0,), (0,)), ((), ())), preferred_element_type=jnp.float32
        ),
        "group",
        scatter_dimension=0,
        tiled=True,
    )
    return (hidden_grad, weight_grad)


def solution(mesh):
    return jax.shard_map(
        on_device,
        mesh=mesh,
        in_specs=(
            P("group", "head"),
            P("group", "head"),
            P("group", "head"),
            P(None, "head"),
            P(None, "head"),
            P("group", None),
            P(),
            P("group", None),
            P("group", "head"),
            P("head", None),
        ),
        out_specs=(P("group", "head"), P("group", "head")),
        check_vma=False,
    )
```

profile of v0, /device:TPU:0, one launch (start us, length us, event | category | flops | bytes accessed | tf_op | source)
XLA Modules:
  0.0 135.0 jit_solution(14031125219246364961)
XLA Ops:
  7.2 0.0 copy-start
  7.2 0.0 reduce-scatter.3.cloned.1.call-start
  7.2 4.1 %copy.16 = bf16[512,2048]{0,1:T(8,128)(2,1)} copy(bf16[512,2048]{1,0:T(8,128)(2,1)} %param.12) | data formatting | bytes 4194304 | tf_op args[2]
  11.3 1.9 %convert_reduce_fusion = f32[512,64]{0,1:T(8,128)S(1)} fusion(bf16[512,32,64]{0,2,1:T(8,128)(2,1)} %bitcast.11), kind=kLoop, calls=%fused_computation | loop fusion | flops 2064384 | bytes 2228224 | tf_op jit(solution)/shard_map/reduce_sum | solution.py:57
  13.2 0.0 copy-start.3
  13.2 0.0 copy-start.4
  13.2 6.0 %fusion.16 = f32[512,512]{0,1:T(8,128)S(1)} fusion(bf16[512,4096]{1,0:T(8,128)(2,1)} %param.10, bf16[512,4096]{1,0:T(8,128)(2,1)} %param.13), kind=kOutput, calls=%fused_computation.34 | convolution fusion | flops 2147483648 | bytes 9437184 | tf_op jit(solution)/shard_map/dot_general | solution.py:52
  19.2 0.0 copy-done.3
  19.2 0.0 copy-done.4
  19.2 0.0 copy-start.2
  19.2 0.0 copy-start.1
  19.2 2.4 %convolution_add_fusion = f32[512,512]{0,1:T(8,128)S(1)} fusion(f32[512,512]{0,1:T(8,128)S(1)} %fusion.16, bf16[512,4096]{1,0:T(8,128)(2,1)S(1)} %copy-done.3, bf16[512,4096]{1,0:T(8,128)(2,1)S(1)} %copy-done.4), kind=kOutput, calls=%fused_computation.2 | convolution fusion | flops 2147745792 | bytes 10485760 | tf_op jit(solution)/shard_map/dot_general | solution.py:53
  21.6 1.1 pad_maximum_fusion
  22.7 0.0 reduce-scatter.3.cloned.1.call-update
  22.7 0.0 reduce-scatter.5.cloned.1.call-start
  22.8 0.9 constant_dynamic-slice_fusion
  23.7 0.1 copy.17
  23.8 0.0 copy-done.2
  23.8 0.1 broadcast_in_dim.9
  24.0 30.8 %reduce-scatter.3.cloned.1.call-done = f32[128,576]{0,1:T(8,128)} async-done(((f32[512,576]{0,1:T(8,128)}), f32[128,576]{0,1:T(8,128)}) %reduce-scatter.3.cloned.1.call-update) | async-done | bytes 294928 | tf_op jit(solution)/shard_map/reduce_scatter | solution.py:59
  54.7 0.0 copy-done.1
  54.7 1.1 fusion
  55.9 1.1 fusion.5
  56.9 0.9 fusion.12
  57.9 16.0 %all_gather.3 = bf16[512,576]{0,1:T(8,128)(2,1)S(1)} all-gather(bf16[128,576]{0,1:T(8,128)(2,1)S(1)} %pad_maximum_fusion.1), channel_id=1, replica_groups=mesh['group'=8,'head'=4] {'head'}, dimensions={0}, use_global_device_ids=true | all-gather | bytes 737280 | tf_op jit(solution)/shard_map/all_gather | solution.py:66
  73.8 4.7 %fusion.17 = f32[576,1792]{1,0:T(8,128)} fusion(bf16[512,576]{0,1:T(8,128)(2,1)S(1)} %all_gather.3, bf16[512,1792]{1,0:T(8,128)(2,1)} %param.18), kind=kOutput, calls=%fused_computation.35 | convolution fusion | flops 1056964608 | bytes 6553600 | tf_op jit(solution)/shard_map/dot_general | solution.py:71
  78.5 0.0 reduce-scatter.5.cloned.1.call-update
  78.5 0.0 copy-done
  78.5 2.8 %convolution_convert_fusion = bf16[512,1792]{1,0:T(8,128)(2,1)} fusion(bf16[512,576]{0,1:T(8,128)(2,1)S(1)} %all_gather.3, bf16[1792,576]{0,1:T(8,128)(2,1)S(1)} %copy-done), kind=kOutput, calls=%fused_computation.1 | convolution fusion | flops 1057882112 | bytes 4489216 | tf_op jit(solution)/shard_map/dot_general | solution.py:67
  81.4 46.8 %reduce-scatter.5.cloned.1.call-done = f32[72,1792]{1,0:T(8,128)} async-done(((f32[576,1792]{1,0:T(8,128)}), f32[72,1792]{1,0:T(8,128)}) %reduce-scatter.5.cloned.1.call-update) | async-done | bytes 516112 | tf_op jit(solution)/shard_map/reduce_scatter | solution.py:70
  (7 shorter events, 0.1 us)
Async XLA Ops:
  7.2 71.3 %copy-start = (bf16[1792,576]{0,1:T(8,128)(2,1)S(1)}, bf16[1792,576]{0,1:T(8,128)(2,1)}, u32[]{:S(2)}) copy-start(bf16[1792,576]{0,1:T(8,128)(2,1)} %param.19) | copy-start | bytes 6193156
  7.2 47.6 %reduce-scatter.3.cloned.1.call-start = ((), (), s32[]{:S(2)}) async-start(), calls=%async_computation.2 | async-start | bytes 1474560 | tf_op jit(solution)/shard_map/reduce_scatter | solution.py:59
  13.2 6.0 %copy-start.3 = (bf16[512,4096]{1,0:T(8,128)(2,1)S(1)}, bf16[512,4096]{1,0:T(8,128)(2,1)}, u32[]{:S(2)}) copy-start(bf16[512,4096]{1,0:T(8,128)(2,1)} %param.11) | copy-start | bytes 12582916
  13.2 6.0 %copy-start.4 = (bf16[512,4096]{1,0:T(8,128)(2,1)S(1)}, bf16[512,4096]{1,0:T(8,128)(2,1)}, u32[]{:S(2)}) copy-start(bf16[512,4096]{1,0:T(8,128)(2,1)} %param.14) | copy-start | bytes 12582916
  19.2 4.6 %copy-start.2 = (s32[1,4]{1,0:T(1,128)S(1)}, s32[1,4]{1,0:T(1,128)}, u32[]{:S(2)}) copy-start(s32[1,4]{1,0:T(1,128)} %param.17) | copy-start | bytes 52
  19.2 35.5 %copy-start.1 = (f32[512]{0:T(512)S(1)}, f32[512]{0:T(512)}, u32[]{:S(2)}) copy-start(f32[512]{0:T(512)} %param.16) | copy-start | bytes 6148
  22.7 105.5 %reduce-scatter.5.cloned.1.call-start = ((), (), s32[]{:S(2)}) async-start(), calls=%async_computation.3 | async-start | bytes 4644864 | tf_op jit(solution)/shard_map/reduce_scatter | solution.py:70
Sparse Core Ops, SparseCore 0:
  22.8 31.8 reduce-scatter.2
  78.6 49.5 reduce-scatter.4
where the time goes:
time: 135 us
  waiting for transfers between devices  77.6 us (57%)
  blocking collectives  16 us (12%)
  matrix products  15.8 us (12%)
  between operations  14.2 us (11%)
  other arithmetic  6.17 us (5%)
  local copies, waits for them, and re-layouts  5.22 us (4%)
    reduce_scatter x1, waiting for transfers between devices, on_device(): lax.psum_scatter(lax.dot_general(kva_grad, hidden, (((0,), (0,)), ((), ()...  46.8 us
    reduce_scatter x1, waiting for transfers between devices, on_device(): shared = lax.psum_scatter(stacked, 'head', scatter_dimension=0, tiled=True)  30.8 us
    all_gather x1, blocking collectives, on_device(): kva_grad = lax.all_gather(own_grad, 'head', axis=0, tiled=True)  16 us
    dot_general x1, matrix products, on_device(): lax.dot_general(key_grad, key_lift, contract, preferred_element_type=jnp....  5.96 us
    dot_general x1, matrix products, on_device(): lax.dot_general(kva_grad, hidden, (((0,), (0,)), ((), ())), preferred_ele...  4.66 us
    unnamed x12, local copies, waits for them, and re-layouts  4.23 us
    dot_general x1, matrix products, on_device(): lax.dot_general(kva_grad, down_proj, contract, preferred_element_type=jnp...  2.85 us
  transfers between devices with their start and end apart: 2, of which 2 were waited for; matrix products, arithmetic and copies ran while one was open for 3% of the time, Pallas kernels for 0%

commit v1 on v0

v1 whole, which is shorter than its diff:
```python
import functools

import jax
import jax.numpy as jnp
import numpy as np
from jax import lax
from jax.experimental import pallas as pl
from jax.experimental.pallas import tpu as pltpu
from jax.sharding import PartitionSpec as P

F32 = jnp.float32
BF16 = jnp.bfloat16
LAST = (((1,), (1,)), ((), ()))
FIRST = (((0,), (0,)), ((), ()))
MIB = 1 << 20


def positions(lengths, token_index):
    doc_ends = jnp.cumsum(lengths, axis=1)
    doc_start = jnp.max(jnp.where(doc_ends <= token_index[:, None], doc_ends, 0), axis=1)
    return token_index - doc_start


def kva_rows_grad(stacked, latent, norm_gain, position):
    width = latent.shape[1]
    latent_part = stacked[:, :width]
    rotary_part = stacked[:, width:]
    values = latent.astype(F32)
    inverse_rms = lax.rsqrt(jnp.mean(values * values, axis=1, keepdims=True) + 1e-06)
    scaled_grad = latent_part * norm_gain[None, :]
    norm_grad = inverse_rms * (
        scaled_grad
        - values * inverse_rms * inverse_rms * jnp.mean(scaled_grad * values, axis=1, keepdims=True)
    )
    half_width = rotary_part.shape[1] // 2
    inv_freq = 10000.0 ** (-(2.0 * jnp.arange(half_width, dtype=F32)) / (2.0 * half_width))
    angles = position.astype(F32)[:, None] * inv_freq[None, :]
    cosine = jnp.cos(angles)
    sine = jnp.sin(angles)
    first_half = rotary_part[:, :half_width]
    second_half = rotary_part[:, half_width:]
    rot_first = first_half * cosine + second_half * sine
    rot_second = second_half * cosine - first_half * sine
    return jnp.concatenate([norm_grad, rot_first, rot_second], axis=1).astype(BF16)


def on_device_any(
    key_grad, value_grad, rope_grad, key_lift, value_lift, latent, norm_gain, doc_lengths, hidden, down_proj
):
    seq_len = key_grad.shape[0]
    rope = down_proj.shape[1] - latent.shape[1]
    head_terms = lax.dot_general(key_grad, key_lift, LAST, preferred_element_type=F32)
    head_terms = head_terms + lax.dot_general(value_grad, value_lift, LAST, preferred_element_type=F32)
    heads_here = rope_grad.shape[1] // rope
    rope_terms = jnp.sum(rope_grad.reshape(seq_len, heads_here, rope), axis=1, dtype=F32)
    stacked = jnp.concatenate([head_terms, rope_terms], axis=1)
    shared = lax.psum_scatter(stacked, "head", scatter_dimension=0, tiled=True)
    share_rows = shared.shape[0]
    first_row = lax.axis_index("head") * share_rows
    own_latent = lax.dynamic_slice_in_dim(latent, first_row, share_rows, 0)
    token_index = first_row + jnp.arange(share_rows, dtype=jnp.int32)
    row_lengths = jnp.broadcast_to(doc_lengths, (share_rows, doc_lengths.shape[1]))
    own_grad = kva_rows_grad(shared, own_latent, norm_gain, positions(row_lengths, token_index))
    kva_grad = lax.all_gather(own_grad, "head", axis=0, tiled=True)
    hidden_grad = lax.dot_general(kva_grad, down_proj, LAST, preferred_element_type=F32).astype(BF16)
    weight_grad = lax.psum_scatter(
        lax.dot_general(kva_grad, hidden, FIRST, preferred_element_type=F32),
        "group",
        scatter_dimension=0,
        tiled=True,
    )
    return (hidden_grad, weight_grad)


def partial_kernel(
    index, lengths,
    kg_a, kg_b, vg_a, vg_b, rg_a, rg_b, kl, vl, lat_a, lat_b, gain, freq,
    out_a, out_b, acc, rope_acc, values, rows,
    *, which, block,
):
    step = pl.program_id(0)
    share = kg_a.shape[0]
    rope = rope_acc.shape[0]
    latent = acc.shape[0]

    @pl.when(step == 0)
    def _():
        acc[...] = jnp.zeros_like(acc)
        rope_acc[...] = jnp.zeros_like(rope_acc)
        values[:, :share] = lat_a[...].astype(F32).T
        values[:, share:] = lat_b[...].astype(F32).T

    keys = jnp.concatenate([kg_a[...], kg_b[...]], axis=0)
    vals = jnp.concatenate([vg_a[...], vg_b[...]], axis=0)
    acc[...] += lax.dot_general(kl[...], keys, LAST, preferred_element_type=F32) + lax.dot_general(
        vl[...], vals, LAST, preferred_element_type=F32
    )
    ropes = jnp.concatenate([rg_a[...], rg_b[...]], axis=0)
    fold_shape = (rope, ropes.shape[1])
    fold = lax.rem(lax.broadcasted_iota(jnp.int32, fold_shape, 1), rope) == lax.broadcasted_iota(
        jnp.int32, fold_shape, 0
    )
    rope_acc[...] += lax.dot_general(fold.astype(BF16), ropes, LAST, preferred_element_type=F32)

    @pl.when(step == pl.num_programs(0) - 1)
    def _():
        gains = jnp.broadcast_to(gain[...], (share, latent)).T
        half = rope // 2
        lane = lax.broadcasted_iota(jnp.int32, (1, share), 1)
        for side in range(2):
            lanes = slice(side * share, (side + 1) * share)
            c = values[:, lanes]
            inv = lax.rsqrt(jnp.mean(c * c, axis=0, keepdims=True) + 1e-06)
            g = acc[:, lanes] * gains
            mean = jnp.mean(g * c, axis=0, keepdims=True)
            rows[:latent, lanes] = inv * (g - c * (inv * inv * mean))
            token = index[which[side]] * share + lane
            start = jnp.zeros_like(token)
            end = jnp.int32(0)
            for doc in range(lengths.shape[1]):
                end = end + lengths[0, doc]
                start = jnp.maximum(start, jnp.where(end <= token, end, 0))
            angle = (token - start).astype(F32) * freq[...]
            cosine, sine = jnp.cos(angle), jnp.sin(angle)
            first, second = rope_acc[:half, lanes], rope_acc[half:, lanes]
            rows[latent : latent + half, lanes] = first * cosine + second * sine
            rows[latent + half :, lanes] = second * cosine - first * sine
        blocks = rows.shape[0] // block
        ordered = jnp.concatenate(
            [rows[pl.ds(pl.multiple_of(index[4 + i] * block, 8), block), :] for i in range(blocks)], axis=0
        )
        out_a[...] = ordered[:, :share].astype(out_a.dtype)
        out_b[...] = ordered[:, share:].astype(out_b.dtype)


def partial_terms(which, out_dtype, index, doc_lengths, kg, vg, rg, kl, vl, latent, gain, freq, share, block):
    tokens, key_cols = kg.shape
    width = latent.shape[1]
    rope = 2 * freq.shape[0]
    kva = width + rope
    steps = max(1, key_cols // 512)
    key_block, rope_block = key_cols // steps, rg.shape[1] // steps
    a, b = which

    def grad_spec(cols, side):
        return pl.BlockSpec((share, cols), lambda k, ix, ln: (ix[side], k))

    def lift_spec():
        return pl.BlockSpec((width, key_block), lambda k, ix, ln: (0, k))

    def latent_spec(side):
        return pl.BlockSpec((share, width), lambda k, ix, ln: (ix[side], 0))

    def whole(shape):
        return pl.BlockSpec(shape, lambda k, ix, ln: (0,) * len(shape))

    return pl.pallas_call(
        functools.partial(partial_kernel, which=which, block=block),
        grid_spec=pltpu.PrefetchScalarGridSpec(
            num_scalar_prefetch=2,
            grid=(steps,),
            in_specs=[
                grad_spec(key_block, a), grad_spec(key_block, b),
                grad_spec(key_block, a), grad_spec(key_block, b),
                grad_spec(rope_block, a), grad_spec(rope_block, b),
                lift_spec(), lift_spec(),
                latent_spec(a), latent_spec(b),
                whole((1, width)), whole(freq.shape),
            ],
            out_specs=[whole((kva, share))] * 2,
            scratch_shapes=[
                pltpu.VMEM((width, 2 * share), F32),
                pltpu.VMEM((rope, 2 * share), F32),
                pltpu.VMEM((width, 2 * share), F32),
                pltpu.VMEM((kva, 2 * share), F32),
            ],
        ),
        out_shape=[jax.ShapeDtypeStruct((kva, share), out_dtype)] * 2,
        compiler_params=pltpu.CompilerParams(vmem_limit_bytes=24 * MIB),
        cost_estimate=pl.CostEstimate(
            flops=2 * 2 * share * width * key_cols * 2,
            bytes_accessed=2 * (2 * width * key_cols + 2 * share * (2 * key_cols + rg.shape[1])),
            transcendentals=0,
        ),
        name="partial_terms",
    )(index, doc_lengths, kg, kg, vg, vg, rg, rg, kl, vl, latent, latent, gain, freq)


def weight_kernel(index, *refs):
    own, sibling, own_hidden, sibling_hidden = refs[:4], refs[4:8], refs[8:12], refs[12:16]
    send, keep = refs[16:18]
    half = own[0].shape[0] // 2
    left = jnp.concatenate([r[:half] for r in own] + [r[half:] for r in sibling], axis=1)
    right = jnp.concatenate([r[...] for r in own_hidden] + [r[...] for r in sibling_hidden], axis=0)
    result = jnp.dot(left, right, preferred_element_type=F32)
    send[...] = result[: half // 2].astype(send.dtype)
    keep[...] = result[half // 2 :]


def weight_terms(index, own, sibling, hidden, sibling_hidden):
    kva, share = own[0].shape
    columns = hidden.shape[1]
    col_block = columns // 2 if columns % 256 == 0 else columns
    quarter = kva // 4

    def hidden_spec(r):
        return pl.BlockSpec((share, col_block), lambda n, ix: (ix[r], n))

    whole = pl.BlockSpec((kva, share), lambda n, ix: (0, 0))
    out = pl.BlockSpec((quarter, col_block), lambda n, ix: (0, n))
    return pl.pallas_call(
        weight_kernel,
        grid_spec=pltpu.PrefetchScalarGridSpec(
            num_scalar_prefetch=1,
            grid=(columns // col_block,),
            in_specs=[whole] * 8 + [hidden_spec(r) for r in range(4)] * 2,
            out_specs=[out, out],
        ),
        out_shape=[
            jax.ShapeDtypeStruct((quarter, columns), BF16),
            jax.ShapeDtypeStruct((quarter, columns), F32),
        ],
        compiler_params=pltpu.CompilerParams(vmem_limit_bytes=32 * MIB),
        cost_estimate=pl.CostEstimate(
            flops=2 * (kva // 2) * 8 * share * columns, bytes_accessed=8 * MIB, transcendentals=0
        ),
        name="weight_terms",
    )(index, *own, *sibling, *([hidden] * 4), *([sibling_hidden] * 4))


def hidden_kernel(index, q0, q1, q2, q3, down_t, out, kva, natural, *, block):
    share = q0.shape[1]

    @pl.when(pl.program_id(0) == 0)
    def _():
        for r, q in enumerate((q0, q1, q2, q3)):
            ordered = q[...].astype(F32)
            for i in range(ordered.shape[0] // block):
                natural[pl.ds(pl.multiple_of(index[4 + i] * block, 8), block), :] = ordered[
                    i * block : (i + 1) * block
                ]
            kva[pl.ds(pl.multiple_of(index[r] * share, 128), share), :] = natural[...].T.astype(BF16)

    out[...] = jnp.dot(kva[...], down_t[...], preferred_element_type=F32).astype(out.dtype)


def hidden_terms(index, gathered, down_t, block):
    kva, share = gathered[0].shape
    columns = down_t.shape[1]
    col_block = columns // 2 if columns % 256 == 0 else columns
    tokens = 4 * share
    whole = pl.BlockSpec((kva, share), lambda n, ix: (0, 0))
    return pl.pallas_call(
        functools.partial(hidden_kernel, block=block),
        grid_spec=pltpu.PrefetchScalarGridSpec(
            num_scalar_prefetch=1,
            grid=(columns // col_block,),
            in_specs=[whole] * 4 + [pl.BlockSpec((kva, col_block), lambda n, ix: (0, n))],
            out_specs=pl.BlockSpec((tokens, col_block), lambda n, ix: (0, n)),
            scratch_shapes=[pltpu.VMEM((tokens, kva), BF16), pltpu.VMEM((kva, share), F32)],
        ),
        out_shape=jax.ShapeDtypeStruct((tokens, columns), BF16),
        compiler_params=pltpu.CompilerParams(vmem_limit_bytes=32 * MIB),
        cost_estimate=pl.CostEstimate(
            flops=2 * tokens * kva * columns, bytes_accessed=5 * MIB, transcendentals=0
        ),
        name="hidden_terms",
    )(index, *gathered, down_t)


def on_device(
    key_grad, value_grad, rope_grad, key_lift, value_lift, latent, norm_gain, doc_lengths, hidden, down_proj
):
    heads, groups = 4, 8
    core_bit, x_bit, y_bit = 1, 2, 4
    share = key_grad.shape[0] // heads
    kva = down_proj.shape[1]
    block = kva // groups
    half = (kva - latent.shape[1]) // 2

    def swap_head(array, bits):
        return lax.ppermute(array, "head", [(i, i ^ bits) for i in range(heads)])

    def swap_group(array, bits_of):
        return lax.ppermute(array, "group", [(i, i ^ bits_of(i)) for i in range(groups)])

    def first_bit(i):
        return y_bit if i & core_bit else x_bit

    def second_bit(i):
        return x_bit if i & core_bit else y_bit

    me, mine = lax.axis_index("head"), lax.axis_index("group")
    other = mine ^ core_bit
    first = jnp.where(mine & core_bit == 0, x_bit, y_bit)
    second = first ^ (x_bit | y_bit)
    both = x_bit | y_bit
    index = jnp.stack(
        [me, me ^ 1, me ^ 2, me ^ 3]
        + [mine ^ both, mine ^ first, mine ^ second, mine]
        + [other ^ both, other ^ second, other ^ first, other]
    ).astype(jnp.int32)

    freq = 10000.0 ** (-(2.0 * np.arange(half)) / (2.0 * half))
    freq = jnp.asarray(np.broadcast_to(freq[:, None], (half, share)), F32)
    gain = norm_gain.reshape(1, -1)
    sibling_hidden = swap_group(hidden, lambda i: core_bit)

    def terms(which, dtype):
        return partial_terms(
            which, dtype, index, doc_lengths, key_grad, value_grad, rope_grad, key_lift, value_lift,
            latent, gain, freq, share, block,
        )

    p3, p1 = terms((3, 1), BF16)
    got3 = swap_head(p3, 1)
    got1 = swap_head(p1, 1)
    p2, p0 = terms((2, 0), F32)
    pair2 = (p2 + got3.astype(F32)).astype(BF16)
    got2 = swap_head(pair2, 2)
    q0 = (p0 + got1.astype(F32) + got2.astype(F32)).astype(BF16)
    q2 = swap_head(q0, 2)
    q1 = swap_head(q0, 1)
    q3 = swap_head(q2, 1)
    gathered = (q0, q1, q2, q3)
    sibling = tuple(swap_group(q, lambda i: core_bit) for q in gathered)

    send, keep = weight_terms(index, gathered, sibling, hidden, sibling_hidden)
    got = swap_group(send, first_bit)
    hidden_grad = hidden_terms(index, gathered, down_proj.T, block)
    summed = keep + got.astype(F32)
    last = swap_group(summed[:block].astype(BF16), second_bit)
    weight_grad = summed[block:] + last.astype(F32)
    return (hidden_grad, weight_grad)


def solution(mesh):
    shape = dict(mesh.shape)
    paired = shape["head"] == 4 and shape["group"] == 8
    return jax.shard_map(
        on_device if paired else on_device_any,
        mesh=mesh,
        in_specs=(
            P("group", "head"),
            P("group", "head"),
            P("group", "head"),
            P(None, "head"),
            P(None, "head"),
            P("group", None),
            P(),
            P("group", None),
            P("group", "head"),
            P("head", None),
        ),
        out_specs=(P("group", "head"), P("group", "head")),
        check_vma=False,
    )
```

time: 135 us -> 76.5 us (0.57)
  waiting for transfers between devices: 77.6 us -> 26.8 us
  Pallas kernels: 0 us -> 19.9 us
  blocking collectives: 16 us -> 0 us
  matrix products: 15.8 us -> 0 us
  starting transfers between devices: 0.08 us -> 14.1 us
  between operations: 14.2 us -> 0.74 us
  local copies, waits for them, and re-layouts: 5.22 us -> 13.6 us
  other arithmetic: 6.17 us -> 1.03 us
    reduce_scatter x2 -> x0, waiting for transfers between devices: 77.6 us -> none  [the longest x1 46.8 us: on_device(): lax.psum_scatter(lax.dot_general(kva_grad, hidden, (((0,), (0,)), ((), ()...]
    ppermute x0 -> x13, waiting for transfers between devices: none -> 26.8 us  [the longest x6 16.9 us: swap_head(): return lax.ppermute(array, 'head', [(i, i ^ bits) for i in range(heads)])]
    pallas_call x0 -> x4, Pallas kernels: none -> 19.9 us  [the longest x2 13.3 us: partial_terms(): pl.pallas_call(functools.partial(partial_kernel, which=which, block=block...]
    all_gather x1 -> x0, blocking collectives: 16 us -> none  [on_device(): kva_grad = lax.all_gather(own_grad, 'head', axis=0, tiled=True)]
    dot_general x4 -> x0, matrix products: 15.8 us -> none  [the longest x1 5.96 us: on_device(): lax.dot_general(key_grad, key_lift, contract, preferred_element_type=jnp....]
    ppermute x0 -> x13, starting transfers between devices: none -> 14.1 us  [the longest x6 9.95 us: swap_head(): return lax.ppermute(array, 'head', [(i, i ^ bits) for i in range(heads)])]
    unnamed x12 -> x22, local copies, waits for them, and re-layouts: 4.23 us -> 13.4 us
    reduce_sum x2 -> x0, other arithmetic: 3 us -> none  [the longest x1 1.9 us: on_device(): jnp.sum(rope_grad.reshape(seq_len, heads_here, ROPE), axis=1, dtype=jnp.f...]
  transfers between devices with their start and end apart: 2 -> 13, of which waited for: 2 -> 6; matrix products, arithmetic and copies ran while one was open for 3% -> 0% of each run, Pallas kernels for 0% -> 23%
where the time goes in v1:
time: 76.5 us; the launch traced here: 76.1 us
  waiting for transfers between devices  26.8 us (35%)
  Pallas kernels  19.9 us (26%)
  starting transfers between devices  14.1 us (18%)
  local copies, waits for them, and re-layouts  13.6 us (18%)
  other arithmetic  1.03 us (1%)
    ppermute x6, waiting for transfers between devices, swap_head(): return lax.ppermute(array, 'head', [(i, i ^ bits) for i in range(heads)])  16.9 us
    unnamed x22, local copies, waits for them, and re-layouts  13.4 us
    pallas_call x2, Pallas kernels, partial_terms(): pl.pallas_call(functools.partial(partial_kernel, which=which, block=block...  13.3 us
    ppermute x6, starting transfers between devices, swap_head(): return lax.ppermute(array, 'head', [(i, i ^ bits) for i in range(heads)])  9.95 us
    ppermute x7, waiting for transfers between devices, swap_group(): lax.ppermute(array, 'group', [(i, i ^ bits_of(i)) for i in range(groups)])  9.94 us
    ppermute x7, starting transfers between devices, swap_group(): lax.ppermute(array, 'group', [(i, i ^ bits_of(i)) for i in range(groups)])  4.12 us
    pallas_call x1, Pallas kernels, hidden_terms(): pl.pallas_call(functools.partial(hidden_kernel, block=block), grid_spec=p...  3.89 us
    pallas_call x1, Pallas kernels, weight_terms(): pl.pallas_call(weight_kernel, grid_spec=pltpu.PrefetchScalarGridSpec(num_...  2.72 us
  transfers between devices with their start and end apart: 13, of which 6 were waited for; matrix products, arithmetic and copies ran while one was open for 0% of the time, Pallas kernels for 23%

profile of v1, /device:TPU:0, one launch (start us, length us, event | category | flops | bytes accessed | tf_op | source)
XLA Modules:
  0.0 76.1 jit_solution(11916683244934924281)
XLA Ops:
  0.6 0.5 collective-permute-start.10
  1.1 0.1 stack.51.index
  1.2 2.2 %copy-done = bf16[512,4096]{1,0:T(8,128)(2,1)S(1)} copy-done((bf16[512,4096]{1,0:T(8,128)(2,1)S(1)}, bf16[512,4096]{1,0:T(8,128)(2,1)}, u32[]{:S(2)}) %copy-start) | copy-done | bytes 4194328
  3.4 2.2 %copy-done.1 = bf16[512,4096]{1,0:T(8,128)(2,1)S(1)} copy-done((bf16[512,4096]{1,0:T(8,128)(2,1)S(1)}, bf16[512,4096]{1,0:T(8,128)(2,1)}, u32[]{:S(2)}) %copy-start.1) | copy-done | bytes 4194328
  5.6 1.6 %copy-done.2 = bf16[512,2048]{1,0:T(8,128)(2,1)S(1)} copy-done((bf16[512,2048]{1,0:T(8,128)(2,1)S(1)}, bf16[512,2048]{1,0:T(8,128)(2,1)}, u32[]{:S(2)}) %copy-start.2) | copy-done | bytes 2097176
  7.2 2.2 %copy-done.4 = bf16[512,4096]{1,0:T(8,128)(2,1)S(1)} copy-done((bf16[512,4096]{1,0:T(8,128)(2,1)S(1)}, bf16[512,4096]{1,0:T(8,128)(2,1)}, u32[]{:S(2)}) %copy-start.4) | copy-done | bytes 4194328
  9.4 2.2 %copy-done.5 = bf16[512,4096]{1,0:T(8,128)(2,1)S(1)} copy-done((bf16[512,4096]{1,0:T(8,128)(2,1)S(1)}, bf16[512,4096]{1,0:T(8,128)(2,1)}, u32[]{:S(2)}) %copy-start.5) | copy-done | bytes 4194328
  11.6 1.0 %copy-done.6 = bf16[512,512]{1,0:T(8,128)(2,1)S(1)} copy-done((bf16[512,512]{1,0:T(8,128)(2,1)S(1)}, bf16[512,512]{1,0:T(8,128)(2,1)}, u32[]{:S(2)}) %copy-start.6) | copy-done | bytes 524312
  12.6 0.7 copy-done.8
  13.3 0.7 copy-done.9
  14.0 0.7 copy-done.10
  14.7 6.6 %partial_terms.3 = (bf16[576,128]{1,0:T(8,128)(2,1)S(1)}, bf16[576,128]{1,0:T(8,128)(2,1)S(1)}) custom-call(s32[12]{0:T(128)S(1)} %stack.51.index, s32[1,4]{1,0:T(1,128)S(1)} %copy-done.10, bf16[512,4096]{1,0:T(8,128)(2,1)S(1)} %copy-done, bf16[512,4096]{1,0:T(8,128)(2,1)S(1)} %copy-done, bf16[512,4096]{1,0:T(8,128)(2,1)S(1)} %copy-done.1, ...), custom_call_target="tpu_custom_call" | custom-call | flops 2147483648 | bytes 13631488 | tf_op jit(solution)/shard_map/partial_terms/pallas_call | solution.py:157
  21.3 2.7 %collective-permute-start.1 = (bf16[576,128]{1,0:T(8,128)(2,1)S(1)}, bf16[576,128]{1,0:T(8,128)(2,1)S(1)}, u32[]{:S(2)}, u32[]{:S(2)}) collective-permute-start(bf16[576,128]{1,0:T(8,128)(2,1)S(1)} %get-tuple-element.11), channel_id=1, source_target_pairs={{0,1},{1,0},{2,3},{3,2},{4,5},{5,4},{6,7},{7,6},{8,9},{9,8},{10,11... | collective-permute-start | bytes 442376 | tf_op jit(solution)/shard_map/ppermute | solution.py:282
  24.0 0.1 collective-permute-start
  24.1 6.7 %partial_terms.2 = (f32[576,128]{1,0:T(8,128)S(1)}, f32[576,128]{1,0:T(8,128)S(1)}) custom-call(s32[12]{0:T(128)S(1)} %stack.51.index, s32[1,4]{1,0:T(1,128)S(1)} %copy-done.10, bf16[512,4096]{1,0:T(8,128)(2,1)S(1)} %copy-done, bf16[512,4096]{1,0:T(8,128)(2,1)S(1)} %copy-done, bf16[512,4096]{1,0:T(8,128)(2,1)S(1)} %copy-done.1, ...), custom_call_target="tpu_custom_call" | custom-call | flops 2147483648 | bytes 13631488 | tf_op jit(solution)/shard_map/partial_terms/pallas_call | solution.py:157
  30.8 3.0 %collective-permute-start.2 = (bf16[576,128]{1,0:T(8,128)(2,1)S(1)}, bf16[576,128]{1,0:T(8,128)(2,1)S(1)}, u32[]{:S(2)}, u32[]{:S(2)}) collective-permute-start(bf16[576,128]{1,0:T(8,128)(2,1)S(1)} %add_convert_fusion.1), channel_id=1, source_target_pairs={{0,2},{1,3},{2,0},{3,1},{4,6},{5,7},{6,4},{7,5},{8,10},{9,11},{10,... | collective-permute-start | bytes 442376 | tf_op jit(solution)/shard_map/ppermute | solution.py:282
  33.8 7.1 %collective-permute-done.2 = bf16[576,128]{1,0:T(8,128)(2,1)S(1)} collective-permute-done((bf16[576,128]{1,0:T(8,128)(2,1)S(1)}, bf16[576,128]{1,0:T(8,128)(2,1)S(1)}, u32[]{:S(2)}, u32[]{:S(2)}) %collective-permute-start.2) | collective-permute-done | bytes 147488 | tf_op jit(solution)/shard_map/ppermute | solution.py:282
  40.9 0.1 add_convert_fusion.q0.refs_0_
  41.0 0.1 collective-permute-start.4
  41.0 4.1 %collective-permute-start.3 = (bf16[576,128]{1,0:T(8,128)(2,1)S(1)}, bf16[576,128]{1,0:T(8,128)(2,1)S(1)}, u32[]{:S(2)}, u32[]{:S(2)}) collective-permute-start(bf16[576,128]{1,0:T(8,128)(2,1)S(1)} %add_convert_fusion.q0.refs_0_), channel_id=1, source_target_pairs={{0,1},{1,0},{2,3},{3,2},{4,5},{5,4},{6,7},{7,6},{8,9},{9,8},{10,11... | collective-permute-start | bytes 442376 | tf_op jit(solution)/shard_map/ppermute | solution.py:282
  45.1 5.2 %collective-permute-done.4.q2.refs_2_ = bf16[576,128]{1,0:T(8,128)(2,1)S(1)} collective-permute-done((bf16[576,128]{1,0:T(8,128)(2,1)S(1)}, bf16[576,128]{1,0:T(8,128)(2,1)S(1)}, u32[]{:S(2)}, u32[]{:S(2)}) %collective-permute-start.4) | collective-permute-done | bytes 147488 | tf_op jit(solution)/shard_map/ppermute | solution.py:282
  50.3 0.5 collective-permute-start.8
  50.8 4.6 %collective-permute-done.5.q3.refs_3_ = bf16[576,128]{1,0:T(8,128)(2,1)S(1)} collective-permute-done((bf16[576,128]{1,0:T(8,128)(2,1)S(1)}, bf16[576,128]{1,0:T(8,128)(2,1)S(1)}, u32[]{:S(2)}, u32[]{:S(2)}) %collective-permute-start.5) | collective-permute-done | bytes 147488 | tf_op jit(solution)/shard_map/ppermute | solution.py:282
  55.5 1.3 %collective-permute-done.9.refs_7_ = bf16[576,128]{1,0:T(8,128)(2,1)S(1)} collective-permute-done((bf16[576,128]{1,0:T(8,128)(2,1)S(1)}, bf16[576,128]{1,0:T(8,128)(2,1)S(1)}, u32[]{:S(2)}, u32[]{:S(2)}) %collective-permute-start.9) | collective-permute-done | bytes 147488 | tf_op jit(solution)/shard_map/ppermute | solution.py:285
  56.8 2.7 %weight_terms.1 = (bf16[144,1792]{1,0:T(8,128)(2,1)S(1)}, f32[144,1792]{1,0:T(8,128)S(1)}) custom-call(s32[12]{0:T(128)S(1)} %stack.51.index, bf16[576,128]{1,0:T(8,128)(2,1)S(1)} %add_convert_fusion.q0.refs_0_, bf16[576,128]{1,0:T(8,128)(2,1)S(1)} %collective-permute-done.3.q1.refs_1_, bf16[576,128]{1,0:T(8,128)(2,1)S(1)} %collective-permute-done.4.q2.refs_2_, ...), custom_call_target="tpu_custom_call" | custom-call | flops 1056964608 | bytes 8388608 | tf_op jit(solution)/shard_map/weight_terms/pallas_call | solution.py:211
  59.6 1.5 %collective-permute-start.11 = (bf16[144,1792]{1,0:T(8,128)(2,1)S(1)}, bf16[144,1792]{1,0:T(8,128)(2,1)S(1)}, u32[]{:S(2)}, u32[]{:S(2)}) collective-permute-start(bf16[144,1792]{1,0:T(8,128)(2,1)S(1)} %get-tuple-element.13), channel_id=1, source_target_pairs={{0,8},{4,20},{8,0},{12,28},{16,24},{20,4},{24,16},{28,12},{1,9},{5... | collective-permute-start | bytes 1548296 | tf_op jit(solution)/shard_map/ppermute | solution.py:285
  61.1 7.6 %collective-permute-done.11 = bf16[144,1792]{1,0:T(8,128)(2,1)S(1)} collective-permute-done((bf16[144,1792]{1,0:T(8,128)(2,1)S(1)}, bf16[144,1792]{1,0:T(8,128)(2,1)S(1)}, u32[]{:S(2)}, u32[]{:S(2)}) %collective-permute-start.11) | collective-permute-done | bytes 516128 | tf_op jit(solution)/shard_map/ppermute | solution.py:285
  68.7 0.1 convert_add_fusion
  68.9 1.6 %collective-permute-start.12 = (bf16[72,1792]{1,0:T(8,128)(2,1)S(1)}, bf16[72,1792]{1,0:T(8,128)(2,1)S(1)}, u32[]{:S(2)}, u32[]{:S(2)}) collective-permute-start(bf16[72,1792]{1,0:T(8,128)(2,1)S(1)} %slice.13), channel_id=1, source_target_pairs={{0,16},{4,12},{8,24},{12,4},{16,0},{20,28},{24,8},{28,20},{1,17},{... | collective-permute-start | bytes 774152 | tf_op jit(solution)/shard_map/ppermute | solution.py:285
  70.4 3.9 %hidden_terms.1 = bf16[512,1792]{1,0:T(8,128)(2,1)} custom-call(s32[12]{0:T(128)S(1)} %stack.51.index, bf16[576,128]{1,0:T(8,128)(2,1)S(1)} %add_convert_fusion.q0.refs_0_, bf16[576,128]{1,0:T(8,128)(2,1)S(1)} %collective-permute-done.3.q1.refs_1_, bf16[576,128]{1,0:T(8,128)(2,1)S(1)} %collective-permute-done.4.q2.refs_2_, ...), custom_call_target="tpu_custom_call" | custom-call | flops 1056964608 | bytes 5242880 | tf_op jit(solution)/shard_map/hidden_terms/pallas_call | solution.py:253
  74.3 0.9 %collective-permute-done.12 = bf16[72,1792]{1,0:T(8,128)(2,1)S(1)} collective-permute-done((bf16[72,1792]{1,0:T(8,128)(2,1)S(1)}, bf16[72,1792]{1,0:T(8,128)(2,1)S(1)}, u32[]{:S(2)}, u32[]{:S(2)}) %collective-permute-start.12) | collective-permute-done | bytes 258080 | tf_op jit(solution)/shard_map/ppermute | solution.py:285
  75.3 0.8 %slice_add_fusion = f32[72,1792]{1,0:T(8,128)} fusion(f32[144,1792]{1,0:T(8,128)S(1)} %convert_add_fusion, bf16[72,1792]{1,0:T(8,128)(2,1)S(1)} %collective-permute-done.12), kind=kLoop, calls=%fused_computation.2 | loop fusion | flops 258048 | bytes 1290240 | tf_op jit(solution)/shard_map/add | solution.py:333
  (26 shorter events, 0.1 us)
Async XLA Ops:
  0.6 56.2 %collective-permute-start.10 = (bf16[512,1792]{1,0:T(8,128)(2,1)}, bf16[512,1792]{1,0:T(8,128)(2,1)S(1)}, u32[]{:S(2)}, u32[]{:S(2)}) collective-permute-start(bf16[512,1792]{1,0:T(8,128)(2,1)} %refs_11_.1), channel_id=1, source_target_pairs={{0,4},{4,0},{8,12},{12,8},{16,20},{20,16},{24,28},{28,24},{1,5},{5... | collective-permute-start | bytes 5505032 | tf_op jit(solution)/shard_map/ppermute | solution.py:285
  1.2 2.2 %copy-start = (bf16[512,4096]{1,0:T(8,128)(2,1)S(1)}, bf16[512,4096]{1,0:T(8,128)(2,1)}, u32[]{:S(2)}) copy-start(bf16[512,4096]{1,0:T(8,128)(2,1)} %kg_b.3) | copy-start | bytes 12582916
  3.4 2.2 %copy-start.1 = (bf16[512,4096]{1,0:T(8,128)(2,1)S(1)}, bf16[512,4096]{1,0:T(8,128)(2,1)}, u32[]{:S(2)}) copy-start(bf16[512,4096]{1,0:T(8,128)(2,1)} %vg_b.3) | copy-start | bytes 12582916
  5.6 1.6 %copy-start.2 = (bf16[512,2048]{1,0:T(8,128)(2,1)S(1)}, bf16[512,2048]{1,0:T(8,128)(2,1)}, u32[]{:S(2)}) copy-start(bf16[512,2048]{1,0:T(8,128)(2,1)} %rg_b.3) | copy-start | bytes 6291460
  7.2 2.2 %copy-start.4 = (bf16[512,4096]{1,0:T(8,128)(2,1)S(1)}, bf16[512,4096]{1,0:T(8,128)(2,1)}, u32[]{:S(2)}) copy-start(bf16[512,4096]{1,0:T(8,128)(2,1)} %kl.3) | copy-start | bytes 12582916
  9.4 2.2 %copy-start.5 = (bf16[512,4096]{1,0:T(8,128)(2,1)S(1)}, bf16[512,4096]{1,0:T(8,128)(2,1)}, u32[]{:S(2)}) copy-start(bf16[512,4096]{1,0:T(8,128)(2,1)} %vl.3) | copy-start | bytes 12582916
  11.6 1.0 %copy-start.6 = (bf16[512,512]{1,0:T(8,128)(2,1)S(1)}, bf16[512,512]{1,0:T(8,128)(2,1)}, u32[]{:S(2)}) copy-start(bf16[512,512]{1,0:T(8,128)(2,1)} %lat_b.3) | copy-start | bytes 1572868
  12.6 0.7 copy-start.8
  13.3 0.7 copy-start.9
  14.0 0.7 copy-start.10
  21.3 9.4 %collective-permute-start.1 = (bf16[576,128]{1,0:T(8,128)(2,1)S(1)}, bf16[576,128]{1,0:T(8,128)(2,1)S(1)}, u32[]{:S(2)}, u32[]{:S(2)}) collective-permute-start(bf16[576,128]{1,0:T(8,128)(2,1)S(1)} %get-tuple-element.11), channel_id=1, source_target_pairs={{0,1},{1,0},{2,3},{3,2},{4,5},{5,4},{6,7},{7,6},{8,9},{9,8},{10,11... | collective-permute-start | bytes 442376 | tf_op jit(solution)/shard_map/ppermute | solution.py:282
  24.0 9.8 %collective-permute-start = (bf16[576,128]{1,0:T(8,128)(2,1)S(1)}, bf16[576,128]{1,0:T(8,128)(2,1)S(1)}, u32[]{:S(2)}, u32[]{:S(2)}) collective-permute-start(bf16[576,128]{1,0:T(8,128)(2,1)S(1)} %get-tuple-element.9), channel_id=1, source_target_pairs={{0,1},{1,0},{2,3},{3,2},{4,5},{5,4},{6,7},{7,6},{8,9},{9,8},{10,11... | collective-permute-start | bytes 442376 | tf_op jit(solution)/shard_map/ppermute | solution.py:282
  24.1 32.8 %copy-start.3 = (bf16[512,1792]{1,0:T(8,128)(2,1)S(1)}, bf16[512,1792]{1,0:T(8,128)(2,1)}, u32[]{:S(2)}) copy-start(bf16[512,1792]{1,0:T(8,128)(2,1)} %refs_11_.1) | copy-start | bytes 5505028
  30.8 10.1 %collective-permute-start.2 = (bf16[576,128]{1,0:T(8,128)(2,1)S(1)}, bf16[576,128]{1,0:T(8,128)(2,1)S(1)}, u32[]{:S(2)}, u32[]{:S(2)}) collective-permute-start(bf16[576,128]{1,0:T(8,128)(2,1)S(1)} %add_convert_fusion.1), channel_id=1, source_target_pairs={{0,2},{1,3},{2,0},{3,1},{4,6},{5,7},{6,4},{7,5},{8,10},{9,11},{10,... | collective-permute-start | bytes 442376 | tf_op jit(solution)/shard_map/ppermute | solution.py:282
  41.0 9.3 %collective-permute-start.4 = (bf16[576,128]{1,0:T(8,128)(2,1)S(1)}, bf16[576,128]{1,0:T(8,128)(2,1)S(1)}, u32[]{:S(2)}, u32[]{:S(2)}) collective-permute-start(bf16[576,128]{1,0:T(8,128)(2,1)S(1)} %add_convert_fusion.q0.refs_0_), channel_id=1, source_target_pairs={{0,2},{1,3},{2,0},{3,1},{4,6},{5,7},{6,4},{7,5},{8,10},{9,11},{10,... | collective-permute-start | bytes 442376 | tf_op jit(solution)/shard_map/ppermute | solution.py:282
  41.0 9.8 %collective-permute-start.3 = (bf16[576,128]{1,0:T(8,128)(2,1)S(1)}, bf16[576,128]{1,0:T(8,128)(2,1)S(1)}, u32[]{:S(2)}, u32[]{:S(2)}) collective-permute-start(bf16[576,128]{1,0:T(8,128)(2,1)S(1)} %add_convert_fusion.q0.refs_0_), channel_id=1, source_target_pairs={{0,1},{1,0},{2,3},{3,2},{4,5},{5,4},{6,7},{7,6},{8,9},{9,8},{10,11... | collective-permute-start | bytes 442376 | tf_op jit(solution)/shard_map/ppermute | solution.py:282
  50.3 5.1 %collective-permute-start.5 = (bf16[576,128]{1,0:T(8,128)(2,1)S(1)}, bf16[576,128]{1,0:T(8,128)(2,1)S(1)}, u32[]{:S(2)}, u32[]{:S(2)}) collective-permute-start(bf16[576,128]{1,0:T(8,128)(2,1)S(1)} %collective-permute-done.4.q2.refs_2_), channel_id=1, source_target_pairs={{0,1},{1,0},{2,3},{3,2},{4,5},{5,4},{6,7},{7,6},{8,9},{9,8},{10,11... | collective-permute-start | bytes 442376 | tf_op jit(solution)/shard_map/ppermute | solution.py:282
  50.3 5.1 %collective-permute-start.6 = (bf16[576,128]{1,0:T(8,128)(2,1)S(1)}, bf16[576,128]{1,0:T(8,128)(2,1)S(1)}, u32[]{:S(2)}, u32[]{:S(2)}) collective-permute-start(bf16[576,128]{1,0:T(8,128)(2,1)S(1)} %add_convert_fusion.q0.refs_0_), channel_id=1, source_target_pairs={{0,4},{4,0},{8,12},{12,8},{16,20},{20,16},{24,28},{28,24},{1,5},{5... | collective-permute-start | bytes 442376 | tf_op jit(solution)/shard_map/ppermute | solution.py:285
  50.3 5.2 %collective-permute-start.8 = (bf16[576,128]{1,0:T(8,128)(2,1)S(1)}, bf16[576,128]{1,0:T(8,128)(2,1)S(1)}, u32[]{:S(2)}, u32[]{:S(2)}) collective-permute-start(bf16[576,128]{1,0:T(8,128)(2,1)S(1)} %collective-permute-done.4.q2.refs_2_), channel_id=1, source_target_pairs={{0,4},{4,0},{8,12},{12,8},{16,20},{20,16},{24,28},{28,24},{1,5},{5... | collective-permute-start | bytes 442376 | tf_op jit(solution)/shard_map/ppermute | solution.py:285
  50.8 4.6 %collective-permute-start.7 = (bf16[576,128]{1,0:T(8,128)(2,1)S(1)}, bf16[576,128]{1,0:T(8,128)(2,1)S(1)}, u32[]{:S(2)}, u32[]{:S(2)}) collective-permute-start(bf16[576,128]{1,0:T(8,128)(2,1)S(1)} %collective-permute-done.3.q1.refs_1_), channel_id=1, source_target_pairs={{0,4},{4,0},{8,12},{12,8},{16,20},{20,16},{24,28},{28,24},{1,5},{5... | collective-permute-start | bytes 442376 | tf_op jit(solution)/shard_map/ppermute | solution.py:285
  55.5 1.4 %collective-permute-start.9 = (bf16[576,128]{1,0:T(8,128)(2,1)S(1)}, bf16[576,128]{1,0:T(8,128)(2,1)S(1)}, u32[]{:S(2)}, u32[]{:S(2)}) collective-permute-start(bf16[576,128]{1,0:T(8,128)(2,1)S(1)} %collective-permute-done.5.q3.refs_3_), channel_id=1, source_target_pairs={{0,4},{4,0},{8,12},{12,8},{16,20},{20,16},{24,28},{28,24},{1,5},{5... | collective-permute-start | bytes 442376 | tf_op jit(solution)/shard_map/ppermute | solution.py:285
  59.6 10.9 %copy-start.7 = (bf16[1792,576]{0,1:T(8,128)(2,1)S(1)}, bf16[1792,576]{0,1:T(8,128)(2,1)}, u32[]{:S(2)}) copy-start(bf16[1792,576]{0,1:T(8,128)(2,1)} %param.20) | copy-start | bytes 6193156
  59.6 9.2 %collective-permute-start.11 = (bf16[144,1792]{1,0:T(8,128)(2,1)S(1)}, bf16[144,1792]{1,0:T(8,128)(2,1)S(1)}, u32[]{:S(2)}, u32[]{:S(2)}) collective-permute-start(bf16[144,1792]{1,0:T(8,128)(2,1)S(1)} %get-tuple-element.13), channel_id=1, source_target_pairs={{0,8},{4,20},{8,0},{12,28},{16,24},{20,4},{24,16},{28,12},{1,9},{5... | collective-permute-start | bytes 1548296 | tf_op jit(solution)/shard_map/ppermute | solution.py:285
  68.9 6.4 %collective-permute-start.12 = (bf16[72,1792]{1,0:T(8,128)(2,1)S(1)}, bf16[72,1792]{1,0:T(8,128)(2,1)S(1)}, u32[]{:S(2)}, u32[]{:S(2)}) collective-permute-start(bf16[72,1792]{1,0:T(8,128)(2,1)S(1)} %slice.13), channel_id=1, source_target_pairs={{0,16},{4,12},{8,24},{12,4},{16,0},{20,28},{24,8},{28,20},{1,17},{... | collective-permute-start | bytes 774152 | tf_op jit(solution)/shard_map/ppermute | solution.py:285

commit v2 on v1

v2 whole, which is shorter than its diff:
```python
import functools
import math

import jax
import jax.numpy as jnp
from jax import lax
from jax.experimental import pallas as pl
from jax.experimental.pallas import tpu as pltpu
from jax.sharding import PartitionSpec as P

F32 = jnp.float32
BF16 = jnp.bfloat16
LAST = (((1,), (1,)), ((), ()))
FIRST = (((0,), (0,)), ((), ()))
MIB = 1 << 20


def positions(lengths, token_index):
    doc_ends = jnp.cumsum(lengths, axis=1)
    doc_start = jnp.max(jnp.where(doc_ends <= token_index[:, None], doc_ends, 0), axis=1)
    return token_index - doc_start


def kva_rows_grad(stacked, latent, norm_gain, position):
    width = latent.shape[1]
    latent_part = stacked[:, :width]
    rotary_part = stacked[:, width:]
    values = latent.astype(F32)
    inverse_rms = lax.rsqrt(jnp.mean(values * values, axis=1, keepdims=True) + 1e-06)
    scaled_grad = latent_part * norm_gain[None, :]
    norm_grad = inverse_rms * (
        scaled_grad
        - values * inverse_rms * inverse_rms * jnp.mean(scaled_grad * values, axis=1, keepdims=True)
    )
    half_width = rotary_part.shape[1] // 2
    inv_freq = 10000.0 ** (-(2.0 * jnp.arange(half_width, dtype=F32)) / (2.0 * half_width))
    angles = position.astype(F32)[:, None] * inv_freq[None, :]
    cosine = jnp.cos(angles)
    sine = jnp.sin(angles)
    first_half = rotary_part[:, :half_width]
    second_half = rotary_part[:, half_width:]
    rot_first = first_half * cosine + second_half * sine
    rot_second = second_half * cosine - first_half * sine
    return jnp.concatenate([norm_grad, rot_first, rot_second], axis=1).astype(BF16)


def on_device_any(
    key_grad, value_grad, rope_grad, key_lift, value_lift, latent, norm_gain, doc_lengths, hidden, down_proj
):
    seq_len = key_grad.shape[0]
    rope = down_proj.shape[1] - latent.shape[1]
    head_terms = lax.dot_general(key_grad, key_lift, LAST, preferred_element_type=F32)
    head_terms = head_terms + lax.dot_general(value_grad, value_lift, LAST, preferred_element_type=F32)
    heads_here = rope_grad.shape[1] // rope
    rope_terms = jnp.sum(rope_grad.reshape(seq_len, heads_here, rope), axis=1, dtype=F32)
    stacked = jnp.concatenate([head_terms, rope_terms], axis=1)
    shared = lax.psum_scatter(stacked, "head", scatter_dimension=0, tiled=True)
    share_rows = shared.shape[0]
    first_row = lax.axis_index("head") * share_rows
    own_latent = lax.dynamic_slice_in_dim(latent, first_row, share_rows, 0)
    token_index = first_row + jnp.arange(share_rows, dtype=jnp.int32)
    row_lengths = jnp.broadcast_to(doc_lengths, (share_rows, doc_lengths.shape[1]))
    own_grad = kva_rows_grad(shared, own_latent, norm_gain, positions(row_lengths, token_index))
    kva_grad = lax.all_gather(own_grad, "head", axis=0, tiled=True)
    hidden_grad = lax.dot_general(kva_grad, down_proj, LAST, preferred_element_type=F32).astype(BF16)
    weight_grad = lax.psum_scatter(
        lax.dot_general(kva_grad, hidden, FIRST, preferred_element_type=F32),
        "group",
        scatter_dimension=0,
        tiled=True,
    )
    return (hidden_grad, weight_grad)


def axis_bits():
    return 1, 2, 4


def row_order(blocks):
    core, x, y = axis_bits()
    mine = lax.axis_index("group")
    first = jnp.where(mine & core == 0, x, y)
    other, second, both = mine ^ core, first ^ (x | y), x | y
    order = [mine ^ both, mine ^ first, mine ^ second, mine]
    order += [other ^ both, other ^ second, other ^ first, other]
    assert len(order) == blocks
    return order


def partial_kernel(
    lengths, kg, vg, rg, kl, vl, lat, gain,
    out_a, out_b, kg_v, vg_v, rg_v, kl_v, vl_v, lat_v, gain_v, lengths_s, sems, acc, rope_acc, values, turns, rows,
    *, which, block, chunks,
):
    share = out_a.shape[1]
    latent, rope = acc.shape[0], rope_acc.shape[0]
    half = rope // 2
    shares = [lax.axis_index("head") ^ r for r in which]
    places = [pl.ds(pl.multiple_of(r * share, share), share) for r in shares]
    sides = [slice(side * share, (side + 1) * share) for side in range(2)]

    def columns(ref, chunk):
        width = ref.shape[1] // chunks
        return slice(chunk * width, (chunk + 1) * width)

    def copies_of(chunk):
        pairs = [
            (src.at[:, columns(src, chunk)], dst.at[:, columns(src, chunk)])
            for src, dst in ((kl, kl_v), (vl, vl_v))
        ]
        for src, dst in ((kg, kg_v), (vg, vg_v), (rg, rg_v)):
            for place, side in zip(places, sides):
                pairs.append((src.at[place, columns(src, chunk)], dst.at[side, columns(src, chunk)]))
        return [pltpu.make_async_copy(src, dst, sems.at[chunk, i]) for i, (src, dst) in enumerate(pairs)]

    small_copies = [
        pltpu.make_async_copy(lat.at[place, :], lat_v.at[side, :], sems.at[chunks, i])
        for i, (place, side) in enumerate(zip(places, sides))
    ]
    small_copies.append(pltpu.make_async_copy(gain, gain_v, sems.at[chunks, 2]))
    small_copies.append(pltpu.make_async_copy(lengths, lengths_s, sems.at[chunks, 3]))
    all_copies = [copies_of(chunk) for chunk in range(chunks)]
    for copy in all_copies[0] + small_copies + [copy for copies in all_copies[1:] for copy in copies]:
        copy.start()

    fold_shape = (rope, rg.shape[1] // chunks)
    fold = lax.rem(lax.broadcasted_iota(jnp.int32, fold_shape, 1), rope) == lax.broadcasted_iota(
        jnp.int32, fold_shape, 0
    )
    fold = fold.astype(BF16)

    for chunk in range(chunks):
        for copy in all_copies[chunk]:
            copy.wait()
        here = columns(kg, chunk)
        term = lax.dot_general(kl_v[:, here], kg_v[:, here], LAST, preferred_element_type=F32)
        term += lax.dot_general(vl_v[:, here], vg_v[:, here], LAST, preferred_element_type=F32)
        rope_term = lax.dot_general(fold, rg_v[:, columns(rg, chunk)], LAST, preferred_element_type=F32)
        acc[...] = term if chunk == 0 else acc[...] + term
        rope_acc[...] = rope_term if chunk == 0 else rope_acc[...] + rope_term
        if chunk == 0:
            for copy in small_copies:
                copy.wait()
            values[...] = lat_v[...].astype(F32).T
            lane = lax.broadcasted_iota(jnp.int32, (1, share), 1)
            pair = lax.broadcasted_iota(jnp.int32, (half, share), 0).astype(F32)
            freq = jnp.exp(pair * (-math.log(10000.0) / half))
            for r, side in zip(shares, sides):
                token = r * share + lane
                start = jnp.zeros_like(token)
                end = jnp.int32(0)
                for doc in range(lengths.shape[1]):
                    end = end + lengths_s[0, doc]
                    start = jnp.maximum(start, jnp.where(end <= token, end, 0))
                angle = (token - start).astype(F32) * freq
                turns[:half, side] = jnp.cos(angle)
                turns[half:, side] = jnp.sin(angle)

    gains = jnp.broadcast_to(gain_v[...], (share, latent)).T
    gains = jnp.concatenate([gains, gains], axis=1)
    c = values[...]
    inv = lax.rsqrt(jnp.mean(c * c, axis=0, keepdims=True) + 1e-06)
    g = acc[...] * gains
    mean = jnp.mean(g * c, axis=0, keepdims=True)
    rows[:latent, :] = inv * (g - c * (inv * inv * mean))
    first, second = rope_acc[:half, :], rope_acc[half:, :]
    rows[latent : latent + half, :] = first * turns[:half, :] + second * turns[half:, :]
    rows[latent + half :, :] = second * turns[:half, :] - first * turns[half:, :]
    ordered = jnp.concatenate(
        [rows[pl.ds(pl.multiple_of(r * block, 8), block), :] for r in row_order(rows.shape[0] // block)], axis=0
    )
    out_a[...] = ordered[:, :share].astype(out_a.dtype)
    out_b[...] = ordered[:, share:].astype(out_b.dtype)


def partial_terms(which, out_dtype, doc_lengths, kg, vg, rg, kl, vl, latent, gain, share, rope, block):
    key_cols = kg.shape[1]
    width = latent.shape[1]
    kva = width + rope
    chunks = 8 if key_cols % 1024 == 0 and rg.shape[1] % 1024 == 0 else 1
    operands = [
        pltpu.with_memory_space_constraint(x, pltpu.HBM) for x in (doc_lengths, kg, vg, rg, kl, vl, latent, gain)
    ]
    return pl.pallas_call(
        functools.partial(partial_kernel, which=which, block=block, chunks=chunks),
        in_specs=[pl.BlockSpec(memory_space=pltpu.HBM)] * len(operands),
        out_specs=[pl.BlockSpec(memory_space=pltpu.VMEM)] * 2,
        scratch_shapes=[
            pltpu.VMEM((2 * share, key_cols), BF16),
            pltpu.VMEM((2 * share, key_cols), BF16),
            pltpu.VMEM((2 * share, rg.shape[1]), BF16),
            pltpu.VMEM((width, key_cols), BF16),
            pltpu.VMEM((width, key_cols), BF16),
            pltpu.VMEM((2 * share, width), BF16),
            pltpu.VMEM(gain.shape, F32),
            pltpu.SMEM(doc_lengths.shape, jnp.int32),
            pltpu.SemaphoreType.DMA((chunks + 1, 8)),
            pltpu.VMEM((width, 2 * share), F32),
            pltpu.VMEM((rope, 2 * share), F32),
            pltpu.VMEM((width, 2 * share), F32),
            pltpu.VMEM((rope, 2 * share), F32),
            pltpu.VMEM((kva, 2 * share), F32),
        ],
        out_shape=[pltpu.VMEM((kva, share), out_dtype)] * 2,
        compiler_params=pltpu.CompilerParams(vmem_limit_bytes=28 * MIB),
        cost_estimate=pl.CostEstimate(
            flops=2 * 2 * share * width * key_cols * 2,
            bytes_accessed=2 * (2 * width * key_cols + 2 * share * (2 * key_cols + rg.shape[1])),
            transcendentals=0,
        ),
        name="partial_terms",
    )(*operands)


def weight_kernel(*refs):
    own, sibling = refs[:4], refs[4:8]
    hidden, sibling_hidden, send, keep = refs[8:12]
    half, share = own[0].shape[0] // 2, own[0].shape[1]
    columns = hidden.shape[1]
    width = 256 if columns % 256 == 0 else columns
    left = jnp.concatenate([r[:half] for r in own] + [r[half:] for r in sibling], axis=1)
    me = lax.axis_index("head")
    places = [pl.ds(pl.multiple_of((me ^ r) * share, share), share) for r in range(4)]
    for n in range(columns // width):
        cols = slice(n * width, (n + 1) * width)
        right = [ref[place, cols] for ref in (hidden, sibling_hidden) for place in places]
        result = jnp.dot(left, jnp.concatenate(right, axis=0), preferred_element_type=F32)
        send[:, cols] = result[: half // 2].astype(send.dtype)
        keep[:, cols] = result[half // 2 :]


def weight_terms(own, sibling, hidden, sibling_hidden):
    kva, share = own[0].shape
    columns = hidden.shape[1]
    quarter = kva // 4
    vmem = pl.BlockSpec(memory_space=pltpu.VMEM)
    return pl.pallas_call(
        weight_kernel,
        in_specs=[vmem] * 10,
        out_specs=[vmem] * 2,
        out_shape=[
            jax.ShapeDtypeStruct((quarter, columns), BF16),
            jax.ShapeDtypeStruct((quarter, columns), F32),
        ],
        compiler_params=pltpu.CompilerParams(vmem_limit_bytes=32 * MIB),
        cost_estimate=pl.CostEstimate(
            flops=2 * (kva // 2) * 8 * share * columns, bytes_accessed=8 * MIB, transcendentals=0
        ),
        name="weight_terms",
    )(*own, *sibling, hidden, sibling_hidden)


def hidden_kernel(q0, q1, q2, q3, down_t, out, kva, natural, *, block):
    share = q0.shape[1]

    @pl.when(pl.program_id(0) == 0)
    def _():
        me = lax.axis_index("head")
        order = row_order(q0.shape[0] // block)
        for r, q in enumerate((q0, q1, q2, q3)):
            ordered = q[...].astype(F32)
            for i, place in enumerate(order):
                natural[pl.ds(pl.multiple_of(place * block, 8), block), :] = ordered[i * block : (i + 1) * block]
            kva[pl.ds(pl.multiple_of((me ^ r) * share, share), share), :] = natural[...].T.astype(BF16)

    out[...] = jnp.dot(kva[...], down_t[...], preferred_element_type=F32).astype(out.dtype)


def hidden_terms(gathered, down_t, block):
    kva, share = gathered[0].shape
    columns = down_t.shape[1]
    col_block = columns // 2 if columns % 256 == 0 else columns
    tokens = 4 * share
    whole = pl.BlockSpec((kva, share), lambda n: (0, 0))
    return pl.pallas_call(
        functools.partial(hidden_kernel, block=block),
        grid=(columns // col_block,),
        in_specs=[whole] * 4 + [pl.BlockSpec((kva, col_block), lambda n: (0, n))],
        out_specs=pl.BlockSpec((tokens, col_block), lambda n: (0, n)),
        scratch_shapes=[pltpu.VMEM((tokens, kva), BF16), pltpu.VMEM((kva, share), F32)],
        out_shape=jax.ShapeDtypeStruct((tokens, columns), BF16),
        compiler_params=pltpu.CompilerParams(vmem_limit_bytes=32 * MIB),
        cost_estimate=pl.CostEstimate(
            flops=2 * tokens * kva * columns, bytes_accessed=5 * MIB, transcendentals=0
        ),
        name="hidden_terms",
    )(*gathered, down_t)


def on_device(
    key_grad, value_grad, rope_grad, key_lift, value_lift, latent, norm_gain, doc_lengths, hidden, down_proj
):
    heads, groups = 4, 8
    core_bit, x_bit, y_bit = axis_bits()
    share = key_grad.shape[0] // heads
    kva = down_proj.shape[1]
    block = kva // groups

    def swap_head(array, bits):
        return lax.ppermute(array, "head", [(i, i ^ bits) for i in range(heads)])

    def swap_group(array, bits_of):
        return lax.ppermute(array, "group", [(i, i ^ bits_of(i)) for i in range(groups)])

    def first_bit(i):
        return y_bit if i & core_bit else x_bit

    def second_bit(i):
        return x_bit if i & core_bit else y_bit

    gain = norm_gain.reshape(1, -1)
    sibling_hidden = swap_group(hidden, lambda i: core_bit)

    def terms(which, dtype):
        return partial_terms(
            which, dtype, doc_lengths, key_grad, value_grad, rope_grad, key_lift, value_lift,
            latent, gain, share, kva - latent.shape[1], block,
        )

    p3, p1 = terms((3, 1), BF16)
    got3 = swap_head(p3, 1)
    got1 = swap_head(p1, 1)
    p2, p0 = terms((2, 0), F32)
    pair2 = (p2 + got3.astype(F32)).astype(BF16)
    got2 = swap_head(pair2, 2)
    q0 = (p0 + got1.astype(F32) + got2.astype(F32)).astype(BF16)
    q2 = swap_head(q0, 2)
    q1 = swap_head(q0, 1)
    q3 = swap_head(q2, 1)
    gathered = (q0, q1, q2, q3)
    sibling = tuple(swap_group(q, lambda i: core_bit) for q in gathered)

    send, keep = weight_terms(gathered, sibling, hidden, sibling_hidden)
    got = swap_group(send, first_bit)
    hidden_grad = hidden_terms(gathered, down_proj.T, block)
    summed = keep + got.astype(F32)
    last = swap_group(summed[:block].astype(BF16), second_bit)
    weight_grad = summed[block:] + last.astype(F32)
    return (hidden_grad, weight_grad)


def solution(mesh):
    shape = dict(mesh.shape)
    paired = shape["head"] == 4 and shape["group"] == 8
    return jax.shard_map(
        on_device if paired else on_device_any,
        mesh=mesh,
        in_specs=(
            P("group", "head"),
            P("group", "head"),
            P("group", "head"),
            P(None, "head"),
            P(None, "head"),
            P("group", None),
            P(),
            P("group", None),
            P("group", "head"),
            P("head", None),
        ),
        out_specs=(P("group", "head"), P("group", "head")),
        check_vma=False,
    )
```

time: 76.5 us -> 62.8 us (0.82)
  local copies, waits for them, and re-layouts: 13.6 us -> 0.04 us
    unnamed x22 -> x4, local copies, waits for them, and re-layouts: 13.4 us -> 0.01 us
    pallas_call x2, Pallas kernels: 6.6 us -> 4.63 us  [the longest x1 3.36 us: hidden_terms(): pl.pallas_call(functools.partial(hidden_kernel, block=block), grid=(colum...]
    pallas_call x2, Pallas kernels: 13.3 us -> 14.8 us  [partial_terms(): pl.pallas_call(functools.partial(partial_kernel, which=which, block=block...]
  transfers between devices with their start and end apart: 13 -> 13, of which waited for: 6 -> 6; matrix products, arithmetic and copies ran while one was open for 0% -> 0% of each run, Pallas kernels for 23% -> 29%
where the time goes in v2:
time: 62.8 us; the launch traced here: 62.6 us
  waiting for transfers between devices  27.5 us (44%)
  Pallas kernels  19.4 us (31%)
  starting transfers between devices  14 us (22%)
  other arithmetic  1.02 us (2%)
  between operations  0.72 us (1%)
    ppermute x6, waiting for transfers between devices, swap_head(): return lax.ppermute(array, 'head', [(i, i ^ bits) for i in range(heads)])  17 us
    pallas_call x2, Pallas kernels, partial_terms(): pl.pallas_call(functools.partial(partial_kernel, which=which, block=block...  14.8 us
    ppermute x7, waiting for transfers between devices, swap_group(): lax.ppermute(array, 'group', [(i, i ^ bits_of(i)) for i in range(groups)])  10.5 us
    ppermute x6, starting transfers between devices, swap_head(): return lax.ppermute(array, 'head', [(i, i ^ bits) for i in range(heads)])  9.92 us
    ppermute x7, starting transfers between devices, swap_group(): lax.ppermute(array, 'group', [(i, i ^ bits_of(i)) for i in range(groups)])  4.03 us
    pallas_call x1, Pallas kernels, hidden_terms(): pl.pallas_call(functools.partial(hidden_kernel, block=block), grid=(colum...  3.36 us
    pallas_call x1, Pallas kernels, weight_terms(): pl.pallas_call(weight_kernel, in_specs=[vmem] * 10, out_specs=[vmem] * 2,...  1.27 us
  transfers between devices with their start and end apart: 13, of which 6 were waited for; matrix products, arithmetic and copies ran while one was open for 0% of the time, Pallas kernels for 29%

profile of v2, /device:TPU:0, one launch (start us, length us, event | category | flops | bytes accessed | tf_op | source)
XLA Modules:
  0.0 62.6 jit_solution(3267165593014082857)
XLA Ops:
  0.6 0.5 collective-permute-start.10
  1.1 7.3 %partial_terms.3 = (bf16[576,128]{1,0:T(8,128)(2,1)S(1)}, bf16[576,128]{1,0:T(8,128)(2,1)S(1)}) custom-call(s32[1,4]{1,0:T(1,128)} %lengths.3, bf16[512,4096]{1,0:T(8,128)(2,1)} %kg.3, bf16[512,4096]{1,0:T(8,128)(2,1)} %vg.3, bf16[512,2048]{1,0:T(8,128)(2,1)} %rg.3, bf16[512,4096]{1,0:T(8,128)(2,1)} %kl.3, bf16[512,4096]{1,0:T(8,128)(2,1)} %vl.3, ...), custom_call_target="tpu_custom_call" | custom-call | flops 2147483648 | bytes 13631488 | tf_op jit(solution)/shard_map/partial_terms/pallas_call | solution.py:184
  8.5 2.7 %collective-permute-start.1 = (bf16[576,128]{1,0:T(8,128)(2,1)S(1)}, bf16[576,128]{1,0:T(8,128)(2,1)S(1)}, u32[]{:S(2)}, u32[]{:S(2)}) collective-permute-start(bf16[576,128]{1,0:T(8,128)(2,1)S(1)} %get-tuple-element.11), channel_id=1, source_target_pairs={{0,1},{1,0},{2,3},{3,2},{4,5},{5,4},{6,7},{7,6},{8,9},{9,8},{10,11... | collective-permute-start | bytes 442376 | tf_op jit(solution)/shard_map/ppermute | solution.py:300
  11.1 0.1 collective-permute-start
  11.2 7.4 %partial_terms.2 = (f32[576,128]{1,0:T(8,128)S(1)}, f32[576,128]{1,0:T(8,128)S(1)}) custom-call(s32[1,4]{1,0:T(1,128)} %lengths.3, bf16[512,4096]{1,0:T(8,128)(2,1)} %kg.3, bf16[512,4096]{1,0:T(8,128)(2,1)} %vg.3, bf16[512,2048]{1,0:T(8,128)(2,1)} %rg.3, bf16[512,4096]{1,0:T(8,128)(2,1)} %kl.3, bf16[512,4096]{1,0:T(8,128)(2,1)} %vl.3, bf16[512,512]{1,0:T(8,128)(2,1)} %lat.3, ...), custom_call_target="tpu_custom_call" | custom-call | flops 2147483648 | bytes 13631488 | tf_op jit(solution)/shard_map/partial_terms/pallas_call | solution.py:184
  18.7 0.0 collective-permute-done.1
  18.7 3.0 %collective-permute-start.2 = (bf16[576,128]{1,0:T(8,128)(2,1)S(1)}, bf16[576,128]{1,0:T(8,128)(2,1)S(1)}, u32[]{:S(2)}, u32[]{:S(2)}) collective-permute-start(bf16[576,128]{1,0:T(8,128)(2,1)S(1)} %add_convert_fusion.1), channel_id=1, source_target_pairs={{0,2},{1,3},{2,0},{3,1},{4,6},{5,7},{6,4},{7,5},{8,10},{9,11},{10,... | collective-permute-start | bytes 442376 | tf_op jit(solution)/shard_map/ppermute | solution.py:300
  21.7 0.0 collective-permute-done
  21.7 7.1 %collective-permute-done.2 = bf16[576,128]{1,0:T(8,128)(2,1)S(1)} collective-permute-done((bf16[576,128]{1,0:T(8,128)(2,1)S(1)}, bf16[576,128]{1,0:T(8,128)(2,1)S(1)}, u32[]{:S(2)}, u32[]{:S(2)}) %collective-permute-start.2) | collective-permute-done | bytes 147488 | tf_op jit(solution)/shard_map/ppermute | solution.py:300
  28.8 0.1 add_convert_fusion.q0.refs_0_
  28.9 0.1 collective-permute-start.4
  29.0 4.1 %collective-permute-start.3 = (bf16[576,128]{1,0:T(8,128)(2,1)S(1)}, bf16[576,128]{1,0:T(8,128)(2,1)S(1)}, u32[]{:S(2)}, u32[]{:S(2)}) collective-permute-start(bf16[576,128]{1,0:T(8,128)(2,1)S(1)} %add_convert_fusion.q0.refs_0_), channel_id=1, source_target_pairs={{0,1},{1,0},{2,3},{3,2},{4,5},{5,4},{6,7},{7,6},{8,9},{9,8},{10,11... | collective-permute-start | bytes 442376 | tf_op jit(solution)/shard_map/ppermute | solution.py:300
  33.1 5.2 %collective-permute-done.4.q2.refs_2_ = bf16[576,128]{1,0:T(8,128)(2,1)S(1)} collective-permute-done((bf16[576,128]{1,0:T(8,128)(2,1)S(1)}, bf16[576,128]{1,0:T(8,128)(2,1)S(1)}, u32[]{:S(2)}, u32[]{:S(2)}) %collective-permute-start.4) | collective-permute-done | bytes 147488 | tf_op jit(solution)/shard_map/ppermute | solution.py:300
  38.3 0.0 collective-permute-start.5
  38.3 0.0 collective-permute-start.6
  38.3 0.5 collective-permute-start.8
  38.8 0.0 collective-permute-start.7
  38.8 4.6 %collective-permute-done.5.q3.refs_3_ = bf16[576,128]{1,0:T(8,128)(2,1)S(1)} collective-permute-done((bf16[576,128]{1,0:T(8,128)(2,1)S(1)}, bf16[576,128]{1,0:T(8,128)(2,1)S(1)}, u32[]{:S(2)}, u32[]{:S(2)}) %collective-permute-start.5) | collective-permute-done | bytes 147488 | tf_op jit(solution)/shard_map/ppermute | solution.py:300
  43.4 0.0 collective-permute-start.9
  43.4 0.0 collective-permute-done.6.refs_4_
  43.4 0.0 collective-permute-done.8.refs_6_
  43.5 1.3 %collective-permute-done.9.refs_7_ = bf16[576,128]{1,0:T(8,128)(2,1)S(1)} collective-permute-done((bf16[576,128]{1,0:T(8,128)(2,1)S(1)}, bf16[576,128]{1,0:T(8,128)(2,1)S(1)}, u32[]{:S(2)}, u32[]{:S(2)}) %collective-permute-start.9) | collective-permute-done | bytes 147488 | tf_op jit(solution)/shard_map/ppermute | solution.py:303
  44.8 0.0 collective-permute-done.10.refs_9_
  44.8 1.3 %weight_terms.1 = (bf16[144,1792]{1,0:T(8,128)(2,1)S(1)}, f32[144,1792]{1,0:T(8,128)S(1)}) custom-call(bf16[576,128]{1,0:T(8,128)(2,1)S(1)} %add_convert_fusion.q0.refs_0_, bf16[576,128]{1,0:T(8,128)(2,1)S(1)} %collective-permute-done.3.q1.refs_1_, bf16[576,128]{1,0:T(8,128)(2,1)S(1)} %collective-permute-done.4.q2.refs_2_, ...), custom_call_target="tpu_custom_call" | custom-call | flops 1056964608 | bytes 8388608 | tf_op jit(solution)/shard_map/weight_terms/pallas_call | solution.py:237
  46.1 0.0 copy-start
  46.1 1.5 %collective-permute-start.11 = (bf16[144,1792]{1,0:T(8,128)(2,1)S(1)}, bf16[144,1792]{1,0:T(8,128)(2,1)S(1)}, u32[]{:S(2)}, u32[]{:S(2)}) collective-permute-start(bf16[144,1792]{1,0:T(8,128)(2,1)S(1)} %get-tuple-element.13), channel_id=1, source_target_pairs={{0,8},{4,20},{8,0},{12,28},{16,24},{20,4},{24,16},{28,12},{1,9},{5... | collective-permute-start | bytes 1548296 | tf_op jit(solution)/shard_map/ppermute | solution.py:303
  47.6 7.7 %collective-permute-done.11 = bf16[144,1792]{1,0:T(8,128)(2,1)S(1)} collective-permute-done((bf16[144,1792]{1,0:T(8,128)(2,1)S(1)}, bf16[144,1792]{1,0:T(8,128)(2,1)S(1)}, u32[]{:S(2)}, u32[]{:S(2)}) %collective-permute-start.11) | collective-permute-done | bytes 516128 | tf_op jit(solution)/shard_map/ppermute | solution.py:303
  55.3 0.1 convert_add_fusion
  55.4 1.5 %collective-permute-start.12 = (bf16[72,1792]{1,0:T(8,128)(2,1)S(1)}, bf16[72,1792]{1,0:T(8,128)(2,1)S(1)}, u32[]{:S(2)}, u32[]{:S(2)}) collective-permute-start(bf16[72,1792]{1,0:T(8,128)(2,1)S(1)} %slice.13), channel_id=1, source_target_pairs={{0,16},{4,12},{8,24},{12,4},{16,0},{20,28},{24,8},{28,20},{1,17},{... | collective-permute-start | bytes 774152 | tf_op jit(solution)/shard_map/ppermute | solution.py:303
  56.9 3.4 %hidden_terms.1 = bf16[512,1792]{1,0:T(8,128)(2,1)} custom-call(bf16[576,128]{1,0:T(8,128)(2,1)S(1)} %add_convert_fusion.q0.refs_0_, bf16[576,128]{1,0:T(8,128)(2,1)S(1)} %collective-permute-done.3.q1.refs_1_, bf16[576,128]{1,0:T(8,128)(2,1)S(1)} %collective-permute-done.4.q2.refs_2_, bf16[576,128]{1,0:T(8,128)(2,1)S(1)} %collective-permute-done.5.q3.refs_3_, ...), custom_call_target="tpu_custom_call" | custom-call | flops 1056964608 | bytes 5242880 | tf_op jit(solution)/shard_map/hidden_terms/pallas_call | solution.py:275
  60.3 1.5 %collective-permute-done.12 = bf16[72,1792]{1,0:T(8,128)(2,1)S(1)} collective-permute-done((bf16[72,1792]{1,0:T(8,128)(2,1)S(1)}, bf16[72,1792]{1,0:T(8,128)(2,1)S(1)}, u32[]{:S(2)}, u32[]{:S(2)}) %collective-permute-start.12) | collective-permute-done | bytes 258080 | tf_op jit(solution)/shard_map/ppermute | solution.py:303
  61.8 0.8 %slice_add_fusion = f32[72,1792]{1,0:T(8,128)} fusion(f32[144,1792]{1,0:T(8,128)S(1)} %convert_add_fusion, bf16[72,1792]{1,0:T(8,128)(2,1)S(1)} %collective-permute-done.12), kind=kLoop, calls=%fused_computation.2 | loop fusion | flops 258048 | bytes 1290240 | tf_op jit(solution)/shard_map/add | solution.py:338
  (7 shorter events, 0.1 us)
Async XLA Ops:
  0.6 44.2 %collective-permute-start.10 = (bf16[512,1792]{1,0:T(8,128)(2,1)}, bf16[512,1792]{1,0:T(8,128)(2,1)S(1)}, u32[]{:S(2)}, u32[]{:S(2)}) collective-permute-start(bf16[512,1792]{1,0:T(8,128)(2,1)} %refs_8_.1), channel_id=1, source_target_pairs={{0,4},{4,0},{8,12},{12,8},{16,20},{20,16},{24,28},{28,24},{1,5},{5... | collective-permute-start | bytes 5505032 | tf_op jit(solution)/shard_map/ppermute | solution.py:303
  8.5 10.2 %collective-permute-start.1 = (bf16[576,128]{1,0:T(8,128)(2,1)S(1)}, bf16[576,128]{1,0:T(8,128)(2,1)S(1)}, u32[]{:S(2)}, u32[]{:S(2)}) collective-permute-start(bf16[576,128]{1,0:T(8,128)(2,1)S(1)} %get-tuple-element.11), channel_id=1, source_target_pairs={{0,1},{1,0},{2,3},{3,2},{4,5},{5,4},{6,7},{7,6},{8,9},{9,8},{10,11... | collective-permute-start | bytes 442376 | tf_op jit(solution)/shard_map/ppermute | solution.py:300
  11.1 10.6 %collective-permute-start = (bf16[576,128]{1,0:T(8,128)(2,1)S(1)}, bf16[576,128]{1,0:T(8,128)(2,1)S(1)}, u32[]{:S(2)}, u32[]{:S(2)}) collective-permute-start(bf16[576,128]{1,0:T(8,128)(2,1)S(1)} %get-tuple-element.9), channel_id=1, source_target_pairs={{0,1},{1,0},{2,3},{3,2},{4,5},{5,4},{6,7},{7,6},{8,9},{9,8},{10,11... | collective-permute-start | bytes 442376 | tf_op jit(solution)/shard_map/ppermute | solution.py:300
  11.2 33.6 %copy-start.1 = (bf16[512,1792]{1,0:T(8,128)(2,1)S(1)}, bf16[512,1792]{1,0:T(8,128)(2,1)}, u32[]{:S(2)}) copy-start(bf16[512,1792]{1,0:T(8,128)(2,1)} %refs_8_.1) | copy-start | bytes 5505028
  18.7 10.1 %collective-permute-start.2 = (bf16[576,128]{1,0:T(8,128)(2,1)S(1)}, bf16[576,128]{1,0:T(8,128)(2,1)S(1)}, u32[]{:S(2)}, u32[]{:S(2)}) collective-permute-start(bf16[576,128]{1,0:T(8,128)(2,1)S(1)} %add_convert_fusion.1), channel_id=1, source_target_pairs={{0,2},{1,3},{2,0},{3,1},{4,6},{5,7},{6,4},{7,5},{8,10},{9,11},{10,... | collective-permute-start | bytes 442376 | tf_op jit(solution)/shard_map/ppermute | solution.py:300
  28.9 9.4 %collective-permute-start.4 = (bf16[576,128]{1,0:T(8,128)(2,1)S(1)}, bf16[576,128]{1,0:T(8,128)(2,1)S(1)}, u32[]{:S(2)}, u32[]{:S(2)}) collective-permute-start(bf16[576,128]{1,0:T(8,128)(2,1)S(1)} %add_convert_fusion.q0.refs_0_), channel_id=1, source_target_pairs={{0,2},{1,3},{2,0},{3,1},{4,6},{5,7},{6,4},{7,5},{8,10},{9,11},{10,... | collective-permute-start | bytes 442376 | tf_op jit(solution)/shard_map/ppermute | solution.py:300
  29.0 9.8 %collective-permute-start.3 = (bf16[576,128]{1,0:T(8,128)(2,1)S(1)}, bf16[576,128]{1,0:T(8,128)(2,1)S(1)}, u32[]{:S(2)}, u32[]{:S(2)}) collective-permute-start(bf16[576,128]{1,0:T(8,128)(2,1)S(1)} %add_convert_fusion.q0.refs_0_), channel_id=1, source_target_pairs={{0,1},{1,0},{2,3},{3,2},{4,5},{5,4},{6,7},{7,6},{8,9},{9,8},{10,11... | collective-permute-start | bytes 442376 | tf_op jit(solution)/shard_map/ppermute | solution.py:300
  38.3 5.1 %collective-permute-start.5 = (bf16[576,128]{1,0:T(8,128)(2,1)S(1)}, bf16[576,128]{1,0:T(8,128)(2,1)S(1)}, u32[]{:S(2)}, u32[]{:S(2)}) collective-permute-start(bf16[576,128]{1,0:T(8,128)(2,1)S(1)} %collective-permute-done.4.q2.refs_2_), channel_id=1, source_target_pairs={{0,1},{1,0},{2,3},{3,2},{4,5},{5,4},{6,7},{7,6},{8,9},{9,8},{10,11... | collective-permute-start | bytes 442376 | tf_op jit(solution)/shard_map/ppermute | solution.py:300
  38.3 5.1 %collective-permute-start.6 = (bf16[576,128]{1,0:T(8,128)(2,1)S(1)}, bf16[576,128]{1,0:T(8,128)(2,1)S(1)}, u32[]{:S(2)}, u32[]{:S(2)}) collective-permute-start(bf16[576,128]{1,0:T(8,128)(2,1)S(1)} %add_convert_fusion.q0.refs_0_), channel_id=1, source_target_pairs={{0,4},{4,0},{8,12},{12,8},{16,20},{20,16},{24,28},{28,24},{1,5},{5... | collective-permute-start | bytes 442376 | tf_op jit(solution)/shard_map/ppermute | solution.py:303
  38.3 5.1 %collective-permute-start.8 = (bf16[576,128]{1,0:T(8,128)(2,1)S(1)}, bf16[576,128]{1,0:T(8,128)(2,1)S(1)}, u32[]{:S(2)}, u32[]{:S(2)}) collective-permute-start(bf16[576,128]{1,0:T(8,128)(2,1)S(1)} %collective-permute-done.4.q2.refs_2_), channel_id=1, source_target_pairs={{0,4},{4,0},{8,12},{12,8},{16,20},{20,16},{24,28},{28,24},{1,5},{5... | collective-permute-start | bytes 442376 | tf_op jit(solution)/shard_map/ppermute | solution.py:303
  38.8 4.6 %collective-permute-start.7 = (bf16[576,128]{1,0:T(8,128)(2,1)S(1)}, bf16[576,128]{1,0:T(8,128)(2,1)S(1)}, u32[]{:S(2)}, u32[]{:S(2)}) collective-permute-start(bf16[576,128]{1,0:T(8,128)(2,1)S(1)} %collective-permute-done.3.q1.refs_1_), channel_id=1, source_target_pairs={{0,4},{4,0},{8,12},{12,8},{16,20},{20,16},{24,28},{28,24},{1,5},{5... | collective-permute-start | bytes 442376 | tf_op jit(solution)/shard_map/ppermute | solution.py:303
  43.4 1.4 %collective-permute-start.9 = (bf16[576,128]{1,0:T(8,128)(2,1)S(1)}, bf16[576,128]{1,0:T(8,128)(2,1)S(1)}, u32[]{:S(2)}, u32[]{:S(2)}) collective-permute-start(bf16[576,128]{1,0:T(8,128)(2,1)S(1)} %collective-permute-done.5.q3.refs_3_), channel_id=1, source_target_pairs={{0,4},{4,0},{8,12},{12,8},{16,20},{20,16},{24,28},{28,24},{1,5},{5... | collective-permute-start | bytes 442376 | tf_op jit(solution)/shard_map/ppermute | solution.py:303
  46.1 10.8 %copy-start = (bf16[1792,576]{0,1:T(8,128)(2,1)S(1)}, bf16[1792,576]{0,1:T(8,128)(2,1)}, u32[]{:S(2)}) copy-start(bf16[1792,576]{0,1:T(8,128)(2,1)} %param.19) | copy-start | bytes 6193156
  46.1 9.2 %collective-permute-start.11 = (bf16[144,1792]{1,0:T(8,128)(2,1)S(1)}, bf16[144,1792]{1,0:T(8,128)(2,1)S(1)}, u32[]{:S(2)}, u32[]{:S(2)}) collective-permute-start(bf16[144,1792]{1,0:T(8,128)(2,1)S(1)} %get-tuple-element.13), channel_id=1, source_target_pairs={{0,8},{4,20},{8,0},{12,28},{16,24},{20,4},{24,16},{28,12},{1,9},{5... | collective-permute-start | bytes 1548296 | tf_op jit(solution)/shard_map/ppermute | solution.py:303
  55.4 6.4 %collective-permute-start.12 = (bf16[72,1792]{1,0:T(8,128)(2,1)S(1)}, bf16[72,1792]{1,0:T(8,128)(2,1)S(1)}, u32[]{:S(2)}, u32[]{:S(2)}) collective-permute-start(bf16[72,1792]{1,0:T(8,128)(2,1)S(1)} %slice.13), channel_id=1, source_target_pairs={{0,16},{4,12},{8,24},{12,4},{16,0},{20,28},{24,8},{28,20},{1,17},{... | collective-permute-start | bytes 774152 | tf_op jit(solution)/shard_map/ppermute | solution.py:303

commit v3 on v2

v3 whole, which is shorter than its diff:
```python
import functools
import math

import jax
import jax.numpy as jnp
from jax import lax
from jax.experimental import pallas as pl
from jax.experimental.pallas import tpu as pltpu
from jax.sharding import PartitionSpec as P

F32 = jnp.float32
BF16 = jnp.bfloat16
LAST = (((1,), (1,)), ((), ()))
FIRST = (((0,), (0,)), ((), ()))
MIB = 1 << 20


def positions(lengths, token_index):
    doc_ends = jnp.cumsum(lengths, axis=1)
    doc_start = jnp.max(jnp.where(doc_ends <= token_index[:, None], doc_ends, 0), axis=1)
    return token_index - doc_start


def kva_rows_grad(stacked, latent, norm_gain, position):
    width = latent.shape[1]
    latent_part = stacked[:, :width]
    rotary_part = stacked[:, width:]
    values = latent.astype(F32)
    inverse_rms = lax.rsqrt(jnp.mean(values * values, axis=1, keepdims=True) + 1e-06)
    scaled_grad = latent_part * norm_gain[None, :]
    norm_grad = inverse_rms * (
        scaled_grad
        - values * inverse_rms * inverse_rms * jnp.mean(scaled_grad * values, axis=1, keepdims=True)
    )
    half_width = rotary_part.shape[1] // 2
    inv_freq = 10000.0 ** (-(2.0 * jnp.arange(half_width, dtype=F32)) / (2.0 * half_width))
    angles = position.astype(F32)[:, None] * inv_freq[None, :]
    cosine = jnp.cos(angles)
    sine = jnp.sin(angles)
    first_half = rotary_part[:, :half_width]
    second_half = rotary_part[:, half_width:]
    rot_first = first_half * cosine + second_half * sine
    rot_second = second_half * cosine - first_half * sine
    return jnp.concatenate([norm_grad, rot_first, rot_second], axis=1).astype(BF16)


def on_device_any(
    key_grad, value_grad, rope_grad, key_lift, value_lift, latent, norm_gain, doc_lengths, hidden, down_proj
):
    seq_len = key_grad.shape[0]
    rope = down_proj.shape[1] - latent.shape[1]
    head_terms = lax.dot_general(key_grad, key_lift, LAST, preferred_element_type=F32)
    head_terms = head_terms + lax.dot_general(value_grad, value_lift, LAST, preferred_element_type=F32)
    heads_here = rope_grad.shape[1] // rope
    rope_terms = jnp.sum(rope_grad.reshape(seq_len, heads_here, rope), axis=1, dtype=F32)
    stacked = jnp.concatenate([head_terms, rope_terms], axis=1)
    shared = lax.psum_scatter(stacked, "head", scatter_dimension=0, tiled=True)
    share_rows = shared.shape[0]
    first_row = lax.axis_index("head") * share_rows
    own_latent = lax.dynamic_slice_in_dim(latent, first_row, share_rows, 0)
    token_index = first_row + jnp.arange(share_rows, dtype=jnp.int32)
    row_lengths = jnp.broadcast_to(doc_lengths, (share_rows, doc_lengths.shape[1]))
    own_grad = kva_rows_grad(shared, own_latent, norm_gain, positions(row_lengths, token_index))
    kva_grad = lax.all_gather(own_grad, "head", axis=0, tiled=True)
    hidden_grad = lax.dot_general(kva_grad, down_proj, LAST, preferred_element_type=F32).astype(BF16)
    weight_grad = lax.psum_scatter(
        lax.dot_general(kva_grad, hidden, FIRST, preferred_element_type=F32),
        "group",
        scatter_dimension=0,
        tiled=True,
    )
    return (hidden_grad, weight_grad)


def axis_bits():
    return 1, 2, 4


def row_order(blocks):
    core, x, y = axis_bits()
    mine = lax.axis_index("group")
    first = jnp.where(mine & core == 0, x, y)
    other, second, both = mine ^ core, first ^ (x | y), x | y
    order = [mine ^ both, mine ^ first, other ^ both, other ^ second]
    order += [mine ^ second, mine, other ^ first, other]
    assert len(order) == blocks
    return order


def partial_kernel(*refs, which, dtypes, rope, block, chunks, lifts_here):
    count = len(which)
    lengths, kg, vg, rg, kl, vl, lat, gain = refs[:8]
    outs, refs = refs[8 : 8 + count], refs[8 + count :]
    if lifts_here:
        kl_v, vl_v = kl, vl
    else:
        (kl_v, vl_v), refs = refs[:2], refs[2:]
    kg_v, vg_v, rg_v, lat_v, gain_v, lengths_s, sems, acc, rope_acc, values, turns, rows = refs
    share = outs[0].shape[1]
    latent = lat.shape[1]
    half = rope // 2
    shares = [lax.axis_index("head") ^ r for r in which]
    places = [pl.ds(pl.multiple_of(r * share, share), share) for r in shares]
    sides = [slice(side * share, (side + 1) * share) for side in range(count)]

    def columns(ref, chunk):
        width = ref.shape[1] // chunks
        return slice(chunk * width, (chunk + 1) * width)

    def copies_of(chunk):
        pairs = []
        if not lifts_here:
            for src, dst in ((kl, kl_v), (vl, vl_v)):
                pairs.append((src.at[:, columns(src, chunk)], dst.at[:, columns(src, chunk)]))
        for src, dst in ((kg, kg_v), (vg, vg_v), (rg, rg_v)):
            for place, side in zip(places, sides):
                pairs.append((src.at[place, columns(src, chunk)], dst.at[side, columns(src, chunk)]))
        return [pltpu.make_async_copy(src, dst, sems.at[chunk, i]) for i, (src, dst) in enumerate(pairs)]

    small = [(lat.at[place, :], lat_v.at[side, :]) for place, side in zip(places, sides)]
    small += [(gain, gain_v), (lengths, lengths_s)]
    small_copies = [pltpu.make_async_copy(src, dst, sems.at[chunks, i]) for i, (src, dst) in enumerate(small)]
    all_copies = [copies_of(chunk) for chunk in range(chunks)]
    for copy in all_copies[0] + small_copies + [copy for copies in all_copies[1:] for copy in copies]:
        copy.start()

    fold_shape = (rope, rg.shape[1] // chunks)
    fold = lax.rem(lax.broadcasted_iota(jnp.int32, fold_shape, 1), rope) == lax.broadcasted_iota(
        jnp.int32, fold_shape, 0
    )
    fold = fold.astype(BF16)

    for chunk in range(chunks):
        for copy in all_copies[chunk]:
            copy.wait()
        here = columns(kg, chunk)
        term = lax.dot_general(kg_v[:, here], kl_v[:, here], LAST, preferred_element_type=F32)
        term += lax.dot_general(vg_v[:, here], vl_v[:, here], LAST, preferred_element_type=F32)
        rope_term = lax.dot_general(fold, rg_v[:, columns(rg, chunk)], LAST, preferred_element_type=F32)
        acc[...] = term if chunk == 0 else acc[...] + term
        rope_acc[...] = rope_term if chunk == 0 else rope_acc[...] + rope_term
        if chunk == 0:
            for copy in small_copies:
                copy.wait()
            values[...] = lat_v[...].astype(F32).T
            lane = lax.broadcasted_iota(jnp.int32, (1, share), 1)
            pair = lax.broadcasted_iota(jnp.int32, (half, share), 0).astype(F32)
            freq = jnp.exp(pair * (-math.log(10000.0) / half))
            for r, side in zip(shares, sides):
                token = r * share + lane
                start = jnp.zeros_like(token)
                end = jnp.int32(0)
                for doc in range(lengths.shape[1]):
                    end = end + lengths_s[0, doc]
                    start = jnp.maximum(start, jnp.where(end <= token, end, 0))
                angle = (token - start).astype(F32) * freq
                turns[:half, side] = jnp.cos(angle)
                turns[half:, side] = jnp.sin(angle)

    gains = jnp.broadcast_to(gain_v[...], (share, latent)).T
    gains = jnp.concatenate([gains] * count, axis=1)
    c = values[...]
    inv = lax.rsqrt(jnp.mean(c * c, axis=0, keepdims=True) + 1e-06)
    g = acc[...].T * gains
    mean = jnp.mean(g * c, axis=0, keepdims=True)
    rows[:latent, :] = inv * (g - c * (inv * inv * mean))
    first, second = rope_acc[:half, :], rope_acc[half:, :]
    rows[latent : latent + half, :] = first * turns[:half, :] + second * turns[half:, :]
    rows[latent + half :, :] = second * turns[:half, :] - first * turns[half:, :]
    ordered = jnp.concatenate(
        [rows[pl.ds(pl.multiple_of(r * block, 8), block), :] for r in row_order(rows.shape[0] // block)], axis=0
    )
    for out, dtype, side in zip(outs, dtypes, sides):
        out[...] = ordered[:, side].astype(dtype)


def partial_terms(which, dtypes, doc_lengths, kg, vg, rg, kl, vl, latent, gain, share, rope, block, lifts_here):
    key_cols = kg.shape[1]
    width = latent.shape[1]
    kva = width + rope
    tokens = len(which) * share
    chunks = 4 if lifts_here else 8
    if key_cols % (chunks * 128) or rg.shape[1] % (chunks * 128):
        chunks = 1
    operands = (doc_lengths, kg, vg, rg, kl, vl, latent, gain)
    spaces = [pltpu.VMEM if lifts_here and i in (4, 5) else pltpu.HBM for i in range(len(operands))]
    out_shape = [pltpu.VMEM((kva, share), dtype) for dtype in dtypes]
    if not lifts_here:
        out_shape += [pltpu.VMEM(kl.shape, BF16), pltpu.VMEM(vl.shape, BF16)]
    return pl.pallas_call(
        functools.partial(
            partial_kernel, which=which, dtypes=dtypes, rope=rope, block=block, chunks=chunks, lifts_here=lifts_here
        ),
        in_specs=[pl.BlockSpec(memory_space=space) for space in spaces],
        out_specs=[pl.BlockSpec(memory_space=pltpu.VMEM)] * len(out_shape),
        scratch_shapes=[
            pltpu.VMEM((tokens, key_cols), BF16),
            pltpu.VMEM((tokens, key_cols), BF16),
            pltpu.VMEM((tokens, rg.shape[1]), BF16),
            pltpu.VMEM((tokens, width), BF16),
            pltpu.VMEM(gain.shape, F32),
            pltpu.SMEM(doc_lengths.shape, jnp.int32),
            pltpu.SemaphoreType.DMA((chunks + 1, 2 + 3 * len(which))),
            pltpu.VMEM((tokens, width), F32),
            pltpu.VMEM((rope, tokens), F32),
            pltpu.VMEM((width, tokens), F32),
            pltpu.VMEM((rope, tokens), F32),
            pltpu.VMEM((kva, tokens), F32),
        ],
        out_shape=out_shape,
        compiler_params=pltpu.CompilerParams(vmem_limit_bytes=28 * MIB),
        cost_estimate=pl.CostEstimate(
            flops=2 * tokens * width * key_cols * 2,
            bytes_accessed=2 * (2 * width * key_cols + tokens * (2 * key_cols + rg.shape[1])),
            transcendentals=0,
        ),
        name="partial_terms",
    )(*[pltpu.with_memory_space_constraint(x, space) for x, space in zip(operands, spaces)])


def weight_kernel(*refs, part, parts):
    own, sibling = refs[:4], refs[4:8]
    hidden, sibling_hidden = refs[8:10]
    outs = refs[10:]
    share = own[0].shape[1]
    block = outs[0].shape[0]
    count = len(outs) * block

    def rows_of(ref, side):
        skip = 2 * part * count if ref.shape[0] == 2 * parts * count else 0
        return ref[skip + side * count : skip + (side + 1) * count]

    left = jnp.concatenate([rows_of(r, 0) for r in own] + [rows_of(r, 1) for r in sibling], axis=1)
    columns = hidden.shape[1]
    width = 256 if columns % 256 == 0 else columns
    me = lax.axis_index("head")
    places = [pl.ds(pl.multiple_of((me ^ r) * share, share), share) for r in range(4)]
    for n in range(columns // width):
        cols = slice(n * width, (n + 1) * width)
        right = [ref[place, cols] for ref in (hidden, sibling_hidden) for place in places]
        result = jnp.dot(left, jnp.concatenate(right, axis=0), preferred_element_type=F32)
        for i, out in enumerate(outs):
            out[:, cols] = result[i * block : (i + 1) * block].astype(out.dtype)


def weight_terms(own, sibling, hidden, sibling_hidden, block, part, parts, dtypes):
    columns = hidden.shape[1]
    vmem = pl.BlockSpec(memory_space=pltpu.VMEM)
    operands = (*own, *sibling, hidden, sibling_hidden)
    return pl.pallas_call(
        functools.partial(weight_kernel, part=part, parts=parts),
        in_specs=[vmem] * len(operands),
        out_specs=[vmem] * len(dtypes),
        out_shape=[pltpu.VMEM((block, columns), dtype) for dtype in dtypes],
        compiler_params=pltpu.CompilerParams(vmem_limit_bytes=24 * MIB),
        cost_estimate=pl.CostEstimate(flops=1000, bytes_accessed=1000, transcendentals=0),
        name="weight_terms",
    )(*[pltpu.with_memory_space_constraint(x, pltpu.VMEM) for x in operands])


def natural_kernel(*refs, block):
    shares, out, natural = refs[:-2], refs[-2], refs[-1]
    me = lax.axis_index("head")
    order = row_order(natural.shape[0] // block)
    share = shares[0].shape[1]
    for r, q in enumerate(shares):
        ordered = q[...].astype(F32)
        for i, place in enumerate(order):
            natural[pl.ds(pl.multiple_of(place * block, 8), block), :] = ordered[i * block : (i + 1) * block]
        out[pl.ds(pl.multiple_of((me ^ r) * share, share), share), :] = natural[...].T.astype(BF16)


def natural_rows(gathered, block):
    kva, share = gathered[0].shape
    return pl.pallas_call(
        functools.partial(natural_kernel, block=block),
        in_specs=[pl.BlockSpec(memory_space=pltpu.VMEM)] * len(gathered),
        out_specs=pl.BlockSpec(memory_space=pltpu.VMEM),
        scratch_shapes=[pltpu.VMEM((kva, share), F32)],
        out_shape=pltpu.VMEM((len(gathered) * share, kva), BF16),
        compiler_params=pltpu.CompilerParams(vmem_limit_bytes=24 * MIB),
        cost_estimate=pl.CostEstimate(flops=1000, bytes_accessed=1000, transcendentals=0),
        name="natural_rows",
    )(*[pltpu.with_memory_space_constraint(x, pltpu.VMEM) for x in gathered])


def hidden_kernel(rows, down_t, out):
    out[...] = jnp.dot(rows[...], down_t[...], preferred_element_type=F32).astype(out.dtype)


def hidden_terms(rows, down_t):
    tokens = rows.shape[0]
    kva, columns = down_t.shape
    col_block = columns // 2 if columns % 256 == 0 else columns
    return pl.pallas_call(
        hidden_kernel,
        grid=(columns // col_block,),
        in_specs=[pl.BlockSpec((tokens, kva), lambda n: (0, 0)), pl.BlockSpec((kva, col_block), lambda n: (0, n))],
        out_specs=pl.BlockSpec((tokens, col_block), lambda n: (0, n)),
        out_shape=jax.ShapeDtypeStruct((tokens, columns), BF16),
        compiler_params=pltpu.CompilerParams(vmem_limit_bytes=24 * MIB),
        cost_estimate=pl.CostEstimate(flops=1000, bytes_accessed=1000, transcendentals=0),
        name="hidden_terms",
    )(rows, down_t)


def on_device(
    key_grad, value_grad, rope_grad, key_lift, value_lift, latent, norm_gain, doc_lengths, hidden, down_proj
):
    heads, groups = 4, 8
    core_bit, x_bit, y_bit = axis_bits()
    share = key_grad.shape[0] // heads
    kva = down_proj.shape[1]
    block = kva // groups

    def swap_head(array, bits):
        return lax.ppermute(array, "head", [(i, i ^ bits) for i in range(heads)])

    def swap_group(array, bits_of):
        return lax.ppermute(array, "group", [(i, i ^ bits_of(i)) for i in range(groups)])

    def first_bit(i):
        return y_bit if i & core_bit else x_bit

    def second_bit(i):
        return x_bit if i & core_bit else y_bit

    gain = norm_gain.reshape(1, -1)
    def terms(which, dtypes, lifts, lifts_here):
        return partial_terms(
            which, dtypes, doc_lengths, key_grad, value_grad, rope_grad, *lifts,
            latent, gain, share, kva - latent.shape[1], block, lifts_here,
        )

    p3, *lifts = terms((3,), (BF16,), (key_lift, value_lift), False)
    got3 = swap_head(p3, 1)
    p2, p1 = terms((2, 1), (F32, BF16), lifts, True)
    pair2 = (p2 + got3.astype(F32)).astype(BF16)
    pair2, p1, hidden, *lifts = lax.optimization_barrier((pair2, p1, hidden, *lifts))
    got2 = swap_head(pair2, 2)
    got1 = swap_head(p1, 1)
    sibling_hidden = swap_group(hidden, lambda i: core_bit)
    (p0,) = terms((0,), (F32,), lifts, True)
    q0 = (p0 + got1.astype(F32) + got2.astype(F32)).astype(BF16)
    q2 = swap_head(q0, 2)
    q1 = swap_head(q0, 1)
    q3 = swap_head(q2, 1)
    gathered = (q0, q1, q2, q3)
    sibling = tuple(swap_group(q, lambda i: core_bit) for q in gathered)

    def weights(part, dtypes):
        return weight_terms(gathered, sibling, hidden, sibling_hidden, block, part, 2, dtypes)

    for_both, for_first = weights(0, (BF16, BF16))
    got_both = swap_group(for_both, first_bit)
    sibling_hidden, for_first, for_both = lax.optimization_barrier((sibling_hidden, for_first, for_both))
    for_second, mine = weights(1, (F32, F32))
    kva_rows = natural_rows(gathered, block)
    for_first, for_second, kva_rows = lax.optimization_barrier((for_first, for_second, kva_rows))
    got_first = swap_group(for_first, first_bit)
    hidden_grad = hidden_terms(kva_rows, down_proj.T)
    got_second = swap_group((for_second + got_both.astype(F32)).astype(BF16), second_bit)
    weight_grad = mine + got_first.astype(F32) + got_second.astype(F32)
    return (hidden_grad, weight_grad)


def solution(mesh):
    shape = dict(mesh.shape)
    paired = shape["head"] == 4 and shape["group"] == 8
    return jax.shard_map(
        on_device if paired else on_device_any,
        mesh=mesh,
        in_specs=(
            P("group", "head"),
            P("group", "head"),
            P("group", "head"),
            P(None, "head"),
            P(None, "head"),
            P("group", None),
            P(),
            P("group", None),
            P("group", "head"),
            P("head", None),
        ),
        out_specs=(P("group", "head"), P("group", "head")),
        check_vma=False,
    )
```

time: 62.8 us -> 54.5 us (0.87)
  waiting for transfers between devices: 27.5 us -> 15.6 us
  starting transfers between devices: 14 us -> 16.8 us
  Pallas kernels: 19.4 us -> 20.2 us
    ppermute x6, waiting for transfers between devices: 17 us -> 9.28 us  [swap_head(): return lax.ppermute(array, 'head', [(i, i ^ bits) for i in range(heads)])]
    ppermute x7 -> x8, waiting for transfers between devices: 10.5 us -> 6.33 us  [swap_group(): lax.ppermute(array, 'group', [(i, i ^ bits_of(i)) for i in range(groups)])]
    ppermute x6, starting transfers between devices: 9.92 us -> 12.5 us  [swap_head(): return lax.ppermute(array, 'head', [(i, i ^ bits) for i in range(heads)])]
    pallas_call x4 -> x7, Pallas kernels: 19.4 us -> 20.2 us  [the longest x3 15.4 us: partial_terms(): pl.pallas_call(functools.partial(partial_kernel, which=which, dtypes=dtyp...]
    ppermute x7 -> x8, starting transfers between devices: 4.03 us -> 4.34 us  [swap_group(): lax.ppermute(array, 'group', [(i, i ^ bits_of(i)) for i in range(groups)])]
  transfers between devices with their start and end apart: 13 -> 14, of which waited for: 6 -> 6; matrix products, arithmetic and copies ran while one was open for 0% -> 0% of each run, Pallas kernels for 29% -> 26%
where the time goes in v3:
time: 54.5 us; the launch traced here: 54.4 us
  Pallas kernels  20.2 us (37%)
  starting transfers between devices  16.8 us (31%)
  waiting for transfers between devices  15.6 us (29%)
  other arithmetic  1.02 us (2%)
  between operations  0.75 us (1%)
    pallas_call x3, Pallas kernels, partial_terms(): pl.pallas_call(functools.partial(partial_kernel, which=which, dtypes=dtyp...  15.4 us
    ppermute x6, starting transfers between devices, swap_head(): return lax.ppermute(array, 'head', [(i, i ^ bits) for i in range(heads)])  12.5 us
    ppermute x6, waiting for transfers between devices, swap_head(): return lax.ppermute(array, 'head', [(i, i ^ bits) for i in range(heads)])  9.28 us
    ppermute x8, waiting for transfers between devices, swap_group(): lax.ppermute(array, 'group', [(i, i ^ bits_of(i)) for i in range(groups)])  6.33 us
    ppermute x8, starting transfers between devices, swap_group(): lax.ppermute(array, 'group', [(i, i ^ bits_of(i)) for i in range(groups)])  4.34 us
    pallas_call x1, Pallas kernels, hidden_terms(): pl.pallas_call(hidden_kernel, grid=(columns // col_block,), in_specs=[pl....  2.99 us
    pallas_call x2, Pallas kernels, weight_terms(): pl.pallas_call(functools.partial(weight_kernel, part=part, parts=parts),...  1.43 us
  transfers between devices with their start and end apart: 14, of which 6 were waited for; matrix products, arithmetic and copies ran while one was open for 0% of the time, Pallas kernels for 26%

profile of v3, /device:TPU:0, one launch (start us, length us, event | category | flops | bytes accessed | tf_op | source)
XLA Modules:
  0.0 54.4 jit_solution(11587605152178840191)
XLA Ops:
  0.6 5.3 %partial_terms.3 = (bf16[576,128]{1,0:T(8,128)(2,1)S(1)}, bf16[512,4096]{1,0:T(8,128)(2,1)S(1)}, bf16[512,4096]{1,0:T(8,128)(2,1)S(1)}) custom-call(s32[1,4]{1,0:T(1,128)} %refs_0_.5, bf16[512,4096]{1,0:T(8,128)(2,1)} %refs_1_.5, bf16[512,4096]{1,0:T(8,128)(2,1)} %refs_2_.5, bf16[512,2048]{1,0:T(8,128)(2,1)} %refs_3_.5, bf16[512,4096]{1,0:T(8,128)(2,1)} %refs_4_.1, ...), custom_call_target="tpu_custom_call" | custom-call | flops 1073741824 | bytes 11010048 | tf_op jit(solution)/shard_map/partial_terms/pallas_call | solution.py:190
  6.0 3.1 %collective-permute-start = (bf16[576,128]{1,0:T(8,128)(2,1)S(1)}, bf16[576,128]{1,0:T(8,128)(2,1)S(1)}, u32[]{:S(2)}, u32[]{:S(2)}) collective-permute-start(bf16[576,128]{1,0:T(8,128)(2,1)S(1)} %get-tuple-element.24), channel_id=1, source_target_pairs={{0,1},{1,0},{2,3},{3,2},{4,5},{5,4},{6,7},{7,6},{8,9},{9,8},{10,11... | collective-permute-start | bytes 442376 | tf_op jit(solution)/shard_map/ppermute | solution.py:317
  9.0 5.4 %partial_terms.4 = (f32[576,128]{1,0:T(8,128)S(1)}, bf16[576,128]{1,0:T(8,128)(2,1)S(1)}) custom-call(s32[1,4]{1,0:T(1,128)} %refs_0_.5, bf16[512,4096]{1,0:T(8,128)(2,1)} %refs_1_.5, bf16[512,4096]{1,0:T(8,128)(2,1)} %refs_2_.5, bf16[512,2048]{1,0:T(8,128)(2,1)} %refs_3_.5, bf16[512,4096]{1,0:T(8,128)(2,1)S(1)} %get-tuple-element.27.refs_4_, ...), custom_call_target="tpu_custom_call" | custom-call | flops 2147483648 | bytes 13631488 | tf_op jit(solution)/shard_map/partial_terms/pallas_call | solution.py:190
  14.4 0.0 collective-permute-done
  14.5 0.1 collective-permute-start.1
  14.6 0.2 collective-permute-start.2
  14.8 2.9 %collective-permute-start.3 = (bf16[576,128]{1,0:T(8,128)(2,1)S(1)}, bf16[576,128]{1,0:T(8,128)(2,1)S(1)}, u32[]{:S(2)}, u32[]{:S(2)}) collective-permute-start(bf16[576,128]{1,0:T(8,128)(2,1)S(1)} %add_convert_fusion.2), channel_id=1, source_target_pairs={{0,2},{1,3},{2,0},{3,1},{4,6},{5,7},{6,4},{7,5},{8,10},{9,11},{10,... | collective-permute-start | bytes 442376 | tf_op jit(solution)/shard_map/ppermute | solution.py:317
  17.7 4.7 %partial_terms.5 = f32[576,128]{1,0:T(8,128)S(1)} custom-call(s32[1,4]{1,0:T(1,128)} %refs_0_.5, bf16[512,4096]{1,0:T(8,128)(2,1)} %refs_1_.5, bf16[512,4096]{1,0:T(8,128)(2,1)} %refs_2_.5, bf16[512,2048]{1,0:T(8,128)(2,1)} %refs_3_.5, bf16[512,4096]{1,0:T(8,128)(2,1)S(1)} %get-tuple-element.27.refs_4_, bf16[512,4096]{1,0:T(8,128)(2,1)S(1)} %get-tuple-element.28.refs_5_, ...), custom_call_target="tpu_custom_call" | custom-call | flops 1073741824 | bytes 11010048 | tf_op jit(solution)/shard_map/partial_terms/pallas_call | solution.py:190
  22.4 1.6 %collective-permute-done.2 = bf16[576,128]{1,0:T(8,128)(2,1)S(1)} collective-permute-done((bf16[576,128]{1,0:T(8,128)(2,1)S(1)}, bf16[576,128]{1,0:T(8,128)(2,1)S(1)}, u32[]{:S(2)}, u32[]{:S(2)}) %collective-permute-start.2) | collective-permute-done | bytes 147488 | tf_op jit(solution)/shard_map/ppermute | solution.py:317
  24.0 0.1 add_convert_fusion.1.refs_0_
  24.1 1.3 %collective-permute-start.5 = (bf16[576,128]{1,0:T(8,128)(2,1)S(1)}, bf16[576,128]{1,0:T(8,128)(2,1)S(1)}, u32[]{:S(2)}, u32[]{:S(2)}) collective-permute-start(bf16[576,128]{1,0:T(8,128)(2,1)S(1)} %add_convert_fusion.1.refs_0_), channel_id=1, source_target_pairs={{0,2},{1,3},{2,0},{3,1},{4,6},{5,7},{6,4},{7,5},{8,10},{9,11},{10,... | collective-permute-start | bytes 442376 | tf_op jit(solution)/shard_map/ppermute | solution.py:317
  25.4 4.0 %collective-permute-start.4 = (bf16[576,128]{1,0:T(8,128)(2,1)S(1)}, bf16[576,128]{1,0:T(8,128)(2,1)S(1)}, u32[]{:S(2)}, u32[]{:S(2)}) collective-permute-start(bf16[576,128]{1,0:T(8,128)(2,1)S(1)} %add_convert_fusion.1.refs_0_), channel_id=1, source_target_pairs={{0,1},{1,0},{2,3},{3,2},{4,5},{5,4},{6,7},{7,6},{8,9},{9,8},{10,11... | collective-permute-start | bytes 442376 | tf_op jit(solution)/shard_map/ppermute | solution.py:317
  29.4 4.0 %collective-permute-done.5.refs_2_ = bf16[576,128]{1,0:T(8,128)(2,1)S(1)} collective-permute-done((bf16[576,128]{1,0:T(8,128)(2,1)S(1)}, bf16[576,128]{1,0:T(8,128)(2,1)S(1)}, u32[]{:S(2)}, u32[]{:S(2)}) %collective-permute-start.5) | collective-permute-done | bytes 147488 | tf_op jit(solution)/shard_map/ppermute | solution.py:317
  33.4 1.0 %collective-permute-start.6 = (bf16[576,128]{1,0:T(8,128)(2,1)S(1)}, bf16[576,128]{1,0:T(8,128)(2,1)S(1)}, u32[]{:S(2)}, u32[]{:S(2)}) collective-permute-start(bf16[576,128]{1,0:T(8,128)(2,1)S(1)} %collective-permute-done.5.refs_2_), channel_id=1, source_target_pairs={{0,1},{1,0},{2,3},{3,2},{4,5},{5,4},{6,7},{7,6},{8,9},{9,8},{10,11... | collective-permute-start | bytes 442376 | tf_op jit(solution)/shard_map/ppermute | solution.py:317
  34.4 0.5 collective-permute-start.9
  34.9 0.0 collective-permute-done.4.refs_1_
  34.9 0.0 collective-permute-start.8
  34.9 3.6 %collective-permute-done.6.refs_3_ = bf16[576,128]{1,0:T(8,128)(2,1)S(1)} collective-permute-done((bf16[576,128]{1,0:T(8,128)(2,1)S(1)}, bf16[576,128]{1,0:T(8,128)(2,1)S(1)}, u32[]{:S(2)}, u32[]{:S(2)}) %collective-permute-start.6) | collective-permute-done | bytes 147488 | tf_op jit(solution)/shard_map/ppermute | solution.py:317
  38.5 0.0 collective-permute-done.9.refs_6_
  38.5 1.3 %collective-permute-done.10.refs_7_ = bf16[576,128]{1,0:T(8,128)(2,1)S(1)} collective-permute-done((bf16[576,128]{1,0:T(8,128)(2,1)S(1)}, bf16[576,128]{1,0:T(8,128)(2,1)S(1)}, u32[]{:S(2)}, u32[]{:S(2)}) %collective-permute-start.10) | collective-permute-done | bytes 147488 | tf_op jit(solution)/shard_map/ppermute | solution.py:320
  39.9 0.7 %weight_terms.2 = (bf16[72,1792]{1,0:T(8,128)(2,1)S(1)}, bf16[72,1792]{1,0:T(8,128)(2,1)S(1)}) custom-call(bf16[576,128]{1,0:T(8,128)(2,1)S(1)} %add_convert_fusion.1.refs_0_, bf16[576,128]{1,0:T(8,128)(2,1)S(1)} %collective-permute-done.4.refs_1_, bf16[576,128]{1,0:T(8,128)(2,1)S(1)} %collective-permute-done.5.refs_2_, ...), custom_call_target="tpu_custom_call" | custom-call | flops 1000 | bytes 1000 | tf_op jit(solution)/shard_map/weight_terms/pallas_call | solution.py:250
  40.6 0.0 copy-start.1
  40.6 1.6 %collective-permute-start.12 = (bf16[72,1792]{1,0:T(8,128)(2,1)S(1)}, bf16[72,1792]{1,0:T(8,128)(2,1)S(1)}, u32[]{:S(2)}, u32[]{:S(2)}) collective-permute-start(bf16[72,1792]{1,0:T(8,128)(2,1)S(1)} %get-tuple-element.32), channel_id=1, source_target_pairs={{0,8},{4,20},{8,0},{12,28},{16,24},{20,4},{24,16},{28,12},{1,9},{5... | collective-permute-start | bytes 774152 | tf_op jit(solution)/shard_map/ppermute | solution.py:320
  42.2 0.3 natural_rows.1.rows
  42.5 0.7 %weight_terms.3 = (f32[72,1792]{1,0:T(8,128)S(1)}, f32[72,1792]{1,0:T(8,128)S(1)}) custom-call(bf16[576,128]{1,0:T(8,128)(2,1)S(1)} %add_convert_fusion.1.refs_0_, bf16[576,128]{1,0:T(8,128)(2,1)S(1)} %collective-permute-done.4.refs_1_, bf16[576,128]{1,0:T(8,128)(2,1)S(1)} %collective-permute-done.5.refs_2_, ...), custom_call_target="tpu_custom_call" | custom-call | flops 1000 | bytes 1000 | tf_op jit(solution)/shard_map/weight_terms/pallas_call | solution.py:250
  43.3 0.6 %collective-permute-start.11 = (bf16[72,1792]{1,0:T(8,128)(2,1)S(1)}, bf16[72,1792]{1,0:T(8,128)(2,1)S(1)}, u32[]{:S(2)}, u32[]{:S(2)}) collective-permute-start(bf16[72,1792]{1,0:T(8,128)(2,1)S(1)} %get-tuple-element.38), channel_id=1, source_target_pairs={{0,8},{4,20},{8,0},{12,28},{16,24},{20,4},{24,16},{28,12},{1,9},{5... | collective-permute-start | bytes 774152 | tf_op jit(solution)/shard_map/ppermute | solution.py:320
  43.9 3.2 %collective-permute-done.12 = bf16[72,1792]{1,0:T(8,128)(2,1)S(1)} collective-permute-done((bf16[72,1792]{1,0:T(8,128)(2,1)S(1)}, bf16[72,1792]{1,0:T(8,128)(2,1)S(1)}, u32[]{:S(2)}, u32[]{:S(2)}) %collective-permute-start.12) | collective-permute-done | bytes 258080 | tf_op jit(solution)/shard_map/ppermute | solution.py:320
  47.0 0.1 add_convert_fusion
  47.1 1.6 %collective-permute-start.13 = (bf16[72,1792]{1,0:T(8,128)(2,1)S(1)}, bf16[72,1792]{1,0:T(8,128)(2,1)S(1)}, u32[]{:S(2)}, u32[]{:S(2)}) collective-permute-start(bf16[72,1792]{1,0:T(8,128)(2,1)S(1)} %add_convert_fusion), channel_id=1, source_target_pairs={{0,16},{4,12},{8,24},{12,4},{16,0},{20,28},{24,8},{28,20},{1,17},{... | collective-permute-start | bytes 774152 | tf_op jit(solution)/shard_map/ppermute | solution.py:320
  48.7 3.0 %hidden_terms.1 = bf16[512,1792]{1,0:T(8,128)(2,1)} custom-call(bf16[512,576]{1,0:T(8,128)(2,1)S(1)} %natural_rows.1.rows, bf16[576,1792]{1,0:T(8,128)(2,1)S(1)} %bitcast.2), custom_call_target="tpu_custom_call" | custom-call | flops 1000 | bytes 1000 | tf_op jit(solution)/shard_map/hidden_terms/pallas_call | solution.py:295
  51.7 1.8 %collective-permute-done.13 = bf16[72,1792]{1,0:T(8,128)(2,1)S(1)} collective-permute-done((bf16[72,1792]{1,0:T(8,128)(2,1)S(1)}, bf16[72,1792]{1,0:T(8,128)(2,1)S(1)}, u32[]{:S(2)}, u32[]{:S(2)}) %collective-permute-start.13) | collective-permute-done | bytes 258080 | tf_op jit(solution)/shard_map/ppermute | solution.py:320
  53.5 0.9 %convert_add_fusion = f32[72,1792]{1,0:T(8,128)} fusion(bf16[72,1792]{1,0:T(8,128)(2,1)S(1)} %collective-permute-done.13, f32[72,1792]{1,0:T(8,128)S(1)} %get-tuple-element.37, bf16[72,1792]{1,0:T(8,128)(2,1)S(1)} %collective-permute-done.11), kind=kLoop, calls=%fused_computation | loop fusion | flops 516096 | bytes 1548288 | tf_op jit(solution)/shard_map/add | solution.py:363
  (11 shorter events, 0.1 us)
Async XLA Ops:
  6.0 8.5 %collective-permute-start = (bf16[576,128]{1,0:T(8,128)(2,1)S(1)}, bf16[576,128]{1,0:T(8,128)(2,1)S(1)}, u32[]{:S(2)}, u32[]{:S(2)}) collective-permute-start(bf16[576,128]{1,0:T(8,128)(2,1)S(1)} %get-tuple-element.24), channel_id=1, source_target_pairs={{0,1},{1,0},{2,3},{3,2},{4,5},{5,4},{6,7},{7,6},{8,9},{9,8},{10,11... | collective-permute-start | bytes 442376 | tf_op jit(solution)/shard_map/ppermute | solution.py:317
  9.0 5.4 %copy-start = (bf16[512,1792]{1,0:T(8,128)(2,1)S(1)}, bf16[512,1792]{1,0:T(8,128)(2,1)}, u32[]{:S(2)}) copy-start(bf16[512,1792]{1,0:T(8,128)(2,1)} %refs_8_.1) | copy-start | bytes 5505028
  14.5 25.4 %collective-permute-start.1 = (bf16[512,1792]{1,0:T(8,128)(2,1)S(1)}, bf16[512,1792]{1,0:T(8,128)(2,1)S(1)}, u32[]{:S(2)}, u32[]{:S(2)}) collective-permute-start(bf16[512,1792]{1,0:T(8,128)(2,1)S(1)} %copy-done), channel_id=1, source_target_pairs={{0,4},{4,0},{8,12},{12,8},{16,20},{20,16},{24,28},{28,24},{1,5},{5... | collective-permute-start | bytes 5505032 | tf_op jit(solution)/shard_map/ppermute | solution.py:320
  14.6 9.4 %collective-permute-start.2 = (bf16[576,128]{1,0:T(8,128)(2,1)S(1)}, bf16[576,128]{1,0:T(8,128)(2,1)S(1)}, u32[]{:S(2)}, u32[]{:S(2)}) collective-permute-start(bf16[576,128]{1,0:T(8,128)(2,1)S(1)} %get-tuple-element.29), channel_id=1, source_target_pairs={{0,1},{1,0},{2,3},{3,2},{4,5},{5,4},{6,7},{7,6},{8,9},{9,8},{10,11... | collective-permute-start | bytes 442376 | tf_op jit(solution)/shard_map/ppermute | solution.py:317
  14.8 9.2 %collective-permute-start.3 = (bf16[576,128]{1,0:T(8,128)(2,1)S(1)}, bf16[576,128]{1,0:T(8,128)(2,1)S(1)}, u32[]{:S(2)}, u32[]{:S(2)}) collective-permute-start(bf16[576,128]{1,0:T(8,128)(2,1)S(1)} %add_convert_fusion.2), channel_id=1, source_target_pairs={{0,2},{1,3},{2,0},{3,1},{4,6},{5,7},{6,4},{7,5},{8,10},{9,11},{10,... | collective-permute-start | bytes 442376 | tf_op jit(solution)/shard_map/ppermute | solution.py:317
  24.1 9.3 %collective-permute-start.5 = (bf16[576,128]{1,0:T(8,128)(2,1)S(1)}, bf16[576,128]{1,0:T(8,128)(2,1)S(1)}, u32[]{:S(2)}, u32[]{:S(2)}) collective-permute-start(bf16[576,128]{1,0:T(8,128)(2,1)S(1)} %add_convert_fusion.1.refs_0_), channel_id=1, source_target_pairs={{0,2},{1,3},{2,0},{3,1},{4,6},{5,7},{6,4},{7,5},{8,10},{9,11},{10,... | collective-permute-start | bytes 442376 | tf_op jit(solution)/shard_map/ppermute | solution.py:317
  25.4 9.5 %collective-permute-start.4 = (bf16[576,128]{1,0:T(8,128)(2,1)S(1)}, bf16[576,128]{1,0:T(8,128)(2,1)S(1)}, u32[]{:S(2)}, u32[]{:S(2)}) collective-permute-start(bf16[576,128]{1,0:T(8,128)(2,1)S(1)} %add_convert_fusion.1.refs_0_), channel_id=1, source_target_pairs={{0,1},{1,0},{2,3},{3,2},{4,5},{5,4},{6,7},{7,6},{8,9},{9,8},{10,11... | collective-permute-start | bytes 442376 | tf_op jit(solution)/shard_map/ppermute | solution.py:317
  33.4 5.1 %collective-permute-start.6 = (bf16[576,128]{1,0:T(8,128)(2,1)S(1)}, bf16[576,128]{1,0:T(8,128)(2,1)S(1)}, u32[]{:S(2)}, u32[]{:S(2)}) collective-permute-start(bf16[576,128]{1,0:T(8,128)(2,1)S(1)} %collective-permute-done.5.refs_2_), channel_id=1, source_target_pairs={{0,1},{1,0},{2,3},{3,2},{4,5},{5,4},{6,7},{7,6},{8,9},{9,8},{10,11... | collective-permute-start | bytes 442376 | tf_op jit(solution)/shard_map/ppermute | solution.py:317
  34.4 4.2 %collective-permute-start.7 = (bf16[576,128]{1,0:T(8,128)(2,1)S(1)}, bf16[576,128]{1,0:T(8,128)(2,1)S(1)}, u32[]{:S(2)}, u32[]{:S(2)}) collective-permute-start(bf16[576,128]{1,0:T(8,128)(2,1)S(1)} %add_convert_fusion.1.refs_0_), channel_id=1, source_target_pairs={{0,4},{4,0},{8,12},{12,8},{16,20},{20,16},{24,28},{28,24},{1,5},{5... | collective-permute-start | bytes 442376 | tf_op jit(solution)/shard_map/ppermute | solution.py:320
  34.4 4.2 %collective-permute-start.9 = (bf16[576,128]{1,0:T(8,128)(2,1)S(1)}, bf16[576,128]{1,0:T(8,128)(2,1)S(1)}, u32[]{:S(2)}, u32[]{:S(2)}) collective-permute-start(bf16[576,128]{1,0:T(8,128)(2,1)S(1)} %collective-permute-done.5.refs_2_), channel_id=1, source_target_pairs={{0,4},{4,0},{8,12},{12,8},{16,20},{20,16},{24,28},{28,24},{1,5},{5... | collective-permute-start | bytes 442376 | tf_op jit(solution)/shard_map/ppermute | solution.py:320
  34.9 3.7 %collective-permute-start.8 = (bf16[576,128]{1,0:T(8,128)(2,1)S(1)}, bf16[576,128]{1,0:T(8,128)(2,1)S(1)}, u32[]{:S(2)}, u32[]{:S(2)}) collective-permute-start(bf16[576,128]{1,0:T(8,128)(2,1)S(1)} %collective-permute-done.4.refs_1_), channel_id=1, source_target_pairs={{0,4},{4,0},{8,12},{12,8},{16,20},{20,16},{24,28},{28,24},{1,5},{5... | collective-permute-start | bytes 442376 | tf_op jit(solution)/shard_map/ppermute | solution.py:320
  38.5 1.4 %collective-permute-start.10 = (bf16[576,128]{1,0:T(8,128)(2,1)S(1)}, bf16[576,128]{1,0:T(8,128)(2,1)S(1)}, u32[]{:S(2)}, u32[]{:S(2)}) collective-permute-start(bf16[576,128]{1,0:T(8,128)(2,1)S(1)} %collective-permute-done.6.refs_3_), channel_id=1, source_target_pairs={{0,4},{4,0},{8,12},{12,8},{16,20},{20,16},{24,28},{28,24},{1,5},{5... | collective-permute-start | bytes 442376 | tf_op jit(solution)/shard_map/ppermute | solution.py:320
  40.6 8.1 %copy-start.1 = (bf16[1792,576]{0,1:T(8,128)(2,1)S(1)}, bf16[1792,576]{0,1:T(8,128)(2,1)}, u32[]{:S(2)}) copy-start(bf16[1792,576]{0,1:T(8,128)(2,1)} %param.19) | copy-start | bytes 6193156
  40.6 6.4 %collective-permute-start.12 = (bf16[72,1792]{1,0:T(8,128)(2,1)S(1)}, bf16[72,1792]{1,0:T(8,128)(2,1)S(1)}, u32[]{:S(2)}, u32[]{:S(2)}) collective-permute-start(bf16[72,1792]{1,0:T(8,128)(2,1)S(1)} %get-tuple-element.32), channel_id=1, source_target_pairs={{0,8},{4,20},{8,0},{12,28},{16,24},{20,4},{24,16},{28,12},{1,9},{5... | collective-permute-start | bytes 774152 | tf_op jit(solution)/shard_map/ppermute | solution.py:320
  43.3 8.4 %collective-permute-start.11 = (bf16[72,1792]{1,0:T(8,128)(2,1)S(1)}, bf16[72,1792]{1,0:T(8,128)(2,1)S(1)}, u32[]{:S(2)}, u32[]{:S(2)}) collective-permute-start(bf16[72,1792]{1,0:T(8,128)(2,1)S(1)} %get-tuple-element.38), channel_id=1, source_target_pairs={{0,8},{4,20},{8,0},{12,28},{16,24},{20,4},{24,16},{28,12},{1,9},{5... | collective-permute-start | bytes 774152 | tf_op jit(solution)/shard_map/ppermute | solution.py:320
  47.1 6.4 %collective-permute-start.13 = (bf16[72,1792]{1,0:T(8,128)(2,1)S(1)}, bf16[72,1792]{1,0:T(8,128)(2,1)S(1)}, u32[]{:S(2)}, u32[]{:S(2)}) collective-permute-start(bf16[72,1792]{1,0:T(8,128)(2,1)S(1)} %add_convert_fusion), channel_id=1, source_target_pairs={{0,16},{4,12},{8,24},{12,4},{16,0},{20,28},{24,8},{28,20},{1,17},{... | collective-permute-start | bytes 774152 | tf_op jit(solution)/shard_map/ppermute | solution.py:320

commit v4 on v3

--- a/solution.py
+++ b/solution.py
@@ -13,6 +13,9 @@
 LAST = (((1,), (1,)), ((), ()))
 FIRST = (((0,), (0,)), ((), ()))
 MIB = 1 << 20
+SHORT = pl.CostEstimate(flops=1000, bytes_accessed=1000, transcendentals=0)
+MEDIUM = pl.CostEstimate(flops=1 << 32, bytes_accessed=1000, transcendentals=0)
+LONG = pl.CostEstimate(flops=1 << 34, bytes_accessed=MIB, transcendentals=0)
 
 
 def positions(lengths, token_index):
@@ -76,13 +79,17 @@
     return 1, 2, 4
 
 
+def after(array, other):
+    return lax.optimization_barrier((array, other))
+
+
 def row_order(blocks):
     core, x, y = axis_bits()
     mine = lax.axis_index("group")
     first = jnp.where(mine & core == 0, x, y)
     other, second, both = mine ^ core, first ^ (x | y), x | y
-    order = [mine ^ both, mine ^ first, other ^ both, other ^ second]
-    order += [mine ^ second, mine, other ^ first, other]
+    order = [mine ^ both, other ^ both]
+    order += [mine ^ first, mine ^ second, mine, other ^ second, other ^ first, other]
     assert len(order) == blocks
     return order
 
@@ -209,28 +216,22 @@
         ],
         out_shape=out_shape,
         compiler_params=pltpu.CompilerParams(vmem_limit_bytes=28 * MIB),
-        cost_estimate=pl.CostEstimate(
-            flops=2 * tokens * width * key_cols * 2,
-            bytes_accessed=2 * (2 * width * key_cols + tokens * (2 * key_cols + rg.shape[1])),
-            transcendentals=0,
-        ),
+        cost_estimate=LONG,
         name="partial_terms",
     )(*[pltpu.with_memory_space_constraint(x, space) for x, space in zip(operands, spaces)])
 
 
-def weight_kernel(*refs, part, parts):
-    own, sibling = refs[:4], refs[4:8]
-    hidden, sibling_hidden = refs[8:10]
-    outs = refs[10:]
-    share = own[0].shape[1]
+def weight_kernel(*refs, skips):
+    shares, hidden, sibling_hidden, outs = refs[:8], refs[8], refs[9], refs[10:]
+    share = shares[0].shape[1]
     block = outs[0].shape[0]
     count = len(outs) * block
 
-    def rows_of(ref, side):
-        skip = 2 * part * count if ref.shape[0] == 2 * parts * count else 0
-        return ref[skip + side * count : skip + (side + 1) * count]
-
-    left = jnp.concatenate([rows_of(r, 0) for r in own] + [rows_of(r, 1) for r in sibling], axis=1)
+    def rows_of(ref, skip, side):
+        return ref[skip : skip + 2 * count].astype(F32)[side * count : (side + 1) * count]
+
+    left = [rows_of(ref, skip, i // 4) for i, (ref, skip) in enumerate(zip(shares, skips))]
+    left = jnp.concatenate(left, axis=1).astype(BF16)
     columns = hidden.shape[1]
     width = 256 if columns % 256 == 0 else columns
     me = lax.axis_index("head")
@@ -243,45 +244,93 @@
             out[:, cols] = result[i * block : (i + 1) * block].astype(out.dtype)
 
 
-def weight_terms(own, sibling, hidden, sibling_hidden, block, part, parts, dtypes):
+def weight_terms(shares, skips, hidden, sibling_hidden, block, dtypes):
     columns = hidden.shape[1]
     vmem = pl.BlockSpec(memory_space=pltpu.VMEM)
-    operands = (*own, *sibling, hidden, sibling_hidden)
-    return pl.pallas_call(
-        functools.partial(weight_kernel, part=part, parts=parts),
+    operands = (*shares, hidden, sibling_hidden)
+    return pl.pallas_call(
+        functools.partial(weight_kernel, skips=skips),
         in_specs=[vmem] * len(operands),
         out_specs=[vmem] * len(dtypes),
         out_shape=[pltpu.VMEM((block, columns), dtype) for dtype in dtypes],
         compiler_params=pltpu.CompilerParams(vmem_limit_bytes=24 * MIB),
-        cost_estimate=pl.CostEstimate(flops=1000, bytes_accessed=1000, transcendentals=0),
+        cost_estimate=SHORT,
         name="weight_terms",
     )(*[pltpu.with_memory_space_constraint(x, pltpu.VMEM) for x in operands])
 
 
 def natural_kernel(*refs, block):
-    shares, out, natural = refs[:-2], refs[-2], refs[-1]
+    even_a, odd_a, even_b, odd_b, out, natural = refs
+    head, rest = even_a.shape[0] // 2, even_b.shape[0] // 2
+    parts = [(ahead[:head], then[:rest]) for ahead, then in ((even_a, even_b), (odd_a, odd_b))]
+    parts += [(ahead[head:], then[rest:]) for ahead, then in ((even_a, even_b), (odd_a, odd_b))]
     me = lax.axis_index("head")
     order = row_order(natural.shape[0] // block)
-    share = shares[0].shape[1]
-    for r, q in enumerate(shares):
-        ordered = q[...].astype(F32)
+    share = natural.shape[1]
+    for r, pieces in enumerate(parts):
+        ordered = jnp.concatenate([piece.astype(F32) for piece in pieces], axis=0)
         for i, place in enumerate(order):
             natural[pl.ds(pl.multiple_of(place * block, 8), block), :] = ordered[i * block : (i + 1) * block]
         out[pl.ds(pl.multiple_of((me ^ r) * share, share), share), :] = natural[...].T.astype(BF16)
 
 
-def natural_rows(gathered, block):
-    kva, share = gathered[0].shape
+def natural_rows(parts, block):
+    kva, share = sum(part.shape[0] for part in parts) // 4, parts[0].shape[1]
     return pl.pallas_call(
         functools.partial(natural_kernel, block=block),
-        in_specs=[pl.BlockSpec(memory_space=pltpu.VMEM)] * len(gathered),
+        in_specs=[pl.BlockSpec(memory_space=pltpu.VMEM)] * len(parts),
         out_specs=pl.BlockSpec(memory_space=pltpu.VMEM),
         scratch_shapes=[pltpu.VMEM((kva, share), F32)],
-        out_shape=pltpu.VMEM((len(gathered) * share, kva), BF16),
+        out_shape=pltpu.VMEM((4 * share, kva), BF16),
         compiler_params=pltpu.CompilerParams(vmem_limit_bytes=24 * MIB),
-        cost_estimate=pl.CostEstimate(flops=1000, bytes_accessed=1000, transcendentals=0),
+        cost_estimate=SHORT,
         name="natural_rows",
-    )(*[pltpu.with_memory_space_constraint(x, pltpu.VMEM) for x in gathered])
+    )(*[pltpu.with_memory_space_constraint(x, pltpu.VMEM) for x in parts])
+
+
+def add_kernel(*refs, starts, waits):
+    outs = refs[len(starts) + waits :]
+    at = 0
+    for out in outs:
+        rows = out.shape[0]
+        total = sum(ref[start + at : start + at + rows].astype(F32) for ref, start in zip(refs, starts))
+        out[...] = total.astype(out.dtype)
+        at += rows
+
+
+def add_rows(terms, starts, outs, waits=()):
+    columns = terms[0].shape[1]
+    vmem = pl.BlockSpec(memory_space=pltpu.VMEM)
+    return pl.pallas_call(
+        functools.partial(add_kernel, starts=starts, waits=len(waits)),
+        in_specs=[vmem] * len(terms) + [pl.BlockSpec(memory_space=pl.ANY)] * len(waits),
+        out_specs=[vmem] * len(outs),
+        out_shape=[pltpu.VMEM((rows, columns), dtype) for rows, dtype in outs],
+        compiler_params=pltpu.CompilerParams(vmem_limit_bytes=24 * MIB),
+        cost_estimate=LONG,
+        name="add_rows",
+    )(*[pltpu.with_memory_space_constraint(x, pltpu.VMEM) for x in terms], *waits)
+
+
+def stack_kernel(*refs, count):
+    out, at = refs[-1], 0
+    for ref in refs[:count]:
+        out[at : at + ref.shape[0]] = ref[...]
+        at += ref.shape[0]
+
+
+def stack(arrays, *waits, cost=None):
+    rows = sum(array.shape[0] for array in arrays)
+    vmem = pl.BlockSpec(memory_space=pltpu.VMEM)
+    return pl.pallas_call(
+        functools.partial(stack_kernel, count=len(arrays)),
+        in_specs=[vmem] * len(arrays) + [pl.BlockSpec(memory_space=pl.ANY)] * len(waits),
+        out_specs=vmem,
+        out_shape=pltpu.VMEM((rows, arrays[0].shape[1]), arrays[0].dtype),
+        compiler_params=pltpu.CompilerParams(vmem_limit_bytes=24 * MIB),
+        cost_estimate=cost or LONG,
+        name="stack",
+    )(*[pltpu.with_memory_space_constraint(x, pltpu.VMEM) for x in arrays], *waits)
 
 
 def hidden_kernel(rows, down_t, out):
@@ -299,7 +348,7 @@
         out_specs=pl.BlockSpec((tokens, col_block), lambda n: (0, n)),
         out_shape=jax.ShapeDtypeStruct((tokens, columns), BF16),
         compiler_params=pltpu.CompilerParams(vmem_limit_bytes=24 * MIB),
-        cost_estimate=pl.CostEstimate(flops=1000, bytes_accessed=1000, transcendentals=0),
+        cost_estimate=LONG,
         name="hidden_terms",
     )(rows, down_t)
 
@@ -319,6 +368,9 @@
     def swap_group(array, bits_of):
         return lax.ppermute(array, "group", [(i, i ^ bits_of(i)) for i in range(groups)])
 
+    def swap_core(array):
+        return swap_group(array, lambda i: core_bit)
+
     def first_bit(i):
         return y_bit if i & core_bit else x_bit
 
@@ -335,31 +387,39 @@
     p3, *lifts = terms((3,), (BF16,), (key_lift, value_lift), False)
     got3 = swap_head(p3, 1)
     p2, p1 = terms((2, 1), (F32, BF16), lifts, True)
-    pair2 = (p2 + got3.astype(F32)).astype(BF16)
+    (pair2,) = add_rows((p2, got3), (0, 0), [(kva, BF16)])
     pair2, p1, hidden, *lifts = lax.optimization_barrier((pair2, p1, hidden, *lifts))
     got2 = swap_head(pair2, 2)
     got1 = swap_head(p1, 1)
-    sibling_hidden = swap_group(hidden, lambda i: core_bit)
+    sibling_hidden = swap_core(hidden)
     (p0,) = terms((0,), (F32,), lifts, True)
-    q0 = (p0 + got1.astype(F32) + got2.astype(F32)).astype(BF16)
-    q2 = swap_head(q0, 2)
-    q1 = swap_head(q0, 1)
-    q3 = swap_head(q2, 1)
-    gathered = (q0, q1, q2, q3)
-    sibling = tuple(swap_group(q, lambda i: core_bit) for q in gathered)
-
-    def weights(part, dtypes):
-        return weight_terms(gathered, sibling, hidden, sibling_hidden, block, part, 2, dtypes)
-
-    for_both, for_first = weights(0, (BF16, BF16))
+    ahead, rest = 2 * block, kva - 2 * block
+    (q0_a,) = add_rows((p0, got1, got2), (0, 0, 0), [(ahead, BF16)])
+    (q0_b,) = add_rows((p0, got1, got2), (ahead,) * 3, [(rest, BF16)], (q0_a,))
+    q2_a, q2_b = swap_head(q0_a, 2), swap_head(q0_b, 2)
+    even_a = stack((q0_a, q2_a))
+    odd_a = swap_head(even_a, 1)
+    q1_b = swap_head(stack((q0_b,), even_a, cost=SHORT), 1)
+    q2_b = stack((q2_b,), even_a)
+    q3_b = swap_head(q2_b, 1)
+    odd_a = stack((odd_a,), q2_b, cost=MEDIUM)
+    even_b = stack((q0_b, q2_b), cost=SHORT)
+
+    def weights(even, odd, dtypes):
+        shares = (even, odd) * 2 + (swap_core(even), swap_core(odd)) * 2
+        half = even.shape[0] // 2
+        return weight_terms(shares, (0, 0, half, half) * 2, hidden, sibling_hidden, block, dtypes)
+
+    (for_both,) = weights(even_a, odd_a, (BF16,))
     got_both = swap_group(for_both, first_bit)
-    sibling_hidden, for_first, for_both = lax.optimization_barrier((sibling_hidden, for_first, for_both))
-    for_second, mine = weights(1, (F32, F32))
-    kva_rows = natural_rows(gathered, block)
-    for_first, for_second, kva_rows = lax.optimization_barrier((for_first, for_second, kva_rows))
+    odd_b = stack((q1_b, q3_b), for_both)
+    for_first, for_second, mine = weights(even_b, odd_b, (BF16, F32, F32))
     got_first = swap_group(for_first, first_bit)
+    kva_rows = natural_rows((even_a, odd_a, even_b, odd_b), block)
+    (to_second,) = add_rows((for_second, got_both), (0, 0), [(block, BF16)], (kva_rows,))
+    got_second = swap_group(to_second, second_bit)
+    kva_rows, to_second = after(kva_rows, to_second)
     hidden_grad = hidden_terms(kva_rows, down_proj.T)
-    got_second = swap_group((for_second + got_both.astype(F32)).astype(BF16), second_bit)
     weight_grad = mine + got_first.astype(F32) + got_second.astype(F32)
     return (hidden_grad, weight_grad)
 

time: 54.5 us -> 50.8 us (0.932)
  waiting for transfers between devices: 15.6 us -> 8.98 us
  starting transfers between devices: 16.8 us -> 19 us
    ppermute x6 -> x8, waiting for transfers between devices: 9.28 us -> 4.89 us  [swap_head(): return lax.ppermute(array, 'head', [(i, i ^ bits) for i in range(heads)])]
    ppermute x8, waiting for transfers between devices: 6.33 us -> 4.09 us  [swap_group(): lax.ppermute(array, 'group', [(i, i ^ bits_of(i)) for i in range(groups)])]
    ppermute x8, starting transfers between devices: 4.34 us -> 5.46 us  [swap_group(): lax.ppermute(array, 'group', [(i, i ^ bits_of(i)) for i in range(groups)])]
    ppermute x6 -> x8, starting transfers between devices: 12.5 us -> 13.6 us  [swap_head(): return lax.ppermute(array, 'head', [(i, i ^ bits) for i in range(heads)])]
    pallas_call x2 -> x12, Pallas kernels: 1.43 us -> 1.98 us  [the longest x2 1.78 us: weight_terms(): pl.pallas_call(functools.partial(weight_kernel, skips=skips), in_specs=[v...]
  transfers between devices with their start and end apart: 14 -> 16, of which waited for: 6 -> 8; matrix products, arithmetic and copies ran while one was open for 0% -> 0% of each run, Pallas kernels for 26% -> 30%
where the time goes in v4:
time: 50.8 us; the launch traced here: 50.3 us
  Pallas kernels  20.6 us (41%)
  starting transfers between devices  19 us (37%)
  waiting for transfers between devices  8.98 us (18%)
  other arithmetic  0.87 us (2%)
  between operations  0.77 us (2%)
    pallas_call x3, Pallas kernels, partial_terms(): pl.pallas_call(functools.partial(partial_kernel, which=which, dtypes=dtyp...  15.3 us
    ppermute x8, starting transfers between devices, swap_head(): return lax.ppermute(array, 'head', [(i, i ^ bits) for i in range(heads)])  13.6 us
    ppermute x8, starting transfers between devices, swap_group(): lax.ppermute(array, 'group', [(i, i ^ bits_of(i)) for i in range(groups)])  5.46 us
    ppermute x8, waiting for transfers between devices, swap_head(): return lax.ppermute(array, 'head', [(i, i ^ bits) for i in range(heads)])  4.89 us
    ppermute x8, waiting for transfers between devices, swap_group(): lax.ppermute(array, 'group', [(i, i ^ bits_of(i)) for i in range(groups)])  4.09 us
    pallas_call x1, Pallas kernels, hidden_terms(): pl.pallas_call(hidden_kernel, grid=(columns // col_block,), in_specs=[pl....  2.98 us
    pallas_call x2, Pallas kernels, weight_terms(): pl.pallas_call(functools.partial(weight_kernel, skips=skips), in_specs=[v...  1.78 us
  transfers between devices with their start and end apart: 16, of which 8 were waited for; matrix products, arithmetic and copies ran while one was open for 0% of the time, Pallas kernels for 30%

profile of v4, /device:TPU:0, one launch (start us, length us, event | category | flops | bytes accessed | tf_op | source)
XLA Modules:
  0.0 50.3 jit_solution(5511050432885833830)
XLA Ops:
  0.6 5.3 %partial_terms.3 = (bf16[576,128]{1,0:T(8,128)(2,1)S(1)}, bf16[512,4096]{1,0:T(8,128)(2,1)S(1)}, bf16[512,4096]{1,0:T(8,128)(2,1)S(1)}) custom-call(s32[1,4]{1,0:T(1,128)} %refs_0_.5, bf16[512,4096]{1,0:T(8,128)(2,1)} %refs_1_.5, bf16[512,4096]{1,0:T(8,128)(2,1)} %refs_2_.5, bf16[512,2048]{1,0:T(8,128)(2,1)} %refs_3_.5, bf16[512,4096]{1,0:T(8,128)(2,1)} %refs_4_.1, ...), custom_call_target="tpu_custom_call" | custom-call | flops 17179869184 | bytes 1048576 | tf_op jit(solution)/shard_map/partial_terms/pallas_call | solution.py:197
  6.0 3.1 %collective-permute-start = (bf16[576,128]{1,0:T(8,128)(2,1)S(1)}, bf16[576,128]{1,0:T(8,128)(2,1)S(1)}, u32[]{:S(2)}, u32[]{:S(2)}) collective-permute-start(bf16[576,128]{1,0:T(8,128)(2,1)S(1)} %get-tuple-element.19), channel_id=1, source_target_pairs={{0,1},{1,0},{2,3},{3,2},{4,5},{5,4},{6,7},{7,6},{8,9},{9,8},{10,11... | collective-permute-start | bytes 442376 | tf_op jit(solution)/shard_map/ppermute | solution.py:366
  9.0 5.3 %partial_terms.4 = (f32[576,128]{1,0:T(8,128)S(1)}, bf16[576,128]{1,0:T(8,128)(2,1)S(1)}) custom-call(s32[1,4]{1,0:T(1,128)} %refs_0_.5, bf16[512,4096]{1,0:T(8,128)(2,1)} %refs_1_.5, bf16[512,4096]{1,0:T(8,128)(2,1)} %refs_2_.5, bf16[512,2048]{1,0:T(8,128)(2,1)} %refs_3_.5, bf16[512,4096]{1,0:T(8,128)(2,1)S(1)} %get-tuple-element.21.refs_4_, ...), custom_call_target="tpu_custom_call" | custom-call | flops 17179869184 | bytes 1048576 | tf_op jit(solution)/shard_map/partial_terms/pallas_call | solution.py:197
  14.3 0.0 copy-start
  14.4 0.4 collective-permute-start.1
  14.7 2.7 %collective-permute-start.2 = (bf16[576,128]{1,0:T(8,128)(2,1)S(1)}, bf16[576,128]{1,0:T(8,128)(2,1)S(1)}, u32[]{:S(2)}, u32[]{:S(2)}) collective-permute-start(bf16[576,128]{1,0:T(8,128)(2,1)S(1)} %add_rows.4), channel_id=1, source_target_pairs={{0,2},{1,3},{2,0},{3,1},{4,6},{5,7},{6,4},{7,5},{8,10},{9,11},{10,... | collective-permute-start | bytes 442376 | tf_op jit(solution)/shard_map/ppermute | solution.py:366
  17.5 4.7 %partial_terms.5.refs_0_ = f32[576,128]{1,0:T(8,128)S(1)} custom-call(s32[1,4]{1,0:T(1,128)} %refs_0_.5, bf16[512,4096]{1,0:T(8,128)(2,1)} %refs_1_.5, bf16[512,4096]{1,0:T(8,128)(2,1)} %refs_2_.5, bf16[512,2048]{1,0:T(8,128)(2,1)} %refs_3_.5, bf16[512,4096]{1,0:T(8,128)(2,1)S(1)} %get-tuple-element.21.refs_4_, ...), custom_call_target="tpu_custom_call" | custom-call | flops 17179869184 | bytes 1048576 | tf_op jit(solution)/shard_map/partial_terms/pallas_call | solution.py:197
  22.2 0.7 %collective-permute-done.1.refs_1_ = bf16[576,128]{1,0:T(8,128)(2,1)S(1)} collective-permute-done((bf16[576,128]{1,0:T(8,128)(2,1)S(1)}, bf16[576,128]{1,0:T(8,128)(2,1)S(1)}, u32[]{:S(2)}, u32[]{:S(2)}) %collective-permute-start.1) | collective-permute-done | bytes 147488 | tf_op jit(solution)/shard_map/ppermute | solution.py:366
  22.9 1.4 %collective-permute-start.3 = (bf16[144,128]{1,0:T(8,128)(2,1)S(1)}, bf16[144,128]{1,0:T(8,128)(2,1)S(1)}, u32[]{:S(2)}, u32[]{:S(2)}) collective-permute-start(bf16[144,128]{1,0:T(8,128)(2,1)S(1)} %add_rows.5.refs_0_.refs_3_), channel_id=1, source_target_pairs={{0,2},{1,3},{2,0},{3,1},{4,6},{5,7},{6,4},{7,5},{8,10},{9,11},{10,... | collective-permute-start | bytes 110600 | tf_op jit(solution)/shard_map/ppermute | solution.py:366
  24.3 1.7 %collective-permute-start.5 = (bf16[432,128]{1,0:T(8,128)(2,1)S(1)}, bf16[432,128]{1,0:T(8,128)(2,1)S(1)}, u32[]{:S(2)}, u32[]{:S(2)}) collective-permute-start(bf16[432,128]{1,0:T(8,128)(2,1)S(1)} %add_rows.6.refs_0_), channel_id=1, source_target_pairs={{0,2},{1,3},{2,0},{3,1},{4,6},{5,7},{6,4},{7,5},{8,10},{9,11},{10,... | collective-permute-start | bytes 331784 | tf_op jit(solution)/shard_map/ppermute | solution.py:366
  26.0 2.5 %collective-permute-done.3.refs_1_ = bf16[144,128]{1,0:T(8,128)(2,1)S(1)} collective-permute-done((bf16[144,128]{1,0:T(8,128)(2,1)S(1)}, bf16[144,128]{1,0:T(8,128)(2,1)S(1)}, u32[]{:S(2)}, u32[]{:S(2)}) %collective-permute-start.3) | collective-permute-done | bytes 36896 | tf_op jit(solution)/shard_map/ppermute | solution.py:366
  28.6 2.1 %collective-permute-start.4 = (bf16[288,128]{1,0:T(8,128)(2,1)S(1)}, bf16[288,128]{1,0:T(8,128)(2,1)S(1)}, u32[]{:S(2)}, u32[]{:S(2)}) collective-permute-start(bf16[288,128]{1,0:T(8,128)(2,1)S(1)} %stack.6.refs_1_.refs_0_.refs_2_), channel_id=1, source_target_pairs={{0,1},{1,0},{2,3},{3,2},{4,5},{5,4},{6,7},{7,6},{8,9},{9,8},{10,11... | collective-permute-start | bytes 221192 | tf_op jit(solution)/shard_map/ppermute | solution.py:366
  30.6 0.1 collective-permute-start.6
  30.7 1.1 %collective-permute-done.5.refs_0_ = bf16[432,128]{1,0:T(8,128)(2,1)S(1)} collective-permute-done((bf16[432,128]{1,0:T(8,128)(2,1)S(1)}, bf16[432,128]{1,0:T(8,128)(2,1)S(1)}, u32[]{:S(2)}, u32[]{:S(2)}) %collective-permute-start.5) | collective-permute-done | bytes 110624 | tf_op jit(solution)/shard_map/ppermute | solution.py:366
  31.8 2.2 %collective-permute-start.7 = (bf16[432,128]{1,0:T(8,128)(2,1)S(1)}, bf16[432,128]{1,0:T(8,128)(2,1)S(1)}, u32[]{:S(2)}, u32[]{:S(2)}) collective-permute-start(bf16[432,128]{1,0:T(8,128)(2,1)S(1)} %stack.7.refs_1_), channel_id=1, source_target_pairs={{0,1},{1,0},{2,3},{3,2},{4,5},{5,4},{6,7},{7,6},{8,9},{9,8},{10,11... | collective-permute-start | bytes 331784 | tf_op jit(solution)/shard_map/ppermute | solution.py:366
  34.0 0.1 collective-permute-start.9
  34.1 0.6 %collective-permute-start.11 = (bf16[864,128]{1,0:T(8,128)(2,1)S(1)}, bf16[864,128]{1,0:T(8,128)(2,1)S(1)}, u32[]{:S(2)}, u32[]{:S(2)}) collective-permute-start(bf16[864,128]{1,0:T(8,128)(2,1)S(1)} %stack.9.refs_2_.refs_0_), channel_id=1, source_target_pairs={{0,4},{4,0},{8,12},{12,8},{16,20},{20,16},{24,28},{28,24},{1,5},{5... | collective-permute-start | bytes 663560 | tf_op jit(solution)/shard_map/ppermute | solution.py:369
  34.7 0.7 %collective-permute-done.9.refs_5_.refs_7_ = bf16[288,128]{1,0:T(8,128)(2,1)S(1)} collective-permute-done((bf16[288,128]{1,0:T(8,128)(2,1)S(1)}, bf16[288,128]{1,0:T(8,128)(2,1)S(1)}, u32[]{:S(2)}, u32[]{:S(2)}) %collective-permute-start.9) | collective-permute-done | bytes 73760 | tf_op jit(solution)/shard_map/ppermute | solution.py:369
  35.3 0.8 %weight_terms.2.refs_2_ = bf16[72,1792]{1,0:T(8,128)(2,1)S(1)} custom-call(bf16[288,128]{1,0:T(8,128)(2,1)S(1)} %stack.6.refs_1_.refs_0_.refs_2_, bf16[288,128]{1,0:T(8,128)(2,1)S(1)} %stack.8.refs_1_.refs_3_, bf16[288,128]{1,0:T(8,128)(2,1)S(1)} %stack.6.refs_1_.refs_0_.refs_2_, bf16[288,128]{1,0:T(8,128)(2,1)S(1)} %stack.8.refs_1_.refs_3_, ...), custom_call_target="tpu_custom_call" | custom-call | flops 1000 | bytes 1000 | tf_op jit(solution)/shard_map/weight_terms/pallas_call | solution.py:251
  36.1 1.5 %collective-permute-start.13 = (bf16[72,1792]{1,0:T(8,128)(2,1)S(1)}, bf16[72,1792]{1,0:T(8,128)(2,1)S(1)}, u32[]{:S(2)}, u32[]{:S(2)}) collective-permute-start(bf16[72,1792]{1,0:T(8,128)(2,1)S(1)} %weight_terms.2.refs_2_), channel_id=1, source_target_pairs={{0,8},{4,20},{8,0},{12,28},{16,24},{20,4},{24,16},{28,12},{1,9},{5... | collective-permute-start | bytes 774152 | tf_op jit(solution)/shard_map/ppermute | solution.py:369
  37.6 0.6 %collective-permute-done.7.refs_1_ = bf16[432,128]{1,0:T(8,128)(2,1)S(1)} collective-permute-done((bf16[432,128]{1,0:T(8,128)(2,1)S(1)}, bf16[432,128]{1,0:T(8,128)(2,1)S(1)}, u32[]{:S(2)}, u32[]{:S(2)}) %collective-permute-start.7) | collective-permute-done | bytes 110624 | tf_op jit(solution)/shard_map/ppermute | solution.py:366
  38.2 0.1 collective-permute-start.12
  38.3 0.4 natural_rows.1.refs_2_.rows
  38.7 1.1 %collective-permute-done.12.refs_5_.refs_7_ = bf16[864,128]{1,0:T(8,128)(2,1)S(1)} collective-permute-done((bf16[864,128]{1,0:T(8,128)(2,1)S(1)}, bf16[864,128]{1,0:T(8,128)(2,1)S(1)}, u32[]{:S(2)}, u32[]{:S(2)}) %collective-permute-start.12) | collective-permute-done | bytes 221216 | tf_op jit(solution)/shard_map/ppermute | solution.py:369
  39.8 1.0 %weight_terms.3 = (bf16[72,1792]{1,0:T(8,128)(2,1)S(1)}, f32[72,1792]{1,0:T(8,128)S(1)}, f32[72,1792]{1,0:T(8,128)S(1)}) custom-call(bf16[864,128]{1,0:T(8,128)(2,1)S(1)} %stack.9.refs_2_.refs_0_, bf16[864,128]{1,0:T(8,128)(2,1)S(1)} %stack.11.refs_3_.refs_1_, bf16[864,128]{1,0:T(8,128)(2,1)S(1)} %stack.9.refs_2_.refs_0_, ...), custom_call_target="tpu_custom_call" | custom-call | flops 1000 | bytes 1000 | tf_op jit(solution)/shard_map/weight_terms/pallas_call | solution.py:251
  40.8 1.6 %collective-permute-start.14 = (bf16[72,1792]{1,0:T(8,128)(2,1)S(1)}, bf16[72,1792]{1,0:T(8,128)(2,1)S(1)}, u32[]{:S(2)}, u32[]{:S(2)}) collective-permute-start(bf16[72,1792]{1,0:T(8,128)(2,1)S(1)} %get-tuple-element.29), channel_id=1, source_target_pairs={{0,8},{4,20},{8,0},{12,28},{16,24},{20,4},{24,16},{28,12},{1,9},{5... | collective-permute-start | bytes 774152 | tf_op jit(solution)/shard_map/ppermute | solution.py:369
  42.4 0.1 collective-permute-done.13.refs_1_
  42.5 0.1 add_rows.7
  42.6 1.6 %collective-permute-start.15 = (bf16[72,1792]{1,0:T(8,128)(2,1)S(1)}, bf16[72,1792]{1,0:T(8,128)(2,1)S(1)}, u32[]{:S(2)}, u32[]{:S(2)}) collective-permute-start(bf16[72,1792]{1,0:T(8,128)(2,1)S(1)} %add_rows.7), channel_id=1, source_target_pairs={{0,16},{4,12},{8,24},{12,4},{16,0},{20,28},{24,8},{28,20},{1,17},{... | collective-permute-start | bytes 774152 | tf_op jit(solution)/shard_map/ppermute | solution.py:369
  44.1 3.0 %hidden_terms.1 = bf16[512,1792]{1,0:T(8,128)(2,1)} custom-call(bf16[512,576]{1,0:T(8,128)(2,1)S(1)} %natural_rows.1.refs_2_.rows, bf16[576,1792]{1,0:T(8,128)(2,1)S(1)} %bitcast.2), custom_call_target="tpu_custom_call" | custom-call | flops 17179869184 | bytes 1048576 | tf_op jit(solution)/shard_map/hidden_terms/pallas_call | solution.py:344
  47.1 2.3 %collective-permute-done.14 = bf16[72,1792]{1,0:T(8,128)(2,1)S(1)} collective-permute-done((bf16[72,1792]{1,0:T(8,128)(2,1)S(1)}, bf16[72,1792]{1,0:T(8,128)(2,1)S(1)}, u32[]{:S(2)}, u32[]{:S(2)}) %collective-permute-start.14) | collective-permute-done | bytes 258080 | tf_op jit(solution)/shard_map/ppermute | solution.py:369
  49.4 0.9 %convert_add_fusion = f32[72,1792]{1,0:T(8,128)} fusion(bf16[72,1792]{1,0:T(8,128)(2,1)S(1)} %collective-permute-done.15, f32[72,1792]{1,0:T(8,128)S(1)} %get-tuple-element.28, bf16[72,1792]{1,0:T(8,128)(2,1)S(1)} %collective-permute-done.14), kind=kLoop, calls=%fused_computation | loop fusion | flops 516096 | bytes 1548288 | tf_op jit(solution)/shard_map/add | solution.py:423
  (22 shorter events, 0.2 us)
Async XLA Ops:
  6.0 8.3 %collective-permute-start = (bf16[576,128]{1,0:T(8,128)(2,1)S(1)}, bf16[576,128]{1,0:T(8,128)(2,1)S(1)}, u32[]{:S(2)}, u32[]{:S(2)}) collective-permute-start(bf16[576,128]{1,0:T(8,128)(2,1)S(1)} %get-tuple-element.19), channel_id=1, source_target_pairs={{0,1},{1,0},{2,3},{3,2},{4,5},{5,4},{6,7},{7,6},{8,9},{9,8},{10,11... | collective-permute-start | bytes 442376 | tf_op jit(solution)/shard_map/ppermute | solution.py:366
  14.3 3.2 %copy-start = (bf16[512,1792]{1,0:T(8,128)(2,1)S(1)}, bf16[512,1792]{1,0:T(8,128)(2,1)}, u32[]{:S(2)}) copy-start(bf16[512,1792]{1,0:T(8,128)(2,1)} %refs_8_.1) | copy-start | bytes 5505028
  14.4 8.5 %collective-permute-start.1 = (bf16[576,128]{1,0:T(8,128)(2,1)S(1)}, bf16[576,128]{1,0:T(8,128)(2,1)S(1)}, u32[]{:S(2)}, u32[]{:S(2)}) collective-permute-start(bf16[576,128]{1,0:T(8,128)(2,1)S(1)} %get-tuple-element.23), channel_id=1, source_target_pairs={{0,1},{1,0},{2,3},{3,2},{4,5},{5,4},{6,7},{7,6},{8,9},{9,8},{10,11... | collective-permute-start | bytes 442376 | tf_op jit(solution)/shard_map/ppermute | solution.py:366
  14.7 8.2 %collective-permute-start.2 = (bf16[576,128]{1,0:T(8,128)(2,1)S(1)}, bf16[576,128]{1,0:T(8,128)(2,1)S(1)}, u32[]{:S(2)}, u32[]{:S(2)}) collective-permute-start(bf16[576,128]{1,0:T(8,128)(2,1)S(1)} %add_rows.4), channel_id=1, source_target_pairs={{0,2},{1,3},{2,0},{3,1},{4,6},{5,7},{6,4},{7,5},{8,10},{9,11},{10,... | collective-permute-start | bytes 442376 | tf_op jit(solution)/shard_map/ppermute | solution.py:366
  17.5 17.9 %collective-permute-start.10 = (bf16[512,1792]{1,0:T(8,128)(2,1)S(1)}, bf16[512,1792]{1,0:T(8,128)(2,1)S(1)}, u32[]{:S(2)}, u32[]{:S(2)}) collective-permute-start(bf16[512,1792]{1,0:T(8,128)(2,1)S(1)} %copy-done), channel_id=1, source_target_pairs={{0,4},{4,0},{8,12},{12,8},{16,20},{20,16},{24,28},{28,24},{1,5},{5... | collective-permute-start | bytes 5505032 | tf_op jit(solution)/shard_map/ppermute | solution.py:369
  22.9 5.6 %collective-permute-start.3 = (bf16[144,128]{1,0:T(8,128)(2,1)S(1)}, bf16[144,128]{1,0:T(8,128)(2,1)S(1)}, u32[]{:S(2)}, u32[]{:S(2)}) collective-permute-start(bf16[144,128]{1,0:T(8,128)(2,1)S(1)} %add_rows.5.refs_0_.refs_3_), channel_id=1, source_target_pairs={{0,2},{1,3},{2,0},{3,1},{4,6},{5,7},{6,4},{7,5},{8,10},{9,11},{10,... | collective-permute-start | bytes 110600 | tf_op jit(solution)/shard_map/ppermute | solution.py:366
  24.3 7.5 %collective-permute-start.5 = (bf16[432,128]{1,0:T(8,128)(2,1)S(1)}, bf16[432,128]{1,0:T(8,128)(2,1)S(1)}, u32[]{:S(2)}, u32[]{:S(2)}) collective-permute-start(bf16[432,128]{1,0:T(8,128)(2,1)S(1)} %add_rows.6.refs_0_), channel_id=1, source_target_pairs={{0,2},{1,3},{2,0},{3,1},{4,6},{5,7},{6,4},{7,5},{8,10},{9,11},{10,... | collective-permute-start | bytes 331784 | tf_op jit(solution)/shard_map/ppermute | solution.py:366
  28.5 5.5 %collective-permute-start.8 = (bf16[288,128]{1,0:T(8,128)(2,1)S(1)}, bf16[288,128]{1,0:T(8,128)(2,1)S(1)}, u32[]{:S(2)}, u32[]{:S(2)}) collective-permute-start(bf16[288,128]{1,0:T(8,128)(2,1)S(1)} %stack.6.refs_1_.refs_0_.refs_2_), channel_id=1, source_target_pairs={{0,4},{4,0},{8,12},{12,8},{16,20},{20,16},{24,28},{28,24},{1,5},{5... | collective-permute-start | bytes 221192 | tf_op jit(solution)/shard_map/ppermute | solution.py:369
  28.6 5.4 %collective-permute-start.4 = (bf16[288,128]{1,0:T(8,128)(2,1)S(1)}, bf16[288,128]{1,0:T(8,128)(2,1)S(1)}, u32[]{:S(2)}, u32[]{:S(2)}) collective-permute-start(bf16[288,128]{1,0:T(8,128)(2,1)S(1)} %stack.6.refs_1_.refs_0_.refs_2_), channel_id=1, source_target_pairs={{0,1},{1,0},{2,3},{3,2},{4,5},{5,4},{6,7},{7,6},{8,9},{9,8},{10,11... | collective-permute-start | bytes 221192 | tf_op jit(solution)/shard_map/ppermute | solution.py:366
  30.6 7.0 %collective-permute-start.6 = (bf16[432,128]{1,0:T(8,128)(2,1)S(1)}, bf16[432,128]{1,0:T(8,128)(2,1)S(1)}, u32[]{:S(2)}, u32[]{:S(2)}) collective-permute-start(bf16[432,128]{1,0:T(8,128)(2,1)S(1)} %stack.10), channel_id=1, source_target_pairs={{0,1},{1,0},{2,3},{3,2},{4,5},{5,4},{6,7},{7,6},{8,9},{9,8},{10,11... | collective-permute-start | bytes 331784 | tf_op jit(solution)/shard_map/ppermute | solution.py:366
  31.8 6.4 %collective-permute-start.7 = (bf16[432,128]{1,0:T(8,128)(2,1)S(1)}, bf16[432,128]{1,0:T(8,128)(2,1)S(1)}, u32[]{:S(2)}, u32[]{:S(2)}) collective-permute-start(bf16[432,128]{1,0:T(8,128)(2,1)S(1)} %stack.7.refs_1_), channel_id=1, source_target_pairs={{0,1},{1,0},{2,3},{3,2},{4,5},{5,4},{6,7},{7,6},{8,9},{9,8},{10,11... | collective-permute-start | bytes 331784 | tf_op jit(solution)/shard_map/ppermute | solution.py:366
  34.0 1.3 %collective-permute-start.9 = (bf16[288,128]{1,0:T(8,128)(2,1)S(1)}, bf16[288,128]{1,0:T(8,128)(2,1)S(1)}, u32[]{:S(2)}, u32[]{:S(2)}) collective-permute-start(bf16[288,128]{1,0:T(8,128)(2,1)S(1)} %stack.8.refs_1_.refs_3_), channel_id=1, source_target_pairs={{0,4},{4,0},{8,12},{12,8},{16,20},{20,16},{24,28},{28,24},{1,5},{5... | collective-permute-start | bytes 221192 | tf_op jit(solution)/shard_map/ppermute | solution.py:369
  34.1 4.6 %collective-permute-start.11 = (bf16[864,128]{1,0:T(8,128)(2,1)S(1)}, bf16[864,128]{1,0:T(8,128)(2,1)S(1)}, u32[]{:S(2)}, u32[]{:S(2)}) collective-permute-start(bf16[864,128]{1,0:T(8,128)(2,1)S(1)} %stack.9.refs_2_.refs_0_), channel_id=1, source_target_pairs={{0,4},{4,0},{8,12},{12,8},{16,20},{20,16},{24,28},{28,24},{1,5},{5... | collective-permute-start | bytes 663560 | tf_op jit(solution)/shard_map/ppermute | solution.py:369
  36.1 6.4 %collective-permute-start.13 = (bf16[72,1792]{1,0:T(8,128)(2,1)S(1)}, bf16[72,1792]{1,0:T(8,128)(2,1)S(1)}, u32[]{:S(2)}, u32[]{:S(2)}) collective-permute-start(bf16[72,1792]{1,0:T(8,128)(2,1)S(1)} %weight_terms.2.refs_2_), channel_id=1, source_target_pairs={{0,8},{4,20},{8,0},{12,28},{16,24},{20,4},{24,16},{28,12},{1,9},{5... | collective-permute-start | bytes 774152 | tf_op jit(solution)/shard_map/ppermute | solution.py:369
  38.2 1.5 %collective-permute-start.12 = (bf16[864,128]{1,0:T(8,128)(2,1)S(1)}, bf16[864,128]{1,0:T(8,128)(2,1)S(1)}, u32[]{:S(2)}, u32[]{:S(2)}) collective-permute-start(bf16[864,128]{1,0:T(8,128)(2,1)S(1)} %stack.11.refs_3_.refs_1_), channel_id=1, source_target_pairs={{0,4},{4,0},{8,12},{12,8},{16,20},{20,16},{24,28},{28,24},{1,5},{5... | collective-permute-start | bytes 663560 | tf_op jit(solution)/shard_map/ppermute | solution.py:369
  40.8 8.6 %collective-permute-start.14 = (bf16[72,1792]{1,0:T(8,128)(2,1)S(1)}, bf16[72,1792]{1,0:T(8,128)(2,1)S(1)}, u32[]{:S(2)}, u32[]{:S(2)}) collective-permute-start(bf16[72,1792]{1,0:T(8,128)(2,1)S(1)} %get-tuple-element.29), channel_id=1, source_target_pairs={{0,8},{4,20},{8,0},{12,28},{16,24},{20,4},{24,16},{28,12},{1,9},{5... | collective-permute-start | bytes 774152 | tf_op jit(solution)/shard_map/ppermute | solution.py:369
  42.5 1.6 %copy-start.1 = (bf16[1792,576]{0,1:T(8,128)(2,1)S(1)}, bf16[1792,576]{0,1:T(8,128)(2,1)}, u32[]{:S(2)}) copy-start(bf16[1792,576]{0,1:T(8,128)(2,1)} %param.19) | copy-start | bytes 6193156
  42.6 6.8 %collective-permute-start.15 = (bf16[72,1792]{1,0:T(8,128)(2,1)S(1)}, bf16[72,1792]{1,0:T(8,128)(2,1)S(1)}, u32[]{:S(2)}, u32[]{:S(2)}) collective-permute-start(bf16[72,1792]{1,0:T(8,128)(2,1)S(1)} %add_rows.7), channel_id=1, source_target_pairs={{0,16},{4,12},{8,24},{12,4},{16,0},{20,28},{24,8},{28,20},{1,17},{... | collective-permute-start | bytes 774152 | tf_op jit(solution)/shard_map/ppermute | solution.py:369

commit v5 on v4

--- a/solution.py
+++ b/solution.py
@@ -186,7 +186,7 @@
     width = latent.shape[1]
     kva = width + rope
     tokens = len(which) * share
-    chunks = 4 if lifts_here else 8
+    chunks = 2 if lifts_here else 8
     if key_cols % (chunks * 128) or rg.shape[1] % (chunks * 128):
         chunks = 1
     operands = (doc_lengths, kg, vg, rg, kl, vl, latent, gain)

time: 50.8 us -> 50.7 us (level)
  no operation moved by 1% of the time
where the time goes in v5:
time: 50.7 us; the launch traced here: 50.1 us
  Pallas kernels  20.3 us (40%)
  starting transfers between devices  19.2 us (38%)
  waiting for transfers between devices  8.95 us (18%)
  other arithmetic  0.87 us (2%)
  between operations  0.77 us (2%)
    pallas_call x3, Pallas kernels, partial_terms(): pl.pallas_call(functools.partial(partial_kernel, which=which, dtypes=dtyp...  15 us
    ppermute x8, starting transfers between devices, swap_head(): return lax.ppermute(array, 'head', [(i, i ^ bits) for i in range(heads)])  13.8 us
    ppermute x8, starting transfers between devices, swap_group(): lax.ppermute(array, 'group', [(i, i ^ bits_of(i)) for i in range(groups)])  5.45 us
    ppermute x8, waiting for transfers between devices, swap_head(): return lax.ppermute(array, 'head', [(i, i ^ bits) for i in range(heads)])  4.84 us
    ppermute x8, waiting for transfers between devices, swap_group(): lax.ppermute(array, 'group', [(i, i ^ bits_of(i)) for i in range(groups)])  4.11 us
    pallas_call x1, Pallas kernels, hidden_terms(): pl.pallas_call(hidden_kernel, grid=(columns // col_block,), in_specs=[pl....  2.99 us
    pallas_call x2, Pallas kernels, weight_terms(): pl.pallas_call(functools.partial(weight_kernel, skips=skips), in_specs=[v...  1.78 us
  transfers between devices with their start and end apart: 16, of which 8 were waited for; matrix products, arithmetic and copies ran while one was open for 0% of the time, Pallas kernels for 30%

profile of v5, /device:TPU:0, one launch (start us, length us, event | category | flops | bytes accessed | tf_op | source)
XLA Modules:
  0.0 50.1 jit_solution(419335482340787888)
XLA Ops:
  0.6 5.3 %partial_terms.3 = (bf16[576,128]{1,0:T(8,128)(2,1)S(1)}, bf16[512,4096]{1,0:T(8,128)(2,1)S(1)}, bf16[512,4096]{1,0:T(8,128)(2,1)S(1)}) custom-call(s32[1,4]{1,0:T(1,128)} %refs_0_.5, bf16[512,4096]{1,0:T(8,128)(2,1)} %refs_1_.5, bf16[512,4096]{1,0:T(8,128)(2,1)} %refs_2_.5, bf16[512,2048]{1,0:T(8,128)(2,1)} %refs_3_.5, bf16[512,4096]{1,0:T(8,128)(2,1)} %refs_4_.1, ...), custom_call_target="tpu_custom_call" | custom-call | flops 17179869184 | bytes 1048576 | tf_op jit(solution)/shard_map/partial_terms/pallas_call | solution.py:197
  6.0 3.1 %collective-permute-start = (bf16[576,128]{1,0:T(8,128)(2,1)S(1)}, bf16[576,128]{1,0:T(8,128)(2,1)S(1)}, u32[]{:S(2)}, u32[]{:S(2)}) collective-permute-start(bf16[576,128]{1,0:T(8,128)(2,1)S(1)} %get-tuple-element.19), channel_id=1, source_target_pairs={{0,1},{1,0},{2,3},{3,2},{4,5},{5,4},{6,7},{7,6},{8,9},{9,8},{10,11... | collective-permute-start | bytes 442376 | tf_op jit(solution)/shard_map/ppermute | solution.py:366
  9.0 5.1 %partial_terms.4 = (f32[576,128]{1,0:T(8,128)S(1)}, bf16[576,128]{1,0:T(8,128)(2,1)S(1)}) custom-call(s32[1,4]{1,0:T(1,128)} %refs_0_.5, bf16[512,4096]{1,0:T(8,128)(2,1)} %refs_1_.5, bf16[512,4096]{1,0:T(8,128)(2,1)} %refs_2_.5, bf16[512,2048]{1,0:T(8,128)(2,1)} %refs_3_.5, bf16[512,4096]{1,0:T(8,128)(2,1)S(1)} %get-tuple-element.21.refs_4_, ...), custom_call_target="tpu_custom_call" | custom-call | flops 17179869184 | bytes 1048576 | tf_op jit(solution)/shard_map/partial_terms/pallas_call | solution.py:197
  14.1 0.0 copy-start
  14.2 0.6 %collective-permute-start.1 = (bf16[576,128]{1,0:T(8,128)(2,1)S(1)}, bf16[576,128]{1,0:T(8,128)(2,1)S(1)}, u32[]{:S(2)}, u32[]{:S(2)}) collective-permute-start(bf16[576,128]{1,0:T(8,128)(2,1)S(1)} %get-tuple-element.23), channel_id=1, source_target_pairs={{0,1},{1,0},{2,3},{3,2},{4,5},{5,4},{6,7},{7,6},{8,9},{9,8},{10,11... | collective-permute-start | bytes 442376 | tf_op jit(solution)/shard_map/ppermute | solution.py:366
  14.7 2.6 %collective-permute-start.2 = (bf16[576,128]{1,0:T(8,128)(2,1)S(1)}, bf16[576,128]{1,0:T(8,128)(2,1)S(1)}, u32[]{:S(2)}, u32[]{:S(2)}) collective-permute-start(bf16[576,128]{1,0:T(8,128)(2,1)S(1)} %add_rows.4), channel_id=1, source_target_pairs={{0,2},{1,3},{2,0},{3,1},{4,6},{5,7},{6,4},{7,5},{8,10},{9,11},{10,... | collective-permute-start | bytes 442376 | tf_op jit(solution)/shard_map/ppermute | solution.py:366
  17.3 4.6 %partial_terms.5.refs_0_ = f32[576,128]{1,0:T(8,128)S(1)} custom-call(s32[1,4]{1,0:T(1,128)} %refs_0_.5, bf16[512,4096]{1,0:T(8,128)(2,1)} %refs_1_.5, bf16[512,4096]{1,0:T(8,128)(2,1)} %refs_2_.5, bf16[512,2048]{1,0:T(8,128)(2,1)} %refs_3_.5, bf16[512,4096]{1,0:T(8,128)(2,1)S(1)} %get-tuple-element.21.refs_4_, ...), custom_call_target="tpu_custom_call" | custom-call | flops 17179869184 | bytes 1048576 | tf_op jit(solution)/shard_map/partial_terms/pallas_call | solution.py:197
  21.9 0.8 %collective-permute-done.1.refs_1_ = bf16[576,128]{1,0:T(8,128)(2,1)S(1)} collective-permute-done((bf16[576,128]{1,0:T(8,128)(2,1)S(1)}, bf16[576,128]{1,0:T(8,128)(2,1)S(1)}, u32[]{:S(2)}, u32[]{:S(2)}) %collective-permute-start.1) | collective-permute-done | bytes 147488 | tf_op jit(solution)/shard_map/ppermute | solution.py:366
  22.7 1.4 %collective-permute-start.3 = (bf16[144,128]{1,0:T(8,128)(2,1)S(1)}, bf16[144,128]{1,0:T(8,128)(2,1)S(1)}, u32[]{:S(2)}, u32[]{:S(2)}) collective-permute-start(bf16[144,128]{1,0:T(8,128)(2,1)S(1)} %add_rows.5.refs_0_.refs_3_), channel_id=1, source_target_pairs={{0,2},{1,3},{2,0},{3,1},{4,6},{5,7},{6,4},{7,5},{8,10},{9,11},{10,... | collective-permute-start | bytes 110600 | tf_op jit(solution)/shard_map/ppermute | solution.py:366
  24.2 1.7 %collective-permute-start.5 = (bf16[432,128]{1,0:T(8,128)(2,1)S(1)}, bf16[432,128]{1,0:T(8,128)(2,1)S(1)}, u32[]{:S(2)}, u32[]{:S(2)}) collective-permute-start(bf16[432,128]{1,0:T(8,128)(2,1)S(1)} %add_rows.6.refs_0_), channel_id=1, source_target_pairs={{0,2},{1,3},{2,0},{3,1},{4,6},{5,7},{6,4},{7,5},{8,10},{9,11},{10,... | collective-permute-start | bytes 331784 | tf_op jit(solution)/shard_map/ppermute | solution.py:366
  25.8 2.6 %collective-permute-done.3.refs_1_ = bf16[144,128]{1,0:T(8,128)(2,1)S(1)} collective-permute-done((bf16[144,128]{1,0:T(8,128)(2,1)S(1)}, bf16[144,128]{1,0:T(8,128)(2,1)S(1)}, u32[]{:S(2)}, u32[]{:S(2)}) %collective-permute-start.3) | collective-permute-done | bytes 36896 | tf_op jit(solution)/shard_map/ppermute | solution.py:366
  28.4 2.0 %collective-permute-start.4 = (bf16[288,128]{1,0:T(8,128)(2,1)S(1)}, bf16[288,128]{1,0:T(8,128)(2,1)S(1)}, u32[]{:S(2)}, u32[]{:S(2)}) collective-permute-start(bf16[288,128]{1,0:T(8,128)(2,1)S(1)} %stack.6.refs_1_.refs_0_.refs_2_), channel_id=1, source_target_pairs={{0,1},{1,0},{2,3},{3,2},{4,5},{5,4},{6,7},{7,6},{8,9},{9,8},{10,11... | collective-permute-start | bytes 221192 | tf_op jit(solution)/shard_map/ppermute | solution.py:366
  30.4 0.1 collective-permute-start.6
  30.6 0.9 %collective-permute-done.5.refs_0_ = bf16[432,128]{1,0:T(8,128)(2,1)S(1)} collective-permute-done((bf16[432,128]{1,0:T(8,128)(2,1)S(1)}, bf16[432,128]{1,0:T(8,128)(2,1)S(1)}, u32[]{:S(2)}, u32[]{:S(2)}) %collective-permute-start.5) | collective-permute-done | bytes 110624 | tf_op jit(solution)/shard_map/ppermute | solution.py:366
  31.5 2.3 %collective-permute-start.7 = (bf16[432,128]{1,0:T(8,128)(2,1)S(1)}, bf16[432,128]{1,0:T(8,128)(2,1)S(1)}, u32[]{:S(2)}, u32[]{:S(2)}) collective-permute-start(bf16[432,128]{1,0:T(8,128)(2,1)S(1)} %stack.7.refs_1_), channel_id=1, source_target_pairs={{0,1},{1,0},{2,3},{3,2},{4,5},{5,4},{6,7},{7,6},{8,9},{9,8},{10,11... | collective-permute-start | bytes 331784 | tf_op jit(solution)/shard_map/ppermute | solution.py:366
  33.8 0.1 collective-permute-start.9
  33.9 0.6 %collective-permute-start.11 = (bf16[864,128]{1,0:T(8,128)(2,1)S(1)}, bf16[864,128]{1,0:T(8,128)(2,1)S(1)}, u32[]{:S(2)}, u32[]{:S(2)}) collective-permute-start(bf16[864,128]{1,0:T(8,128)(2,1)S(1)} %stack.9.refs_2_.refs_0_), channel_id=1, source_target_pairs={{0,4},{4,0},{8,12},{12,8},{16,20},{20,16},{24,28},{28,24},{1,5},{5... | collective-permute-start | bytes 663560 | tf_op jit(solution)/shard_map/ppermute | solution.py:369
  34.5 0.7 %collective-permute-done.9.refs_5_.refs_7_ = bf16[288,128]{1,0:T(8,128)(2,1)S(1)} collective-permute-done((bf16[288,128]{1,0:T(8,128)(2,1)S(1)}, bf16[288,128]{1,0:T(8,128)(2,1)S(1)}, u32[]{:S(2)}, u32[]{:S(2)}) %collective-permute-start.9) | collective-permute-done | bytes 73760 | tf_op jit(solution)/shard_map/ppermute | solution.py:369
  35.1 0.8 %weight_terms.2.refs_2_ = bf16[72,1792]{1,0:T(8,128)(2,1)S(1)} custom-call(bf16[288,128]{1,0:T(8,128)(2,1)S(1)} %stack.6.refs_1_.refs_0_.refs_2_, bf16[288,128]{1,0:T(8,128)(2,1)S(1)} %stack.8.refs_1_.refs_3_, bf16[288,128]{1,0:T(8,128)(2,1)S(1)} %stack.6.refs_1_.refs_0_.refs_2_, bf16[288,128]{1,0:T(8,128)(2,1)S(1)} %stack.8.refs_1_.refs_3_, ...), custom_call_target="tpu_custom_call" | custom-call | flops 1000 | bytes 1000 | tf_op jit(solution)/shard_map/weight_terms/pallas_call | solution.py:251
  35.9 1.5 %collective-permute-start.13 = (bf16[72,1792]{1,0:T(8,128)(2,1)S(1)}, bf16[72,1792]{1,0:T(8,128)(2,1)S(1)}, u32[]{:S(2)}, u32[]{:S(2)}) collective-permute-start(bf16[72,1792]{1,0:T(8,128)(2,1)S(1)} %weight_terms.2.refs_2_), channel_id=1, source_target_pairs={{0,8},{4,20},{8,0},{12,28},{16,24},{20,4},{24,16},{28,12},{1,9},{5... | collective-permute-start | bytes 774152 | tf_op jit(solution)/shard_map/ppermute | solution.py:369
  37.5 0.6 %collective-permute-done.7.refs_1_ = bf16[432,128]{1,0:T(8,128)(2,1)S(1)} collective-permute-done((bf16[432,128]{1,0:T(8,128)(2,1)S(1)}, bf16[432,128]{1,0:T(8,128)(2,1)S(1)}, u32[]{:S(2)}, u32[]{:S(2)}) %collective-permute-start.7) | collective-permute-done | bytes 110624 | tf_op jit(solution)/shard_map/ppermute | solution.py:366
  38.1 0.1 collective-permute-start.12
  38.1 0.4 natural_rows.1.refs_2_.rows
  38.5 1.1 %collective-permute-done.12.refs_5_.refs_7_ = bf16[864,128]{1,0:T(8,128)(2,1)S(1)} collective-permute-done((bf16[864,128]{1,0:T(8,128)(2,1)S(1)}, bf16[864,128]{1,0:T(8,128)(2,1)S(1)}, u32[]{:S(2)}, u32[]{:S(2)}) %collective-permute-start.12) | collective-permute-done | bytes 221216 | tf_op jit(solution)/shard_map/ppermute | solution.py:369
  39.6 1.0 %weight_terms.3 = (bf16[72,1792]{1,0:T(8,128)(2,1)S(1)}, f32[72,1792]{1,0:T(8,128)S(1)}, f32[72,1792]{1,0:T(8,128)S(1)}) custom-call(bf16[864,128]{1,0:T(8,128)(2,1)S(1)} %stack.9.refs_2_.refs_0_, bf16[864,128]{1,0:T(8,128)(2,1)S(1)} %stack.11.refs_3_.refs_1_, bf16[864,128]{1,0:T(8,128)(2,1)S(1)} %stack.9.refs_2_.refs_0_, ...), custom_call_target="tpu_custom_call" | custom-call | flops 1000 | bytes 1000 | tf_op jit(solution)/shard_map/weight_terms/pallas_call | solution.py:251
  40.6 1.6 %collective-permute-start.14 = (bf16[72,1792]{1,0:T(8,128)(2,1)S(1)}, bf16[72,1792]{1,0:T(8,128)(2,1)S(1)}, u32[]{:S(2)}, u32[]{:S(2)}) collective-permute-start(bf16[72,1792]{1,0:T(8,128)(2,1)S(1)} %get-tuple-element.29), channel_id=1, source_target_pairs={{0,8},{4,20},{8,0},{12,28},{16,24},{20,4},{24,16},{28,12},{1,9},{5... | collective-permute-start | bytes 774152 | tf_op jit(solution)/shard_map/ppermute | solution.py:369
  42.2 0.1 collective-permute-done.13.refs_1_
  42.3 0.1 add_rows.7
  42.4 1.6 %collective-permute-start.15 = (bf16[72,1792]{1,0:T(8,128)(2,1)S(1)}, bf16[72,1792]{1,0:T(8,128)(2,1)S(1)}, u32[]{:S(2)}, u32[]{:S(2)}) collective-permute-start(bf16[72,1792]{1,0:T(8,128)(2,1)S(1)} %add_rows.7), channel_id=1, source_target_pairs={{0,16},{4,12},{8,24},{12,4},{16,0},{20,28},{24,8},{28,20},{1,17},{... | collective-permute-start | bytes 774152 | tf_op jit(solution)/shard_map/ppermute | solution.py:369
  43.9 3.0 %hidden_terms.1 = bf16[512,1792]{1,0:T(8,128)(2,1)} custom-call(bf16[512,576]{1,0:T(8,128)(2,1)S(1)} %natural_rows.1.refs_2_.rows, bf16[576,1792]{1,0:T(8,128)(2,1)S(1)} %bitcast.2), custom_call_target="tpu_custom_call" | custom-call | flops 17179869184 | bytes 1048576 | tf_op jit(solution)/shard_map/hidden_terms/pallas_call | solution.py:344
  46.9 2.3 %collective-permute-done.14 = bf16[72,1792]{1,0:T(8,128)(2,1)S(1)} collective-permute-done((bf16[72,1792]{1,0:T(8,128)(2,1)S(1)}, bf16[72,1792]{1,0:T(8,128)(2,1)S(1)}, u32[]{:S(2)}, u32[]{:S(2)}) %collective-permute-start.14) | collective-permute-done | bytes 258080 | tf_op jit(solution)/shard_map/ppermute | solution.py:369
  49.2 0.9 %convert_add_fusion = f32[72,1792]{1,0:T(8,128)} fusion(bf16[72,1792]{1,0:T(8,128)(2,1)S(1)} %collective-permute-done.15, f32[72,1792]{1,0:T(8,128)S(1)} %get-tuple-element.28, bf16[72,1792]{1,0:T(8,128)(2,1)S(1)} %collective-permute-done.14), kind=kLoop, calls=%fused_computation | loop fusion | flops 516096 | bytes 1548288 | tf_op jit(solution)/shard_map/add | solution.py:423
  (22 shorter events, 0.2 us)
Async XLA Ops:
  6.0 8.2 %collective-permute-start = (bf16[576,128]{1,0:T(8,128)(2,1)S(1)}, bf16[576,128]{1,0:T(8,128)(2,1)S(1)}, u32[]{:S(2)}, u32[]{:S(2)}) collective-permute-start(bf16[576,128]{1,0:T(8,128)(2,1)S(1)} %get-tuple-element.19), channel_id=1, source_target_pairs={{0,1},{1,0},{2,3},{3,2},{4,5},{5,4},{6,7},{7,6},{8,9},{9,8},{10,11... | collective-permute-start | bytes 442376 | tf_op jit(solution)/shard_map/ppermute | solution.py:366
  14.1 3.2 %copy-start = (bf16[512,1792]{1,0:T(8,128)(2,1)S(1)}, bf16[512,1792]{1,0:T(8,128)(2,1)}, u32[]{:S(2)}) copy-start(bf16[512,1792]{1,0:T(8,128)(2,1)} %refs_8_.1) | copy-start | bytes 5505028
  14.2 8.6 %collective-permute-start.1 = (bf16[576,128]{1,0:T(8,128)(2,1)S(1)}, bf16[576,128]{1,0:T(8,128)(2,1)S(1)}, u32[]{:S(2)}, u32[]{:S(2)}) collective-permute-start(bf16[576,128]{1,0:T(8,128)(2,1)S(1)} %get-tuple-element.23), channel_id=1, source_target_pairs={{0,1},{1,0},{2,3},{3,2},{4,5},{5,4},{6,7},{7,6},{8,9},{9,8},{10,11... | collective-permute-start | bytes 442376 | tf_op jit(solution)/shard_map/ppermute | solution.py:366
  14.7 8.0 %collective-permute-start.2 = (bf16[576,128]{1,0:T(8,128)(2,1)S(1)}, bf16[576,128]{1,0:T(8,128)(2,1)S(1)}, u32[]{:S(2)}, u32[]{:S(2)}) collective-permute-start(bf16[576,128]{1,0:T(8,128)(2,1)S(1)} %add_rows.4), channel_id=1, source_target_pairs={{0,2},{1,3},{2,0},{3,1},{4,6},{5,7},{6,4},{7,5},{8,10},{9,11},{10,... | collective-permute-start | bytes 442376 | tf_op jit(solution)/shard_map/ppermute | solution.py:366
  17.3 17.8 %collective-permute-start.10 = (bf16[512,1792]{1,0:T(8,128)(2,1)S(1)}, bf16[512,1792]{1,0:T(8,128)(2,1)S(1)}, u32[]{:S(2)}, u32[]{:S(2)}) collective-permute-start(bf16[512,1792]{1,0:T(8,128)(2,1)S(1)} %copy-done), channel_id=1, source_target_pairs={{0,4},{4,0},{8,12},{12,8},{16,20},{20,16},{24,28},{28,24},{1,5},{5... | collective-permute-start | bytes 5505032 | tf_op jit(solution)/shard_map/ppermute | solution.py:369
  22.7 5.6 %collective-permute-start.3 = (bf16[144,128]{1,0:T(8,128)(2,1)S(1)}, bf16[144,128]{1,0:T(8,128)(2,1)S(1)}, u32[]{:S(2)}, u32[]{:S(2)}) collective-permute-start(bf16[144,128]{1,0:T(8,128)(2,1)S(1)} %add_rows.5.refs_0_.refs_3_), channel_id=1, source_target_pairs={{0,2},{1,3},{2,0},{3,1},{4,6},{5,7},{6,4},{7,5},{8,10},{9,11},{10,... | collective-permute-start | bytes 110600 | tf_op jit(solution)/shard_map/ppermute | solution.py:366
  24.2 7.3 %collective-permute-start.5 = (bf16[432,128]{1,0:T(8,128)(2,1)S(1)}, bf16[432,128]{1,0:T(8,128)(2,1)S(1)}, u32[]{:S(2)}, u32[]{:S(2)}) collective-permute-start(bf16[432,128]{1,0:T(8,128)(2,1)S(1)} %add_rows.6.refs_0_), channel_id=1, source_target_pairs={{0,2},{1,3},{2,0},{3,1},{4,6},{5,7},{6,4},{7,5},{8,10},{9,11},{10,... | collective-permute-start | bytes 331784 | tf_op jit(solution)/shard_map/ppermute | solution.py:366
  28.4 5.5 %collective-permute-start.8 = (bf16[288,128]{1,0:T(8,128)(2,1)S(1)}, bf16[288,128]{1,0:T(8,128)(2,1)S(1)}, u32[]{:S(2)}, u32[]{:S(2)}) collective-permute-start(bf16[288,128]{1,0:T(8,128)(2,1)S(1)} %stack.6.refs_1_.refs_0_.refs_2_), channel_id=1, source_target_pairs={{0,4},{4,0},{8,12},{12,8},{16,20},{20,16},{24,28},{28,24},{1,5},{5... | collective-permute-start | bytes 221192 | tf_op jit(solution)/shard_map/ppermute | solution.py:369
  28.4 5.4 %collective-permute-start.4 = (bf16[288,128]{1,0:T(8,128)(2,1)S(1)}, bf16[288,128]{1,0:T(8,128)(2,1)S(1)}, u32[]{:S(2)}, u32[]{:S(2)}) collective-permute-start(bf16[288,128]{1,0:T(8,128)(2,1)S(1)} %stack.6.refs_1_.refs_0_.refs_2_), channel_id=1, source_target_pairs={{0,1},{1,0},{2,3},{3,2},{4,5},{5,4},{6,7},{7,6},{8,9},{9,8},{10,11... | collective-permute-start | bytes 221192 | tf_op jit(solution)/shard_map/ppermute | solution.py:366
  30.4 7.0 %collective-permute-start.6 = (bf16[432,128]{1,0:T(8,128)(2,1)S(1)}, bf16[432,128]{1,0:T(8,128)(2,1)S(1)}, u32[]{:S(2)}, u32[]{:S(2)}) collective-permute-start(bf16[432,128]{1,0:T(8,128)(2,1)S(1)} %stack.10), channel_id=1, source_target_pairs={{0,1},{1,0},{2,3},{3,2},{4,5},{5,4},{6,7},{7,6},{8,9},{9,8},{10,11... | collective-permute-start | bytes 331784 | tf_op jit(solution)/shard_map/ppermute | solution.py:366
  31.5 6.5 %collective-permute-start.7 = (bf16[432,128]{1,0:T(8,128)(2,1)S(1)}, bf16[432,128]{1,0:T(8,128)(2,1)S(1)}, u32[]{:S(2)}, u32[]{:S(2)}) collective-permute-start(bf16[432,128]{1,0:T(8,128)(2,1)S(1)} %stack.7.refs_1_), channel_id=1, source_target_pairs={{0,1},{1,0},{2,3},{3,2},{4,5},{5,4},{6,7},{7,6},{8,9},{9,8},{10,11... | collective-permute-start | bytes 331784 | tf_op jit(solution)/shard_map/ppermute | solution.py:366
  33.8 1.3 %collective-permute-start.9 = (bf16[288,128]{1,0:T(8,128)(2,1)S(1)}, bf16[288,128]{1,0:T(8,128)(2,1)S(1)}, u32[]{:S(2)}, u32[]{:S(2)}) collective-permute-start(bf16[288,128]{1,0:T(8,128)(2,1)S(1)} %stack.8.refs_1_.refs_3_), channel_id=1, source_target_pairs={{0,4},{4,0},{8,12},{12,8},{16,20},{20,16},{24,28},{28,24},{1,5},{5... | collective-permute-start | bytes 221192 | tf_op jit(solution)/shard_map/ppermute | solution.py:369
  33.9 4.6 %collective-permute-start.11 = (bf16[864,128]{1,0:T(8,128)(2,1)S(1)}, bf16[864,128]{1,0:T(8,128)(2,1)S(1)}, u32[]{:S(2)}, u32[]{:S(2)}) collective-permute-start(bf16[864,128]{1,0:T(8,128)(2,1)S(1)} %stack.9.refs_2_.refs_0_), channel_id=1, source_target_pairs={{0,4},{4,0},{8,12},{12,8},{16,20},{20,16},{24,28},{28,24},{1,5},{5... | collective-permute-start | bytes 663560 | tf_op jit(solution)/shard_map/ppermute | solution.py:369
  35.9 6.4 %collective-permute-start.13 = (bf16[72,1792]{1,0:T(8,128)(2,1)S(1)}, bf16[72,1792]{1,0:T(8,128)(2,1)S(1)}, u32[]{:S(2)}, u32[]{:S(2)}) collective-permute-start(bf16[72,1792]{1,0:T(8,128)(2,1)S(1)} %weight_terms.2.refs_2_), channel_id=1, source_target_pairs={{0,8},{4,20},{8,0},{12,28},{16,24},{20,4},{24,16},{28,12},{1,9},{5... | collective-permute-start | bytes 774152 | tf_op jit(solution)/shard_map/ppermute | solution.py:369
  38.1 1.5 %collective-permute-start.12 = (bf16[864,128]{1,0:T(8,128)(2,1)S(1)}, bf16[864,128]{1,0:T(8,128)(2,1)S(1)}, u32[]{:S(2)}, u32[]{:S(2)}) collective-permute-start(bf16[864,128]{1,0:T(8,128)(2,1)S(1)} %stack.11.refs_3_.refs_1_), channel_id=1, source_target_pairs={{0,4},{4,0},{8,12},{12,8},{16,20},{20,16},{24,28},{28,24},{1,5},{5... | collective-permute-start | bytes 663560 | tf_op jit(solution)/shard_map/ppermute | solution.py:369
  40.6 8.6 %collective-permute-start.14 = (bf16[72,1792]{1,0:T(8,128)(2,1)S(1)}, bf16[72,1792]{1,0:T(8,128)(2,1)S(1)}, u32[]{:S(2)}, u32[]{:S(2)}) collective-permute-start(bf16[72,1792]{1,0:T(8,128)(2,1)S(1)} %get-tuple-element.29), channel_id=1, source_target_pairs={{0,8},{4,20},{8,0},{12,28},{16,24},{20,4},{24,16},{28,12},{1,9},{5... | collective-permute-start | bytes 774152 | tf_op jit(solution)/shard_map/ppermute | solution.py:369
  42.3 1.6 %copy-start.1 = (bf16[1792,576]{0,1:T(8,128)(2,1)S(1)}, bf16[1792,576]{0,1:T(8,128)(2,1)}, u32[]{:S(2)}) copy-start(bf16[1792,576]{0,1:T(8,128)(2,1)} %param.19) | copy-start | bytes 6193156
  42.4 6.9 %collective-permute-start.15 = (bf16[72,1792]{1,0:T(8,128)(2,1)S(1)}, bf16[72,1792]{1,0:T(8,128)(2,1)S(1)}, u32[]{:S(2)}, u32[]{:S(2)}) collective-permute-start(bf16[72,1792]{1,0:T(8,128)(2,1)S(1)} %add_rows.7), channel_id=1, source_target_pairs={{0,16},{4,12},{8,24},{12,4},{16,0},{20,28},{24,8},{28,20},{1,17},{... | collective-permute-start | bytes 774152 | tf_op jit(solution)/shard_map/ppermute | solution.py:369
